TPU v7x, 32 devices: a whole 2x2x4 slice. The times are simulated.
32 devices in a mesh: dp: 8 (over z, x), tensor: 4 (over y, core).
Axes of the slice: x: 2, y: 2, z: 4, core: 2. Of those that a mesh axis runs over, the one named last changes fastest.
Arguments:
- tokens: bfloat16 [16384, 1024], P(('dp', 'tensor')), may hold values from -6 to 6
- cotangent: bfloat16 [16384, 1024], P(('dp', 'tensor')), may hold values from -6 to 6
- qkv_weight: bfloat16 [2, 1024, 3072], P(None, None, 'tensor'), may hold values from -0.25 to 0.25
- qkv_bias: bfloat16 [2, 3072], P(None, 'tensor'), may hold values from -3 to 3
- out_weight: bfloat16 [2, 1024, 1024], P(None, 'tensor'), may hold values from -0.5 to 0.5
- out_bias: bfloat16 [2, 1024], replicated, may hold values from -3 to 3
- up_weight: bfloat16 [2, 1024, 4096], P(None, None, 'tensor'), may hold values from -0.1875 to 0.1875
- up_bias: bfloat16 [2, 4096], P(None, 'tensor'), may hold values from -3 to 3
- down_weight: bfloat16 [2, 4096, 1024], P(None, 'tensor'), may hold values from -0.125 to 0.125
- down_bias: bfloat16 [2, 1024], replicated, may hold values from -3 to 3
- norm_gain: bfloat16 [2, 2, 1024], replicated, may hold values from 0.5 to 1.5
- norm_shift: bfloat16 [2, 2, 1024], replicated, may hold values from -2 to 2
Outputs:
- output: float32 [16384, 1024], P(('dp', 'tensor'))
- input_grad: float32 [16384, 1024], P(('dp', 'tensor'))
- qkv_weight_grad: float32 [2, 1024, 3072], P(None, None, 'tensor')
- qkv_bias_grad: float32 [2, 3072], P(None, 'tensor')
- out_weight_grad: float32 [2, 1024, 1024], P(None, 'tensor')
- out_bias_grad: float32 [2, 1024], replicated
- up_weight_grad: float32 [2, 1024, 4096], P(None, None, 'tensor')
- up_bias_grad: float32 [2, 4096], P(None, 'tensor')
- down_weight_grad: float32 [2, 4096, 1024], P(None, 'tensor')
- down_bias_grad: float32 [2, 1024], replicated
- norm_gain_grad: float32 [2, 2, 1024], replicated
- norm_shift_grad: float32 [2, 2, 1024], replicated
- layer_stats: float32 [2, 3], replicated
All inputs are finite; a program needn't handle non-finite values.
Results may differ from a plain program's by a relative error of at most 0.025.
The roundings to bfloat16 on the way count: a program that leaves them out, or rounds other values in their place, can miss the bound.
Values may be sent and summed in bfloat16 or wider, within the bound.
A program may use at most 512 MiB of HBM per device.

v0:
```python
import math

import jax
import jax.numpy as jnp
from jax import lax
from jax.sharding import PartitionSpec as P

HEAD = 64
ROT = 16
LAYERS = 2
SEQ_LEN = 1024
BLOCK = 512


EPS = 1e-05
NEG = -1e30
F32 = jnp.float32
B16 = jnp.bfloat16


def layer_norm(stream, gain_vec, shift_vec):
    average = jnp.mean(stream, axis=-1, keepdims=True)
    centred = stream - average
    variance = jnp.mean(centred * centred, axis=-1, keepdims=True)
    return centred * lax.rsqrt(variance + EPS) * gain_vec + shift_vec


def both_norms(stream, gains, shifts):
    return (layer_norm(stream, gains[0], shifts[0]), layer_norm(stream, gains[1], shifts[1]))


def rope_tables(length):
    positions = (jnp.arange(length, dtype=jnp.int32) % SEQ_LEN).astype(F32)
    inverse = jnp.exp(jnp.arange(ROT // 2, dtype=F32) * (-2.0 * math.log(10000.0) / ROT))
    angles = positions[:, None] * inverse[None, :]
    angles = jnp.concatenate([angles, angles], axis=1)
    return (jnp.cos(angles), jnp.sin(angles))


def rotate(tensor_in, cosine_table, sine_table):
    head_part = tensor_in[..., :ROT]
    front_half = head_part[..., : ROT // 2]
    back_half = head_part[..., ROT // 2 :]
    turned = jnp.concatenate([-back_half, front_half], axis=-1)
    return jnp.concatenate(
        [head_part * cosine_table + turned * sine_table, tensor_in[..., ROT:]], axis=-1
    )


def matmul_tn(left, right):
    return lax.dot_general(left, right, (((0,), (0,)), ((), ())), preferred_element_type=F32)


def matmul_nt(left, right):
    return lax.dot_general(left, right, (((1,), (1,)), ((), ())), preferred_element_type=F32)


def masked_scores(q_block, key_part, first_row):
    scaling = HEAD ** (-0.5)
    columns = jnp.arange(key_part.shape[0], dtype=jnp.int32)
    scores = jnp.einsum("qhe,khe->hqk", q_block, key_part, preferred_element_type=F32) * scaling
    row_index = first_row + jnp.arange(BLOCK, dtype=jnp.int32)
    return jnp.where(columns[None, None, :] <= row_index[None, :, None], scores, NEG)


def attend_forward(queries, key_rows, value_rows):
    context_list = []
    max_list = []
    total_list = []
    for block_index in range(SEQ_LEN // BLOCK):
        first_row = block_index * BLOCK
        key_count = first_row + BLOCK
        q_block = queries[first_row:key_count]
        scores = masked_scores(q_block, key_rows[:key_count], first_row)
        row_max = jnp.max(scores, axis=-1)
        exponent = jnp.exp(scores - row_max[..., None])
        totals = jnp.sum(exponent, axis=-1)
        weights_low = (exponent / totals[..., None]).astype(B16)
        context = jnp.einsum(
            "hqk,khe->qhe", weights_low, value_rows[:key_count], preferred_element_type=F32
        )
        context_list.append(context.astype(B16))
        max_list.append(row_max)
        total_list.append(totals)
    return (jnp.concatenate(context_list, axis=0), jnp.stack(max_list), jnp.stack(total_list))


def attend_backward(queries, key_rows, value_rows, d_context, row_max, totals):
    scaling = HEAD ** (-0.5)
    d_keys = jnp.zeros(key_rows.shape, F32)
    d_values = jnp.zeros(key_rows.shape, F32)
    query_list = []
    for block_index in range(SEQ_LEN // BLOCK):
        first_row = block_index * BLOCK
        key_count = first_row + BLOCK
        q_block = queries[first_row:key_count]
        d_block = d_context[first_row:key_count]
        key_part = key_rows[:key_count]
        scores = masked_scores(q_block, key_part, first_row)
        weights = jnp.exp(scores - row_max[block_index][..., None]) / totals[block_index][..., None]
        d_weights = jnp.einsum(
            "qhe,khe->hqk", d_block, value_rows[:key_count], preferred_element_type=F32
        )
        inner_sum = jnp.sum(weights * d_weights, axis=-1, keepdims=True)
        d_scores = (weights * (d_weights - inner_sum)).astype(B16)
        query_list.append(
            jnp.einsum("hqk,khe->qhe", d_scores, key_part, preferred_element_type=F32) * scaling
        )
        padding = ((0, SEQ_LEN - key_count), (0, 0), (0, 0))
        key_term = (
            jnp.einsum("hqk,qhe->khe", d_scores, q_block, preferred_element_type=F32) * scaling
        )
        value_term = jnp.einsum(
            "hqk,qhe->khe", weights.astype(B16), d_block, preferred_element_type=F32
        )
        d_keys = d_keys + jnp.pad(key_term, padding)
        d_values = d_values + jnp.pad(value_term, padding)
    return (jnp.concatenate(query_list, axis=0), d_keys, d_values)


def on_device(
    tokens,
    cotangent,
    qkv_weight,
    qkv_bias,
    out_weight,
    out_bias,
    up_weight,
    up_bias,
    down_weight,
    down_bias,
    norm_gain,
    norm_shift,
):
    local_rows = tokens.shape[0]
    features = tokens.shape[1]
    group_rows = local_rows * lax.axis_size("tensor")
    sequences = group_rows // SEQ_LEN
    heads_dev = qkv_weight.shape[2] // (3 * HEAD)
    cosine_table, sine_table = rope_tables(group_rows)
    cosine_table = cosine_table[:, None, None, :]
    sine_table = sine_table[:, None, None, :]
    seq_shape = (sequences, SEQ_LEN, heads_dev, HEAD)
    flat_shape = (group_rows, heads_dev, HEAD)
    stream = tokens.astype(F32)
    stored = []
    stat_terms = []
    for layer_index in range(LAYERS):
        gains = norm_gain[layer_index].astype(F32)
        shifts = norm_shift[layer_index].astype(F32)
        normed_a, normed_b = both_norms(stream, gains, shifts)
        low_a = normed_a.astype(B16)
        low_b = normed_b.astype(B16)
        rows_a, ffn_input = (
            lax.all_gather(low_a, "tensor", axis=0, tiled=True),
            lax.all_gather(low_b, "tensor", axis=0, tiled=True),
        )
        up_local = up_weight[layer_index]
        up_bias_local = up_bias[layer_index]
        down_local = down_weight[layer_index]
        qkv_rows = jnp.dot(rows_a, qkv_weight[layer_index], preferred_element_type=F32) + qkv_bias[
            layer_index
        ].astype(F32)
        qkv_rows = qkv_rows.reshape(group_rows, heads_dev, 3, HEAD)
        turned = rotate(qkv_rows[:, :, :2], cosine_table, sine_table).astype(B16)
        queries = turned[:, :, 0].reshape(seq_shape)
        key_rows = turned[:, :, 1].reshape(seq_shape)
        value_rows = qkv_rows[:, :, 2].astype(B16).reshape(seq_shape)
        context, row_max, totals = lax.map(
            lambda parts: attend_forward(parts[0], parts[1], parts[2]),
            (queries, key_rows, value_rows),
        )
        context = context.reshape(group_rows, heads_dev * HEAD)
        pre_gelu = jnp.dot(ffn_input, up_local, preferred_element_type=F32) + up_bias_local.astype(
            F32
        )
        hidden = jax.nn.gelu(pre_gelu, approximate=False).astype(B16)
        out_local = out_weight[layer_index]
        context_part = lax.slice_in_dim(context, 0, local_rows * lax.axis_size("tensor"), axis=0)
        hidden_part = lax.slice_in_dim(hidden, 0, local_rows * lax.axis_size("tensor"), axis=0)
        both_terms = lax.psum_scatter(
            jnp.concatenate(
                [
                    jnp.dot(context_part, out_local, preferred_element_type=F32),
                    jnp.dot(hidden_part, down_local, preferred_element_type=F32),
                ],
                axis=1,
            ),
            "tensor",
            scatter_dimension=0,
            tiled=True,
        )
        attention_out = both_terms[:, :features] + out_bias[layer_index].astype(F32)
        ffn_out = both_terms[:, features:] + down_bias[layer_index].astype(F32)
        new_stream = stream + attention_out + ffn_out
        stat_terms.append(
            jnp.stack(
                [
                    jnp.sum(new_stream * new_stream),
                    jnp.sum(attention_out * attention_out),
                    jnp.sum(ffn_out * ffn_out),
                ]
            )
        )
        stored.append(
            (
                stream,
                rows_a,
                ffn_input,
                queries,
                key_rows,
                value_rows,
                context,
                row_max,
                totals,
                pre_gelu,
                hidden,
                up_local,
                down_local,
            )
        )
        stream = new_stream
    grad_stream = cotangent.astype(F32)
    qkv_w_list = [None] * LAYERS
    qkv_b_list = [None] * LAYERS
    out_w_list = [None] * LAYERS
    up_w_list = [None] * LAYERS
    up_b_list = [None] * LAYERS
    down_w_list = [None] * LAYERS
    bias_list = [None] * LAYERS
    gain_list = [None] * LAYERS
    shift_list = [None] * LAYERS
    for layer_index in reversed(range(LAYERS)):
        (
            stream_in,
            rows_a,
            ffn_input,
            queries,
            key_rows,
            value_rows,
            context,
            row_max,
            totals,
            pre_gelu,
            hidden,
            up_local,
            down_local,
        ) = stored[layer_index]
        gains = norm_gain[layer_index].astype(F32)
        shifts = norm_shift[layer_index].astype(F32)
        low_grad = grad_stream.astype(B16)
        grad_rows = lax.all_gather(low_grad, "tensor", axis=0, tiled=True)
        out_w_grad = matmul_tn(context, grad_rows)
        d_context = matmul_nt(grad_rows, out_weight[layer_index]).astype(B16).reshape(seq_shape)
        d_queries, d_keys, d_values = lax.map(
            lambda parts: attend_backward(
                parts[0], parts[1], parts[2], parts[3], parts[4], parts[5]
            ),
            (queries, key_rows, value_rows, d_context, row_max, totals),
        )
        pair_grads = jnp.stack([d_queries.reshape(flat_shape), d_keys.reshape(flat_shape)], axis=2)
        rope_input = jnp.zeros((group_rows, heads_dev, 2, HEAD), F32)
        rope_back = jax.vjp(
            lambda tensor_in: rotate(tensor_in, cosine_table, sine_table), rope_input
        )[1]
        d_turned = rope_back(pair_grads)[0]
        d_qkv = jnp.concatenate([d_turned, d_values.reshape(flat_shape)[:, :, None]], axis=2)
        d_qkv = d_qkv.reshape(group_rows, heads_dev * 3 * HEAD).astype(B16)
        qkv_b_grad = jnp.sum(d_qkv, axis=0, dtype=F32)
        qkv_w_grad = matmul_tn(rows_a, d_qkv)
        down_w_grad = matmul_tn(hidden, grad_rows)
        d_hidden = matmul_nt(grad_rows, down_local)
        gelu_back = jax.vjp(lambda pre_value: jax.nn.gelu(pre_value, approximate=False), pre_gelu)[
            1
        ]
        d_pre = gelu_back(d_hidden)[0].astype(B16)
        up_b_grad = jnp.sum(d_pre, axis=0, dtype=F32)
        up_w_grad = matmul_tn(ffn_input, d_pre)
        qkv_local = qkv_weight[layer_index]
        pre_part = lax.slice_in_dim(d_pre, 0, local_rows * lax.axis_size("tensor"), axis=0)
        both_grads = lax.psum_scatter(
            jnp.concatenate([matmul_nt(d_qkv, qkv_local), matmul_nt(pre_part, up_local)], axis=1),
            "tensor",
            scatter_dimension=0,
            tiled=True,
        )
        norm_back = jax.vjp(both_norms, stream_in, gains, shifts)[1]
        d_stream, gain_grad, shift_grad = norm_back(
            (both_grads[:, :features], both_grads[:, features:])
        )
        grad_stream = grad_stream + d_stream
        qkv_w_list[layer_index] = qkv_w_grad
        qkv_b_list[layer_index] = qkv_b_grad
        out_w_list[layer_index] = out_w_grad
        up_w_list[layer_index] = up_w_grad
        up_b_list[layer_index] = up_b_grad
        down_w_list[layer_index] = down_w_grad
        bias_list[layer_index] = jnp.sum(low_grad, axis=0, dtype=F32)
        gain_list[layer_index] = gain_grad
        shift_list[layer_index] = shift_grad
    qkv_w_all = jnp.stack(qkv_w_list)
    qkv_b_all = jnp.stack(qkv_b_list)
    out_w_all = jnp.stack(out_w_list)
    up_w_all = jnp.stack(up_w_list)
    up_b_all = jnp.stack(up_b_list)
    down_w_all = jnp.stack(down_w_list)
    qkv_w_all, qkv_b_all, out_w_all, up_w_all, up_b_all, down_w_all = lax.psum(
        (qkv_w_all, qkv_b_all, out_w_all, up_w_all, up_b_all, down_w_all), "dp"
    )
    bias_all, gain_all, shift_all, stat_all = lax.psum(
        (jnp.stack(bias_list), jnp.stack(gain_list), jnp.stack(shift_list), jnp.stack(stat_terms)),
        ("dp", "tensor"),
    )
    total_cells = local_rows * lax.axis_size("dp") * lax.axis_size("tensor") * features
    layer_stats = jnp.sqrt(stat_all / total_cells)
    return (
        stream,
        grad_stream,
        qkv_w_all,
        qkv_b_all,
        out_w_all,
        bias_all,
        up_w_all,
        up_b_all,
        down_w_all,
        bias_all,
        gain_all,
        shift_all,
        layer_stats,
    )


def solution(mesh):
    in_specs = (
        P(("dp", "tensor"), None),
        P(("dp", "tensor"), None),
        P(None, None, "tensor"),
        P(None, "tensor"),
        P(None, "tensor", None),
        P(),
        P(None, None, "tensor"),
        P(None, "tensor"),
        P(None, "tensor", None),
        P(),
        P(),
        P(),
    )
    out_specs = (
        P(("dp", "tensor"), None),
        P(("dp", "tensor"), None),
        P(None, None, "tensor"),
        P(None, "tensor"),
        P(None, "tensor", None),
        P(),
        P(None, None, "tensor"),
        P(None, "tensor"),
        P(None, "tensor", None),
        P(),
        P(),
        P(),
        P(),
    )
    return jax.shard_map(
        on_device, mesh=mesh, in_specs=in_specs, out_specs=out_specs, check_vma=False
    )
```

profile of v0, /device:TPU:0, one launch (start us, length us, event | category | flops | bytes accessed | tf_op | source)
XLA Modules:
  0.0 2084.7 jit_solution(10877414772915968582)
XLA Ops:
  16.2 35.0 %all-gather.7.cloned.1.call-done = bf16[2048,1024]{0,1:T(8,128)(2,1)} async-done(((bf16[512,1024]{0,1:T(8,128)(2,1)}), bf16[2048,1024]{0,1:T(8,128)(2,1)}) %all-gather.7.cloned.1.call-update) | async-done | bytes 4194320 | tf_op jit(solution)/shard_map/all_gather | solution.py:155
  71.7 30.4 %while.60 = (s32[]{:T(128)}, bf16[2,1024,4,64]{1,3,2,0:T(8,128)(2,1)S(1)}, f32[2,2,4,512]{3,2,1,0:T(4,128)}, f32[2,2,4,512]{3,2,1,0:T(4,128)}, bf16[2,1024,4,64]...) while((s32[]{:T(128)}, ...), condition=%wide.region_7.8_spmd, body=%wide.region_2.7_spmd.sunk | while | flops 845152768 | bytes 44718728 | solution.py:169
  109.1 26.6 %multiply_convert_fusion.5 = (bf16[2048,1024]{1,0:T(8,128)(2,1)S(1)}, f32[2048,1024]{1,0:T(8,128)}, f32[2048,1024]{1,0:T(8,128)}) fusion(f32[1024]{0:T(1024)S(1)} %bitcast.668, bf16[2048,1024]{0,1:T(8,128)(2,1)} %all-gather.9.cloned.1.call-done, bf16[2,1024,1024]{2,1,0:T(8,128)(2,1)} %param.26), kind=kOutput, calls=%fused_computation.225 | convolution fusion | flops 4433379328 | bytes 27267072 | tf_op jit(solution)/shard_map/dot_general | solution.py:174
  148.9 124.3 %reduce-scatter.5.cloned.1.call-done = f32[512,2048]{0,1:T(8,128)} async-done(((f32[2048,2048]{0,1:T(8,128)}), f32[512,2048]{0,1:T(8,128)}) %reduce-scatter.5.cloned.1.call-update) | async-done | bytes 4194320 | tf_op jit(solution)/shard_map/reduce_scatter | solution.py:181
  282.5 26.7 %all-gather.15.cloned.1.call-done = bf16[2048,1024]{1,0:T(8,128)(2,1)} async-done(((bf16[512,1024]{1,0:T(8,128)(2,1)}), bf16[2048,1024]{1,0:T(8,128)(2,1)}) %all-gather.15.cloned.1.call-update) | async-done | bytes 4194320 | tf_op jit(solution)/shard_map/all_gather | solution.py:252
  316.0 29.8 %all-gather.11.cloned.1.call-done = bf16[2048,1024]{0,1:T(8,128)(2,1)} async-done(((bf16[512,1024]{0,1:T(8,128)(2,1)}), bf16[2048,1024]{0,1:T(8,128)(2,1)}) %all-gather.11.cloned.1.call-update) | async-done | bytes 4194320 | tf_op jit(solution)/shard_map/all_gather | solution.py:155
  364.9 29.0 %while.61 = (s32[]{:T(128)}, bf16[2,1024,4,64]{1,3,2,0:T(8,128)(2,1)S(1)}, f32[2,2,4,512]{3,2,1,0:T(4,128)S(1)}, f32[2,2,4,512]{3,2,1,0:T(4,128)S(1)}, bf16[2,10...) while((s32[]{:T(128)}, ...), condition=%wide.region_16.17_spmd, body=%wide.region_11.16_spmd.sunk | while | flops 845152768 | bytes 44718728 | solution.py:169
  398.0 167.1 %while.62 = (s32[]{:T(128)}, f32[2,1024,4,64]{1,0,3,2:T(2,128)}, f32[2,1024,4,64]{1,0,3,2:T(2,128)}, bf16[2,1024,4,64]{1,0,3,2:T(2,128)(2,1)}, bf16[2,1024,4,64]...) while((s32[]{:T(128)}, f32[2,1024,4,64]{1,0,3,2:T(2,128)}, ...), condition=%wide.region_21.22_spmd, body=%wide.region_18.21_spmd.sunk | while | flops 2047209984 | bytes 117843160 | solution.py:255
  426.6 17.5 dynamic_update_slice.79
  444.2 18.8 dynamic_update_slice.78
  462.9 18.8 dynamic_update_slice.77
  509.9 17.5 dynamic_update_slice.79
  527.5 18.8 dynamic_update_slice.78
  546.2 18.8 dynamic_update_slice.77
  587.5 26.7 %multiply_convert_fusion.4 = (bf16[2048,1024]{1,0:T(8,128)(2,1)}, f32[2048,1024]{1,0:T(8,128)}, f32[2048,1024]{1,0:T(8,128)}) fusion(f32[1024]{0:T(1024)S(1)} %bitcast.670, bf16[2048,1024]{0,1:T(8,128)(2,1)} %all-gather.13.cloned.1.call-done, bf16[2,1024,1024]{2,1,0:T(8,128)(2,1)} %param.26), kind=kOutput, calls=%fused_computation.212 | convolution fusion | flops 4433379328 | bytes 27267072 | tf_op jit(solution)/shard_map/dot_general | solution.py:174
  614.3 12.6 convert_reduce_fusion
  650.1 10.1 pad_maximum_fusion.1
  662.3 102.2 %reduce-scatter.9.cloned.1.call-done = f32[512,2048]{0,1:T(8,128)} async-done(((f32[2048,2048]{0,1:T(8,128)}), f32[512,2048]{0,1:T(8,128)}) %reduce-scatter.9.cloned.1.call-update) | async-done | bytes 4194320 | tf_op jit(solution)/shard_map/reduce_scatter | solution.py:281
  768.6 124.7 %reduce-scatter.7.cloned.1.call-done = f32[512,2048]{0,1:T(8,128)} async-done(((f32[2048,2048]{0,1:T(8,128)}), f32[512,2048]{0,1:T(8,128)}) %reduce-scatter.7.cloned.1.call-update) | async-done | bytes 4194320 | tf_op jit(solution)/shard_map/reduce_scatter | solution.py:181
  902.7 34.6 %all-gather.17.cloned.1.call-done = bf16[2048,1024]{0,1:T(8,128)(2,1)} async-done(((bf16[512,1024]{0,1:T(8,128)(2,1)}), bf16[2048,1024]{0,1:T(8,128)(2,1)}) %all-gather.17.cloned.1.call-update) | async-done | bytes 4194320 | tf_op jit(solution)/shard_map/all_gather | solution.py:252
  948.1 168.6 %while.63 = (s32[]{:T(128)}, f32[2,1024,4,64]{1,0,3,2:T(2,128)}, f32[2,1024,4,64]{1,0,3,2:T(2,128)}, bf16[2,1024,4,64]{1,0,3,2:T(2,128)(2,1)}, bf16[2,1024,4,64]...) while((s32[]{:T(128)}, f32[2,1024,4,64]{1,0,3,2:T(2,128)}, ...), condition=%wide.region_30.31_spmd, body=%wide.region_27.30_spmd.sunk | while | flops 2047209984 | bytes 117843160 | solution.py:255
  977.2 17.6 dynamic_update_slice.82
  994.8 18.8 dynamic_update_slice.81
  1013.6 18.8 dynamic_update_slice.80
  1061.3 17.6 dynamic_update_slice.82
  1078.8 18.8 dynamic_update_slice.81
  1097.6 18.8 dynamic_update_slice.80
  1144.9 13.3 convert_reduce_fusion.1
  1235.3 38.1 %all-reduce.21 = (f32[2,768]{1,0:T(2,128)}, f32[2,1024]{1,0:T(2,128)}) all-reduce(f32[2,768]{1,0:T(2,128)S(1)} %pad_maximum_fusion.15, f32[2,1024]{1,0:T(2,128)S(1)} %pad_maximum_fusion.14), channel_id=1, replica_groups=mesh['dp'=8,'tensor'=4] {'dp'}, use_global_device_ids=true, to_apply=%region_39.40 | all-reduce | flops 3584 | bytes 28672 | tf_op jit(solution)/shard_map/psum | solution.py:307
  1273.4 27.7 %reduce-scatter.11.cloned.1.call-done = f32[512,2048]{0,1:T(8,128)} async-done(((f32[2048,2048]{0,1:T(8,128)}), f32[512,2048]{0,1:T(8,128)}) %reduce-scatter.11.cloned.1.call-update) | async-done | bytes 4194320 | tf_op jit(solution)/shard_map/reduce_scatter | solution.py:281
  1310.0 45.9 %all-reduce.20 = (f32[2,1024]{1,0:T(2,128)S(1)}, f32[2,2,1024]{2,1,0:T(2,128)}, f32[2,2,1024]{2,1,0:T(2,128)}, f32[2,3]{1,0:T(2,128)S(1)}) all-reduce(f32[2,1024]{1,0:T(2,128)S(1)} %pad_maximum_fusion.13, f32[2,2,1024]{2,1,0:T(2,128)S(1)} %pad_maximum_fusion.11, ...), channel_id=1, replica_groups=mesh['dp'=8,'tensor'=4] {'dp','tensor'}, use_global_device_ids=true, to_apply=%region_43.44 | all-reduce | flops 10246 | bytes 81968 | tf_op jit(solution)/shard_map/psum | solution.py:310
  1359.3 700.1 %all-reduce.25.cloned.1.call-done = (f32[2,1024,768]{2,1,0:T(8,128)}, f32[2,256,1024]{2,1,0:T(8,128)}, f32[2,1024,1024]{2,1,0:T(8,128)}, f32[2,1024,1024]{2,1,0:T(8,128)}) async-done(((f32[2,1024,768]{2,1,0:T(8,128)}, f32[2,256,1024]{2,1,0:T(8,128)}, f32[2,1024,1024]{2,1,0:T(8,128)}, f32[2,1024,1024]{2,1,0:T(8,128)}), (f32[2,1024,768]{2,1,0:T(8,128)}, f32[2,256,1024]{2,1,0:T(8,128)}, ...) | async-done | bytes 25165840 | tf_op jit(solution)/shard_map/psum | solution.py:307
  (536 shorter events, 468.7 us)
Async XLA Ops:
  7.2 44.0 %all-gather.7.cloned.1.call-start = ((), (), s32[]{:S(2)}) async-start(), calls=%async_computation.4 | async-start | bytes 5242880 | tf_op jit(solution)/shard_map/all_gather | solution.py:155
  10.1 46.8 %copy-start = (bf16[512,1024]{0,1:T(8,128)(2,1)}, bf16[512,1024]{0,1:T(8,128)(2,1)S(1)}, u32[]{:S(2)}) copy-start(bf16[512,1024]{0,1:T(8,128)(2,1)S(1)} %copy.137) | copy-start | bytes 3145732
  13.8 95.3 %all-gather.9.cloned.1.call-start = ((), (), s32[]{:S(2)}) async-start(), calls=%async_computation.5 | async-start | bytes 5242880 | tf_op jit(solution)/shard_map/all_gather | solution.py:156
  14.6 258.6 %reduce-scatter.5.cloned.1.call-start = ((), (), s32[]{:S(2)}) async-start(), calls=%async_computation.6 | async-start | bytes 20971520 | tf_op jit(solution)/shard_map/reduce_scatter | solution.py:181
  15.9 93.3 %copy-start.87 = (f32[1,1024]{1,0:T(1,128)}, f32[1,1024]{1,0:T(1,128)S(1)}, u32[]{:S(2)}) copy-start(f32[1,1024]{1,0:T(1,128)S(1)} %get-tuple-element.727) | copy-start | bytes 12292
  16.2 48.4 %copy-start.29 = (f32[2048,16]{0,1:T(8,128)}, f32[2048,16]{0,1:T(8,128)S(1)}, u32[]{:S(2)}) copy-start(f32[2048,16]{0,1:T(8,128)S(1)} %get-tuple-element.710) | copy-start | bytes 393220
  16.2 48.4 %copy-start.33 = (f32[2048,16]{0,1:T(8,128)}, f32[2048,16]{0,1:T(8,128)S(1)}, u32[]{:S(2)}) copy-start(f32[2048,16]{0,1:T(8,128)S(1)} %get-tuple-element.711) | copy-start | bytes 393220
  147.0 126.2 %copy-start.1 = (bf16[512,1024]{0,1:T(8,128)(2,1)S(1)}, bf16[512,1024]{0,1:T(8,128)(2,1)}, u32[]{:S(2)}) copy-start(bf16[512,1024]{0,1:T(8,128)(2,1)} %copy-done) | copy-start | bytes 3145732
  147.0 162.2 %all-gather.15.cloned.1.call-start = ((), (), s32[]{:S(2)}) async-start(), calls=%async_computation.10 | async-start | bytes 5242880 | tf_op jit(solution)/shard_map/all_gather | solution.py:252
  147.6 198.2 %all-gather.11.cloned.1.call-start = ((), (), s32[]{:S(2)}) async-start(), calls=%async_computation.7 | async-start | bytes 5242880 | tf_op jit(solution)/shard_map/all_gather | solution.py:155
  280.0 307.6 %all-gather.13.cloned.1.call-start = ((), (), s32[]{:S(2)}) async-start(), calls=%async_computation.8 | async-start | bytes 5242880 | tf_op jit(solution)/shard_map/all_gather | solution.py:156
  316.0 448.5 %reduce-scatter.9.cloned.1.call-start = ((), (), s32[]{:S(2)}) async-start(), calls=%async_computation.11 | async-start | bytes 20971520 | tf_op jit(solution)/shard_map/reduce_scatter | solution.py:281
  638.2 255.1 %reduce-scatter.7.cloned.1.call-start = ((), (), s32[]{:S(2)}) async-start(), calls=%async_computation.9 | async-start | bytes 20971520 | tf_op jit(solution)/shard_map/reduce_scatter | solution.py:181
  660.2 104.3 %copy-start.4 = (f32[512,1024]{0,1:T(8,128)S(1)}, f32[512,1024]{0,1:T(8,128)}, u32[]{:S(2)}) copy-start(f32[512,1024]{0,1:T(8,128)} %copy-done.3) | copy-start | bytes 6291460
  660.2 104.3 %copy-start.54 = (f32[1,1,1024]{2,1,0:T(1,128)S(1)}, f32[1,1,1024]{2,1,0:T(1,128)}, u32[]{:S(2)}) copy-start(f32[1,1,1024]{2,1,0:T(1,128)} %get-tuple-element.712) | copy-start | bytes 12292
  660.2 104.3 %copy-start.56 = (f32[1,1,1024]{2,1,0:T(1,128)S(1)}, f32[1,1,1024]{2,1,0:T(1,128)}, u32[]{:S(2)}) copy-start(f32[1,1,1024]{2,1,0:T(1,128)} %get-tuple-element.713) | copy-start | bytes 12292
  660.2 104.3 %copy-start.58 = (f32[512]{0:T(512)S(1)}, f32[512]{0:T(512)}, u32[]{:S(2)}) copy-start(f32[512]{0:T(512)} %copy-done.57) | copy-start | bytes 6148
  660.2 104.3 %copy-start.60 = (f32[512]{0:T(512)S(1)}, f32[512]{0:T(512)}, u32[]{:S(2)}) copy-start(f32[512]{0:T(512)} %copy-done.59) | copy-start | bytes 6148
  660.2 108.3 %copy-start.71 = (f32[512]{0:T(512)S(1)}, f32[512]{0:T(512)}, u32[]{:S(2)}) copy-start(f32[512]{0:T(512)} %copy-done.70) | copy-start | bytes 6148
  660.3 233.0 %copy-start.72 = (f32[1,1024]{1,0:T(1,128)S(1)}, f32[1,1024]{1,0:T(1,128)}, u32[]{:S(2)}) copy-start(f32[1,1024]{1,0:T(1,128)} %get-tuple-element.724) | copy-start | bytes 12292
  660.3 233.0 %copy-start.73 = (f32[1,1024]{1,0:T(1,128)S(1)}, f32[1,1024]{1,0:T(1,128)}, u32[]{:S(2)}) copy-start(f32[1,1024]{1,0:T(1,128)} %get-tuple-element.729) | copy-start | bytes 12292
  660.3 277.0 %all-gather.17.cloned.1.call-start = ((), (), s32[]{:S(2)}) async-start(), calls=%async_computation.12 | async-start | bytes 5242880 | tf_op jit(solution)/shard_map/all_gather | solution.py:252
  662.3 237.0 %copy-start.12 = (bf16[512,1024]{0,1:T(8,128)(2,1)}, bf16[512,1024]{0,1:T(8,128)(2,1)S(1)}, u32[]{:S(2)}) copy-start(bf16[512,1024]{0,1:T(8,128)(2,1)S(1)} %copy.154) | copy-start | bytes 3145732
  902.6 398.5 %reduce-scatter.11.cloned.1.call-start = ((), (), s32[]{:S(2)}) async-start(), calls=%async_computation.13 | async-start | bytes 20971520 | tf_op jit(solution)/shard_map/reduce_scatter | solution.py:281
  1174.8 884.7 %all-reduce.25.cloned.1.call-start = ((), (), s32[]{:S(2)}) async-start(), calls=%async_computation.14 | async-start | bytes 50331648 | tf_op jit(solution)/shard_map/psum | solution.py:307
  1227.7 73.4 %copy-start.2 = (bf16[512,1024]{0,1:T(8,128)(2,1)S(1)}, bf16[512,1024]{0,1:T(8,128)(2,1)}, u32[]{:S(2)}) copy-start(bf16[512,1024]{0,1:T(8,128)(2,1)} %copy-done) | copy-start | bytes 3145732
  1227.7 73.4 %copy-start.48 = (f32[1,1,1024]{2,1,0:T(1,128)S(1)}, f32[1,1,1024]{2,1,0:T(1,128)}, u32[]{:S(2)}) copy-start(f32[1,1,1024]{2,1,0:T(1,128)} %copy-done.47) | copy-start | bytes 12292
  1227.7 73.4 %copy-start.50 = (f32[1,1,1024]{2,1,0:T(1,128)S(1)}, f32[1,1,1024]{2,1,0:T(1,128)}, u32[]{:S(2)}) copy-start(f32[1,1,1024]{2,1,0:T(1,128)} %copy-done.49) | copy-start | bytes 12292
  1227.7 73.4 %copy-start.52 = (f32[512]{0:T(512)S(1)}, f32[512]{0:T(512)}, u32[]{:S(2)}) copy-start(f32[512]{0:T(512)} %copy-done.51) | copy-start | bytes 6148
  1229.4 74.7 %copy-start.69 = (f32[512]{0:T(512)S(1)}, f32[512]{0:T(512)}, u32[]{:S(2)}) copy-start(f32[512]{0:T(512)} %copy-done.68) | copy-start | bytes 6148
  1229.4 74.8 %copy-start.62 = (f32[512]{0:T(512)S(1)}, f32[512]{0:T(512)}, u32[]{:S(2)}) copy-start(f32[512]{0:T(512)} %copy-done.61) | copy-start | bytes 6148
  1355.9 710.7 %copy-start.85 = (f32[2,1024]{1,0:T(2,128)}, f32[2,1024]{1,0:T(2,128)S(1)}, u32[]{:S(2)}) copy-start(f32[2,1024]{1,0:T(2,128)S(1)} %get-tuple-element.1183) | copy-start | bytes 24580
  (94 other events, 688.5 us)
Sparse Core Ops, SparseCore 0:
  14.0 37.1 all-gather.6
  53.3 34.4 all-gather.8
  147.1 126.0 reduce-scatter.4
  274.7 34.4 all-gather.14
  311.3 34.4 all-gather.10
  347.3 34.4 all-gather.12
  638.3 126.1 reduce-scatter.8
  767.0 126.1 reduce-scatter.6
  902.7 34.4 all-gather.16
  1174.9 126.1 reduce-scatter.10
  1307.2 752.2 all-reduce.24
where the time goes:
time: 2110 us; the launch traced here: 2080 us
  waiting for transfers between devices  1210 us (57%)
  local copies, waits for them, and re-layouts  357 us (17%)
  matrix products  299 us (14%)
  other arithmetic  120 us (6%)
  blocking collectives  84 us (4%)
    psum x1, waiting for transfers between devices, on_device(): lax.psum((qkv_w_all, qkv_b_all, out_w_all, up_w_all, up_b_all, down_w_all...  700 us
    reduce_scatter x2, waiting for transfers between devices, on_device(): lax.psum_scatter(jnp.concatenate([jnp.dot(context_part, out_local, prefer...  249 us
    dynamic_update_slice x24, local copies, waits for them, and re-layouts, on_device(): lax.map(lambda parts: attend_backward(parts[0], parts[1], parts[2], parts...  232 us
    reduce_scatter x2, waiting for transfers between devices, on_device(): lax.psum_scatter(jnp.concatenate([matmul_nt(d_qkv, qkv_local), matmul_nt(...  130 us
    all_gather x2, waiting for transfers between devices, on_device(): lax.all_gather(low_a, 'tensor', axis=0, tiled=True)  64.7 us
    all_gather x2, waiting for transfers between devices, on_device(): grad_rows = lax.all_gather(low_grad, 'tensor', axis=0, tiled=True)  61.3 us
    unnamed x248, local copies, waits for them, and re-layouts  61.2 us
    dot_general x2, matrix products, on_device(): jnp.dot(ffn_input, up_local, preferred_element_type=F32)  53.3 us
  transfers between devices with their start and end apart: 11, of which 9 were waited for; matrix products, arithmetic and copies ran while one was open for 19% of the time, Pallas kernels for 0%

commit v1 on v0

v1 whole, which is shorter than its diff:
```python
import functools
import math

import jax
import jax.numpy as jnp
from jax import lax
from jax.experimental import pallas as pl
from jax.experimental.pallas import tpu as pltpu
from jax.sharding import PartitionSpec as P

HEAD = 64
ROT = 16
LAYERS = 2
SEQ_LEN = 1024
QB = 256
SCALE = HEAD ** (-0.5)

EPS = 1e-05
NEG = -1e30
F32 = jnp.float32
B16 = jnp.bfloat16
MIB = 1024 * 1024


def dot_nn(left, right):
    return lax.dot_general(left, right, (((1,), (0,)), ((), ())), preferred_element_type=F32)


def dot_nt(left, right):
    return lax.dot_general(left, right, (((1,), (1,)), ((), ())), preferred_element_type=F32)


def dot_tn(left, right):
    return lax.dot_general(left, right, (((0,), (0,)), ((), ())), preferred_element_type=F32)


def rope_tables(seq, width):
    positions = jnp.arange(seq, dtype=jnp.int32).astype(F32)
    inverse = jnp.exp(jnp.arange(ROT // 2, dtype=F32) * (-2.0 * math.log(10000.0) / ROT))
    angles = positions[:, None] * inverse[None, :]
    cosine, sine = jnp.cos(angles), jnp.sin(angles)
    zero = jnp.zeros_like(sine)
    rest = jnp.zeros((seq, HEAD - ROT), F32)
    repeat = lambda parts: jnp.tile(jnp.concatenate(parts, axis=1), (1, width // HEAD))
    return (
        repeat([cosine, cosine, rest + 1.0]),
        repeat([-sine, zero, rest]),
        repeat([zero, sine, rest]),
    )


def rope(rows, cos, sin_lo, sin_hi, sign):
    width = cos.shape[1]
    parts = []
    for j in range(rows.shape[1] // width):
        part = rows[:, j * width : (j + 1) * width]
        turned = (
            pltpu.roll(part, width - ROT // 2, 1) * sin_lo + pltpu.roll(part, ROT // 2, 1) * sin_hi
        )
        parts.append(part * cos + turned if sign > 0 else part * cos - turned)
    return parts[0] if len(parts) == 1 else jnp.concatenate(parts, axis=1)


def attend_forward_kernel(
    w, seq, x_ref, w_ref, b_ref, cos_ref, lo_ref, hi_ref, qkv_ref, ctx_ref, lse_ref
):
    h = pl.program_id(0)
    blocks = seq // QB
    shift = (lax.axis_index("tensor") % 2) * (blocks // 2)
    swapped = lambda i: pl.ds(pl.multiple_of(lax.rem(i + shift, blocks) * QB, QB), QB)

    @pl.when(h == 0)
    def _():
        lse_ref[...] = jnp.zeros_like(lse_ref)
        ctx_ref[...] = jnp.zeros_like(ctx_ref)

        @pl.loop(0, seq // QB)
        def _(r):
            rows = pl.ds(pl.multiple_of(r * QB, QB), QB)
            acc = dot_nn(x_ref[swapped(r), :], w_ref[...]) + b_ref[...]
            turned = rope(acc[:, : 2 * w], cos_ref[rows, :], lo_ref[rows, :], hi_ref[rows, :], 1)
            qkv_ref[rows, : 2 * w] = turned.astype(B16)
            qkv_ref[rows, 2 * w :] = acc[:, 2 * w :].astype(B16)

    mine = (lax.broadcasted_iota(jnp.int32, (1, w), 1) // HEAD) == h
    keep = jnp.where(mine, SCALE, 0.0).astype(B16)
    for i in range(seq // QB):
        n = (i + 1) * QB
        q = qkv_ref[i * QB : n, :w] * keep
        s = dot_nt(q, qkv_ref[:n, w : 2 * w])
        tri = lax.broadcasted_iota(jnp.int32, (QB, QB), 0) >= lax.broadcasted_iota(
            jnp.int32, (QB, QB), 1
        )
        last = jnp.where(tri, s[:, n - QB :], NEG)
        s = last if i == 0 else jnp.concatenate([s[:, : n - QB], last], axis=1)
        top = jnp.max(s, axis=1, keepdims=True)
        p = jnp.exp(s - top)
        total = jnp.sum(p, axis=1, keepdims=True)
        low = (p * (1.0 / total)).astype(B16)
        c = dot_nn(low, qkv_ref[:n, 2 * w :])
        old = ctx_ref[swapped(i), :]
        ctx_ref[swapped(i), :] = jnp.where(mine, c, old.astype(F32)).astype(B16)
        lane = lax.broadcasted_iota(jnp.int32, (QB, 128), 1)
        lse_ref[i * QB : n, :] = jnp.where(lane == h, top + jnp.log(total), lse_ref[i * QB : n, :])


def whole(shape):
    return pl.BlockSpec(shape, lambda h: (0,) * len(shape))


def attend_forward(x, weight, bias, tables):
    seq, features = x.shape
    w = weight.shape[1] // 3
    heads = w // HEAD
    table = tables[0].shape
    return pl.pallas_call(
        functools.partial(attend_forward_kernel, w, seq),
        grid=(heads,),
        in_specs=[
            whole((seq, features)),
            whole((features, 3 * w)),
            whole((1, 3 * w)),
            whole(table),
            whole(table),
            whole(table),
        ],
        out_specs=[whole((seq, 3 * w)), whole((seq, w)), whole((seq, 128))],
        out_shape=[
            jax.ShapeDtypeStruct((seq, 3 * w), B16),
            jax.ShapeDtypeStruct((seq, w), B16),
            jax.ShapeDtypeStruct((seq, 128), F32),
        ],
        compiler_params=pltpu.CompilerParams(
            vmem_limit_bytes=40 * MIB, dimension_semantics=("arbitrary",)
        ),
        cost_estimate=pl.CostEstimate(
            flops=2 * seq * features * 3 * w + 4 * seq * seq * 256 * heads,
            bytes_accessed=2 * seq * features + 6 * features * w + 8 * seq * w,
            transcendentals=seq * seq * heads // 2,
        ),
        name="attend_forward",
    )(x, weight, bias, *tables)


def attend_backward_kernel(
    w,
    seq,
    qkv_ref,
    d_ref,
    lse_ref,
    cos_ref,
    lo_ref,
    hi_ref,
    out_ref,
    bias_ref,
    dq_ref,
    dk_ref,
    dv_ref,
):
    h = pl.program_id(0)
    heads = w // HEAD
    blocks = seq // QB
    shift = (lax.axis_index("tensor") % 2) * (blocks // 2)
    swapped = lambda i: pl.ds(pl.multiple_of(lax.rem(i + shift, blocks) * QB, QB), QB)

    @pl.when(h == 0)
    def _():
        dq_ref[...] = jnp.zeros_like(dq_ref)
        dk_ref[...] = jnp.zeros_like(dk_ref)
        dv_ref[...] = jnp.zeros_like(dv_ref)

    mine = (lax.broadcasted_iota(jnp.int32, (1, w), 1) // HEAD) == h
    keep = jnp.where(mine, SCALE, 0.0).astype(B16)
    keep_value = jnp.where(mine, 1.0, 0.0).astype(B16)
    for i in range(seq // QB):
        n = (i + 1) * QB
        q = qkv_ref[i * QB : n, :w] * keep
        d = d_ref[swapped(i), :] * keep_value
        s = dot_nt(q, qkv_ref[:n, w : 2 * w])
        lane = lax.broadcasted_iota(jnp.int32, (QB, 128), 1)
        lse = jnp.sum(jnp.where(lane == h, lse_ref[i * QB : n, :], 0.0), axis=1, keepdims=True)
        tri = lax.broadcasted_iota(jnp.int32, (QB, QB), 0) >= lax.broadcasted_iota(
            jnp.int32, (QB, QB), 1
        )
        last = jnp.where(tri, s[:, n - QB :], NEG)
        s = last if i == 0 else jnp.concatenate([s[:, : n - QB], last], axis=1)
        p = jnp.exp(s - lse)
        dp = dot_nt(d, qkv_ref[:n, 2 * w :])
        inner = jnp.sum(p * dp, axis=1, keepdims=True)
        ds = (p * (dp - inner)).astype(B16)
        dq_ref[i * QB : n, :] += dot_nn(ds, qkv_ref[:n, w : 2 * w] * keep)
        dk_ref[:n, :] += dot_tn(ds, q)
        dv_ref[:n, :] += dot_tn(p.astype(B16), d)

    @pl.when(h == heads - 1)
    def _():
        bias_ref[...] = jnp.zeros_like(bias_ref)

        @pl.loop(0, seq // QB)
        def _(r):
            rows = pl.ds(pl.multiple_of(r * QB, QB), QB)
            qk = jnp.concatenate([dq_ref[rows, :], dk_ref[rows, :]], axis=1)
            qk = rope(qk, cos_ref[rows, :], lo_ref[rows, :], hi_ref[rows, :], -1).astype(B16)
            v = dv_ref[rows, :].astype(B16)
            out_ref[swapped(r), : 2 * w] = qk
            out_ref[swapped(r), 2 * w :] = v
            bias_ref[:, : 2 * w] += jnp.sum(qk.astype(F32), axis=0, keepdims=True)
            bias_ref[:, 2 * w :] += jnp.sum(v.astype(F32), axis=0, keepdims=True)


def attend_backward(qkv, d_context, lse, tables):
    seq = qkv.shape[0]
    w = qkv.shape[1] // 3
    heads = w // HEAD
    table = tables[0].shape
    return pl.pallas_call(
        functools.partial(attend_backward_kernel, w, seq),
        grid=(heads,),
        in_specs=[
            whole((seq, 3 * w)),
            whole((seq, w)),
            whole((seq, 128)),
            whole(table),
            whole(table),
            whole(table),
        ],
        out_specs=[whole((seq, 3 * w)), whole((1, 3 * w))],
        out_shape=[
            jax.ShapeDtypeStruct((seq, 3 * w), B16),
            jax.ShapeDtypeStruct((1, 3 * w), F32),
        ],
        scratch_shapes=[pltpu.VMEM((seq, w), F32)] * 3,
        compiler_params=pltpu.CompilerParams(
            vmem_limit_bytes=40 * MIB, dimension_semantics=("arbitrary",)
        ),
        cost_estimate=pl.CostEstimate(
            flops=10 * seq * seq * 256 * heads,
            bytes_accessed=16 * seq * w,
            transcendentals=seq * seq * heads // 2,
        ),
        name="attend_backward",
    )(qkv, d_context, lse, *tables)


def normal_parts(u):
    x = jnp.abs(u) * (0.5**0.5)
    t = 1.0 / (1.0 + 0.3275911 * x)
    bell = jnp.exp(-0.5 * u * u)
    poly = t * (
        0.254829592
        + t * (-0.284496736 + t * (1.421413741 + t * (-1.453152027 + t * 1.061405429)))
    )
    half_tail = 0.5 * poly * bell
    return jnp.where(u >= 0.0, 1.0 - half_tail, half_tail), bell


def gelu(u):
    return u * normal_parts(u)[0]


def gelu_slope(u):
    share, bell = normal_parts(u)
    return share + u * bell * ((2.0 * math.pi) ** -0.5)


def standardize(x):
    average = jnp.mean(x, axis=-1, keepdims=True)
    centred = x - average
    variance = jnp.mean(centred * centred, axis=-1, keepdims=True)
    inverse = lax.rsqrt(variance + EPS)
    return centred * inverse, inverse


def swap(x, axis, bit):
    size = lax.axis_size(axis)
    return lax.ppermute(x, axis, [(i, i ^ bit) for i in range(size)])


def all_bits(size):
    bits = []
    bit = 1
    while bit < size:
        bits.append(bit)
        bit *= 2
    return bits


def after(x, *others):
    return lax.optimization_barrier((x,) + others)[0]


def on_device(
    tokens,
    cotangent,
    qkv_weight,
    qkv_bias,
    out_weight,
    out_bias,
    up_weight,
    up_bias,
    down_weight,
    down_bias,
    norm_gain,
    norm_shift,
):
    rows, features = tokens.shape
    tensor = lax.axis_size("tensor")
    dp = lax.axis_size("dp")
    chips = tensor // 2
    dp_index = lax.axis_index("dp")
    core = lax.axis_index("tensor") % 2
    w = qkv_weight.shape[2] // 3
    ff = up_weight.shape[2]
    heads = w // HEAD
    tables = rope_tables(SEQ_LEN, min(128, 2 * w))
    streams = range(chips)
    chip_bits = all_bits(chips)
    dp_bits = all_bits(dp)

    def core_gather(half):
        return jnp.concatenate([half, swap(half, "tensor", 1)], axis=0)

    def chip_gather(half):
        found = [half]
        for bit in chip_bits:
            found = found + [swap(item, "tensor", 2 * bit) for item in found]
        return found

    def chip_scatter(parts):
        for bit in reversed(chip_bits):
            sent = [swap(part.astype(B16), "tensor", 2 * bit) for part in parts[bit:]]
            parts = [part + got.astype(F32) for part, got in zip(parts[:bit], sent)]
        return parts[0]

    def chip_reduce(parts):
        for bit in chip_bits:
            low = [part.astype(B16) for part in parts]
            sent = [swap(part, "tensor", 2 * bit) for part in low]
            parts = [low[k].astype(F32) + sent[k ^ bit].astype(F32) for k in range(len(parts))]
        return parts

    def core_product(left, right, dot):
        got = swap(dot(left[rows:], right), "tensor", 1)
        return dot(left[:rows], right) + got

    def regroup(columns, back):
        lead = columns.shape[:-1]
        order = (3, heads, HEAD) if back else (heads, 3, HEAD)
        return jnp.swapaxes(columns.reshape(lead + order), -3, -2).reshape(columns.shape)

    qkv_w = [regroup(qkv_weight[l], False) for l in range(LAYERS)]
    qkv_b = [regroup(qkv_bias[l].astype(F32), False)[None] for l in range(LAYERS)]

    share = out_weight.shape[1] // dp
    piece = lax.dynamic_slice_in_dim(out_weight, dp_index * share, share, axis=1)
    near = [out_weight]
    for j in range(1, chips):
        near.append(lax.all_gather(swap(piece, "tensor", 2 * j), "dp", axis=1, tiled=True))
    far = [swap(item, "tensor", 1) for item in near]
    out_all = jnp.concatenate([x for pair in zip(near, far) for x in pair], axis=1)

    x_half = [t.astype(F32) for t in chip_gather(tokens)]
    stored = []
    stat_terms = []
    tick = tokens
    for l in range(LAYERS):
        final = l == LAYERS - 1
        gains = norm_gain[l].astype(F32)
        shifts = norm_shift[l].astype(F32)
        order = list(streams) if l == 0 else list(reversed(streams))
        na, nb, pre, hidden, ffn, qkv, ctx, lse, near = ([None] * chips for _ in range(9))
        up_b = up_bias[l].astype(F32)

        def feed(k):
            u = dot_nn(nb[k], up_weight[l]) + up_b
            pre[k] = u
            hidden[k] = gelu(u).astype(B16)
            ffn[k] = core_product(hidden[k], down_weight[l], dot_nn)

        def attend(k):
            qkv[k], ctx[k], lse[k] = attend_forward(na[k], qkv_w[l], qkv_b[l], tables)
            got = swap(ctx[k][rows:], "tensor", 1)
            near[k] = jnp.concatenate([ctx[k][:rows], got], axis=1)

        for k in order:
            z, _ = standardize(x_half[k])
            na[k] = core_gather((z * gains[0] + shifts[0]).astype(B16))
            nb[k] = core_gather((z * gains[1] + shifts[1]).astype(B16))
        if l == 0:
            for k in order:
                nb[k] = after(nb[k], tick)
                feed(k)
                na[k] = after(na[k], hidden[k])
                attend(k)
                tick = ctx[k]
        else:
            for k in order:
                nb[k] = after(nb[k], tick)
                feed(k)
                tick = hidden[k]
            for k in order:
                na[k] = after(na[k], tick)
                attend(k)
                tick = ctx[k]
        if final:
            ffn = [chip_scatter(ffn)]
        else:
            ffn = chip_reduce(ffn)
        x_next = []
        for k in streams if not final else range(1):
            blocks = [near[k]] + [swap(near[k ^ j], "tensor", 2 * j) for j in range(1, chips)]
            attn = dot_nn(jnp.concatenate(blocks, axis=1), out_all[l]) + out_bias[l].astype(F32)
            ffn_out = ffn[k] + down_bias[l].astype(F32)
            x_next.append(x_half[k] + attn + ffn_out)
            if k == 0:
                stat_terms.append(
                    jnp.stack(
                        [
                            jnp.sum(x_next[0] * x_next[0]),
                            jnp.sum(attn * attn),
                            jnp.sum(ffn_out * ffn_out),
                        ]
                    )
                )
        stored.append((x_half, na, nb, pre, hidden, qkv, ctx, lse))
        if l == 0:
            grad_low_half = chip_gather(after(cotangent, x_next[0]))
        x_half = x_next
    output = x_half[0]

    grad = cotangent.astype(F32)
    big = [None] * LAYERS
    small_all = [None] * LAYERS
    small_dp = [None] * LAYERS
    summed = None
    for l in reversed(range(LAYERS)):
        x_half, na, nb, pre, hidden, qkv, ctx, lse = stored[l]
        gains = norm_gain[l].astype(F32)
        low = grad.astype(B16)
        if l < LAYERS - 1:
            grad_low_half = chip_gather(low)
        g = [core_gather(item) for item in grad_low_half]
        g[0] = after(g[0], tick)
        d_pre, d_qkv, d_z = [None] * chips, [None] * chips, [None] * chips
        down_g = sum(dot_tn(hidden[k], g[k]) for k in streams)
        up_bias_g = jnp.zeros((ff,), F32)
        qkv_bias_g = jnp.zeros((1, 3 * w), F32)
        sums = 0.0
        for k in streams:
            d_pre[k] = (dot_nt(g[k], down_weight[l]) * gelu_slope(pre[k])).astype(B16)
            up_bias_g = up_bias_g + jnp.sum(d_pre[k], axis=0, dtype=F32)
        up_g = sum(dot_tn(nb[k], d_pre[k]) for k in streams)
        first = (down_g.astype(B16), up_g.astype(B16))
        if summed is not None:
            first = lax.optimization_barrier(first + summed[:1])[:2]
        first = lax.psum(first, "dp")
        tick = up_g
        for k in reversed(streams):
            d_ctx = dot_nt(g[k], out_weight[l]).astype(B16)
            d_qkv[k], bias_k = attend_backward(qkv[k], after(d_ctx, tick), lse[k], tables)
            tick = d_qkv[k]
            qkv_bias_g = qkv_bias_g + bias_k
            d_na = core_product(d_qkv[k], qkv_w[l], dot_nt)
            d_nb = core_product(d_pre[k], up_weight[l], dot_nt)
            z, inverse = standardize(x_half[k])
            sums = sums + jnp.stack(
                [
                    jnp.sum(d_na * z, axis=0),
                    jnp.sum(d_nb * z, axis=0),
                    jnp.sum(d_na, axis=0),
                    jnp.sum(d_nb, axis=0),
                ]
            )
            d_z[k] = d_na * gains[0] + d_nb * gains[1]
        total = chip_scatter(d_z)
        slope = total - jnp.mean(total, axis=-1, keepdims=True)
        slope = slope - z * jnp.mean(total * z, axis=-1, keepdims=True)
        bias_g = jnp.sum(low, axis=0, dtype=F32)
        grad = grad + slope * inverse
        out_g = sum(dot_tn(ctx[k], g[k]) for k in streams)
        qkv_g = sum(dot_tn(na[k], d_qkv[k]) for k in streams)
        second = (qkv_g.astype(B16), out_g.astype(B16))
        second = lax.optimization_barrier(second + first[:1])[:2]
        second = lax.psum(second, "dp")
        small_all[l] = jnp.concatenate(
            [sums, bias_g[None], jnp.pad(stat_terms[l], (0, features - 3))[None]], axis=0
        )
        small_dp[l] = jnp.concatenate([up_bias_g, qkv_bias_g[0]])
        big[l] = first + second
        summed = second
    small = jnp.stack(small_all)
    for bit in all_bits(tensor):
        small = small + swap(small, "tensor", bit)
    vector = jnp.stack(small_dp)
    for bit in dp_bits:
        small = small + swap(small, "dp", bit)
        vector = vector + swap(vector, "dp", bit)
    down_all = jnp.stack([item[0] for item in big]).astype(F32)
    up_all = jnp.stack([item[1] for item in big]).astype(F32)
    qkv_all = jnp.stack([regroup(item[2], True) for item in big]).astype(F32)
    out_w_all = jnp.stack([item[3] for item in big]).astype(F32)
    layer_stats = jnp.sqrt(small[:, 5, :3] / (rows * dp * tensor * features))
    bias_all = small[:, 4]
    return (
        output,
        grad,
        qkv_all,
        regroup(vector[:, ff:], True),
        out_w_all,
        bias_all,
        up_all,
        vector[:, :ff],
        down_all,
        bias_all,
        small[:, 0:2],
        small[:, 2:4],
        layer_stats,
    )


MESH = pl.DeviceIdType.MESH
ANY = pl.BlockSpec(memory_space=pl.ANY)
VMEM = pl.BlockSpec(memory_space=pltpu.VMEM)
DMA = pltpu.SemaphoreType.DMA


def partners():
    me = lax.axis_index("tensor")
    return me + 1 - 2 * lax.rem(me, 2), lax.rem(me + 2, 4)


def greet(others):
    barrier = pltpu.get_barrier_semaphore()
    for other in others:
        pl.semaphore_signal(barrier, inc=1, device_id={"tensor": other}, device_id_type=MESH)
    pl.semaphore_wait(barrier, len(others))


def remote(src, dst, sems, index, target):
    return pltpu.make_async_remote_copy(
        src_ref=src,
        dst_ref=dst,
        send_sem=sems[0].at[index],
        recv_sem=sems[1].at[index],
        device_id={"tensor": target},
        device_id_type=MESH,
    )


def block(i, size=QB):
    return pl.ds(pl.multiple_of(i * size, size), size)


def by_kind(rows, heads):
    return jnp.concatenate(
        [
            rows[:, (3 * h + j) * HEAD : (3 * h + j + 1) * HEAD]
            for j in range(3)
            for h in range(heads)
        ],
        axis=1,
    )


def by_head(rows, heads):
    return jnp.concatenate(
        [
            rows[:, (heads * j + h) * HEAD : (heads * j + h + 1) * HEAD]
            for h in range(heads)
            for j in range(3)
        ],
        axis=1,
    )


def causal(s, n):
    tri = lax.broadcasted_iota(jnp.int32, (QB, QB), 0) >= lax.broadcasted_iota(
        jnp.int32, (QB, QB), 1
    )
    last = jnp.where(tri, s[:, n - QB :], NEG)
    return last if n == QB else jnp.concatenate([s[:, : n - QB], last], axis=1)


def forward_layer_kernel(first, final, rows, w, *refs):
    it = iter(refs)
    x_ref, up_ref, upb_ref, down_ref, qkvw_ref, qkvb_ref = (next(it) for _ in range(6))
    out_ref, ob_ref, gain_ref, shift_ref = (next(it) for _ in range(4))
    cos_ref, lo_ref, hi_ref = (next(it) for _ in range(3))
    cot_ref = next(it) if final else None
    na_o, nb_o, u_o, hid_o, qkv_o, ctx_o, lse_o, x_o = (next(it) for _ in range(8))
    far_o = next(it) if first or final else None
    na_s, nb_s, u_s, hid_s, psend, precv, ysend, yrecv = (next(it) for _ in range(8))
    qkv_s, ctx_s, lse_s = (next(it) for _ in range(3))
    far_s = next(it) if first or final else None
    mine_s = next(it)
    send, recv, local, u_sem = (next(it) for _ in range(4))
    sems = (send, recv)

    seq = 2 * rows
    heads = w // HEAD
    blocks = seq // QB
    half_blocks = rows // QB
    shift = lax.rem(lax.axis_index("tensor"), 2) * half_blocks
    core, far = partners()
    greet((core, far))
    outs = []

    def keep(src, dst, index):
        copy = pltpu.make_async_copy(src, dst, local.at[index])
        copy.start()
        outs.append(copy)

    far_copy = None
    if first or final:
        far_copy = remote(x_ref if first else cot_ref, far_s, sems, 0, far)
        far_copy.start()

    def x_rows(k, r):
        if not first:
            return x_ref[block(r + k * half_blocks), :]
        return (far_s if k else x_ref)[block(r), :].astype(F32)

    gathers = {}

    def norms(k):
        @pl.loop(0, half_blocks)
        def _(r):
            z, _ = standardize(x_rows(k, r))
            na_s[k, block(r), :] = (z * gain_ref[0:1, :] + shift_ref[0:1, :]).astype(B16)
            nb_s[k, block(r), :] = (z * gain_ref[1:2, :] + shift_ref[1:2, :]).astype(B16)

        gathers[k] = []
        for at, buf in ((0, nb_s), (1, na_s)):
            copy = remote(
                buf.at[k, pl.ds(0, rows), :],
                buf.at[k, pl.ds(rows, rows), :],
                sems,
                1 + 2 * k + at,
                core,
            )
            copy.start()
            gathers[k].append(copy)

    products = {}
    u_out = []

    def feed(k):
        gathers[k][0].wait()
        keep(nb_s.at[k], nb_o.at[pl.ds(k * seq, seq), :], 2 * k)
        for h in (1, 0):
            for copy in u_out:
                copy.wait()
            u_out.clear()

            @pl.loop(0, half_blocks)
            def _(r):
                at = block(r + h * half_blocks)
                u = dot_nn(nb_s[k, at, :], up_ref[...]) + upb_ref[...]
                u_s[r] = u
                hid_s[k, at, :] = gelu(u).astype(B16)

            for r in range(half_blocks):
                copy = pltpu.make_async_copy(
                    u_s.at[r], u_o.at[pl.ds(k * seq + h * rows + r * QB, QB), :], u_sem.at[r]
                )
                copy.start()
                u_out.append(copy)
        keep(hid_s.at[k], hid_o.at[pl.ds(k * seq, seq), :], 2 * k + 1)

    def join(k):
        @pl.loop(0, half_blocks)
        def _(r):
            at = block(r + half_blocks)
            psend[k, block(r), :] = dot_nn(hid_s[k, at, :], down_ref[...]) + dot_nn(
                ctx_s[k, at, :], out_ref[...]
            )

        product = remote(psend.at[k], precv.at[k], sems, 5 + k, core)
        product.start()
        products[k] = product

        @pl.loop(0, half_blocks)
        def _(r):
            at = block(r)
            mine_s[at, :] = dot_nn(hid_s[k, at, :], down_ref[...]) + dot_nn(
                ctx_s[k, at, :], out_ref[...]
            )

        product.wait_recv()

        @pl.loop(0, half_blocks)
        def _(r):
            at = block(r)
            total = precv[k, at, :] + mine_s[at, :]
            if final and k == 0:
                precv[k, at, :] = total
            else:
                ysend[k, at, :] = total.astype(B16)

        if not (final and k == 0):
            sums[k] = remote(ysend.at[k], yrecv.at[1 - k], sems, 7 + k, far)
            sums[k].start()

    sums = {}

    def attend(k):
        gathers[k][1].wait()
        keep(na_s.at[k], na_o.at[pl.ds(k * seq, seq), :], 4 + 2 * k)
        swapped = lambda i: block(lax.rem(i + shift, blocks))

        @pl.loop(0, blocks)
        def _(r):
            acc = dot_nn(na_s[k, swapped(r), :], qkvw_ref[...]) + qkvb_ref[...]
            acc = by_kind(acc, heads)
            turned = rope(
                acc[:, : 2 * w], cos_ref[block(r), :], lo_ref[block(r), :], hi_ref[block(r), :], 1
            )
            qkv_s[k, block(r), : 2 * w] = turned.astype(B16)
            qkv_s[k, block(r), 2 * w :] = acc[:, 2 * w :].astype(B16)
            ctx_s[k, block(r), :] = jnp.zeros((QB, w), B16)
            lse_s[k, block(r), :] = jnp.zeros((QB, 128), F32)

        @pl.loop(0, heads)
        def _(h):
            mine = (lax.broadcasted_iota(jnp.int32, (1, w), 1) // HEAD) == h
            scale = jnp.where(mine, SCALE, 0.0).astype(B16)
            lane = lax.broadcasted_iota(jnp.int32, (QB, 128), 1)
            for i in range(blocks):
                n = (i + 1) * QB
                q = qkv_s[k, i * QB : n, :w] * scale
                s = causal(dot_nt(q, qkv_s[k, :n, w : 2 * w]), n)
                top = jnp.max(s, axis=1, keepdims=True)
                p = jnp.exp(s - top)
                total = jnp.sum(p, axis=1, keepdims=True)
                low = (p * (1.0 / total)).astype(B16)
                c = dot_nn(low, qkv_s[k, :n, 2 * w :])
                old = ctx_s[k, swapped(i), :]
                ctx_s[k, swapped(i), :] = jnp.where(mine, c, old.astype(F32)).astype(B16)
                lse_s[k, i * QB : n, :] = jnp.where(
                    lane == h, top + jnp.log(total), lse_s[k, i * QB : n, :]
                )

        keep(qkv_s.at[k], qkv_o.at[pl.ds(k * seq, seq), :], 5 + 2 * k)
        keep(ctx_s.at[k], ctx_o.at[pl.ds(k * seq, seq), :], 8 + 2 * k)
        keep(lse_s.at[k], lse_o.at[pl.ds(k * seq, seq), :], 9 + 2 * k)

    def finish(k):
        sums[1 - k].wait_recv()

        @pl.loop(0, half_blocks)
        def _(r):
            at = block(r)
            mine = precv[k, at, :] if final else ysend[k, at, :].astype(F32)
            both = mine + yrecv[k, at, :].astype(F32)
            precv[k, at, :] = x_rows(k, r) + (both + ob_ref[...])

        keep(precv.at[k], x_o.at[pl.ds(k * rows, rows), :], 12 + k)

    if first:
        norms(0)
        feed(0)
        attend(0)
        join(0)
        far_copy.wait_recv()
        norms(1)
        feed(1)
        attend(1)
        join(1)
    else:
        norms(1)
        norms(0)
        feed(1)
        attend(1)
        join(1)
        feed(0)
        attend(0)
        join(0)
    if final and not first:
        far_copy.wait_recv()
    if first or final:
        keep(far_s, far_o, 14)
    finish(0)
    if not final:
        finish(1)

    if first or final:
        far_copy.wait_send()
    for copy in u_out + outs:
        copy.wait()
    for copy in products.values():
        copy.wait_send()
    for copy in sums.values():
        copy.wait_send()


def forward_layer(l, layers, x, up, upb, down, qkvw, qkvb, out, ob, gains, shifts, tables, cot):
    first, final = l == 0, l == layers - 1
    features = x.shape[1]
    rows = x.shape[0] if first else x.shape[0] // 2
    seq = 2 * rows
    w = qkvw.shape[1] // 3
    ff = up.shape[1]
    shape = jax.ShapeDtypeStruct
    out_shape = [
        shape((2 * seq, features), B16),
        shape((2 * seq, features), B16),
        shape((2 * seq, ff), F32),
        shape((2 * seq, ff), B16),
        shape((2 * seq, 3 * w), B16),
        shape((2 * seq, w), B16),
        shape((2 * seq, 128), F32),
        shape((rows if final else 2 * rows, features), F32),
    ]
    if first or final:
        out_shape.append(shape((rows, features), B16))
    args = [x, up, upb, down, qkvw, qkvb, out, ob, gains, shifts, *tables]
    if final:
        args.append(cot)
    scratch = [
        pltpu.VMEM((2, seq, features), B16),
        pltpu.VMEM((2, seq, features), B16),
        pltpu.VMEM((rows // QB, QB, ff), F32),
        pltpu.VMEM((2, seq, ff), B16),
        pltpu.VMEM((2, rows, features), F32),
        pltpu.VMEM((2, rows, features), F32),
        pltpu.VMEM((2, rows, features), B16),
        pltpu.VMEM((2, rows, features), B16),
        pltpu.VMEM((2, seq, 3 * w), B16),
        pltpu.VMEM((2, seq, w), B16),
        pltpu.VMEM((2, seq, 128), F32),
    ]
    if first or final:
        scratch.append(pltpu.VMEM((rows, features), B16))
    scratch.append(pltpu.VMEM((rows, features), F32))
    scratch += [DMA((9,)), DMA((9,)), DMA((15,)), DMA((rows // QB,))]
    return pl.pallas_call(
        functools.partial(forward_layer_kernel, first, final, rows, w),
        in_specs=[VMEM] * len(args),
        out_specs=[ANY] * len(out_shape),
        out_shape=out_shape,
        scratch_shapes=scratch,
        compiler_params=pltpu.CompilerParams(
            vmem_limit_bytes=63 * MIB, collective_id=l, has_side_effects=True
        ),
        cost_estimate=pl.CostEstimate(
            flops=2 * 2 * seq * features * (3 * w + 2 * ff + w) * 2,
            bytes_accessed=40 * MIB,
            transcendentals=4 * seq * seq * w // HEAD,
        ),
        name="forward_layer",
    )(*args)


def backward_layer_kernel(first, final, rows, w, *refs):
    it = iter(refs)
    grad_ref, u_ref, down_ref, up_ref, ow_ref, qkvw_ref = (next(it) for _ in range(6))
    qkv_ref, lse_ref, ctx_ref, outall_ref, ob_ref, xn_ref, x_ref = (next(it) for _ in range(7))
    far_ref = next(it) if first else None
    farg_ref = next(it) if final else None
    gain_ref, cos_ref, lo_ref, hi_ref = (next(it) for _ in range(4))
    g_o, dpre_o, dqkv_o = (next(it) for _ in range(3))
    dx_ref, small_ref = (next(it) for _ in range(2))
    g_s, dpre_s, dqkv_s, dq_s, dk_s, dv_s, dctx_s = (next(it) for _ in range(7))
    u_s, bsend, brecv, asend, arecv, zown, ysend, yrecv = (next(it) for _ in range(8))
    cfull, got_s = (next(it) for _ in range(2))
    send, recv, local, u_sem = (next(it) for _ in range(4))
    sems = (send, recv)

    seq = 2 * rows
    ff = up_ref.shape[1]
    heads = w // HEAD
    blocks = seq // QB
    half_blocks = rows // QB
    shift = lax.rem(lax.axis_index("tensor"), 2) * half_blocks
    swapped = lambda i: block(lax.rem(i + shift, blocks))
    core, far = partners()
    diag = lax.rem(core + 2, 4)
    greet((core, far, diag))
    outs = []

    def keep(src, dst, index):
        copy = pltpu.make_async_copy(src, dst, local.at[index])
        copy.start()
        outs.append(copy)

    def load_u(k, i):
        return pltpu.make_async_copy(
            u_ref.at[pl.ds(k * seq + i * QB, QB), :], u_s.at[i % 2], u_sem.at[i % 2]
        )

    small_ref[...] = jnp.zeros_like(small_ref)
    load_u(0, 0).start()
    load_u(0, 1).start()

    @pl.loop(0, half_blocks)
    def _(r):
        low = grad_ref[block(r), :].astype(B16)
        g_s[0, block(r), :] = low
        small_ref[4:5, :] += jnp.sum(low.astype(F32), axis=0, keepdims=True)

    own_half = lambda buf, k: buf.at[k, pl.ds(0, rows), :]
    other_half = lambda buf, k: buf.at[k, pl.ds(rows, rows), :]
    if final:
        g_s[1, :rows, :] = farg_ref[...]
    else:
        across = remote(own_half(g_s, 0), own_half(g_s, 1), sems, 0, far)
        across.start()
    near0 = remote(own_half(g_s, 0), other_half(g_s, 0), sems, 1, core)
    near0.start()
    cfull[:, :w] = ctx_ref[:rows, :]
    contexts = [
        remote(ctx_ref.at[pl.ds(rows, rows), :], cfull.at[:, pl.ds(w, w)], sems, 8, core),
        remote(ctx_ref.at[pl.ds(seq, rows), :], cfull.at[:, pl.ds(2 * w, w)], sems, 9, far),
        remote(ctx_ref.at[pl.ds(seq + rows, rows), :], cfull.at[:, pl.ds(3 * w, w)], sems, 10, diag),
    ]
    for copy in contexts:
        copy.start()

    swaps = {}

    def feed(k):
        for i in range(blocks):
            load_u(k, i).wait()
            at = pl.ds(i * QB, QB)
            d_hidden = dot_nt(g_s[k, at, :], down_ref[...])
            d_pre = (d_hidden * gelu_slope(u_s[i % 2])).astype(B16)
            dpre_s[k, at, :] = d_pre
            small_ref[8:9, :ff] += jnp.sum(d_pre.astype(F32), axis=0, keepdims=True)
            if i + 2 < blocks:
                load_u(k, i + 2).start()
            elif k == 0:
                load_u(1, i + 2 - blocks).start()

        @pl.loop(0, half_blocks)
        def _(r):
            bsend[k, block(r), :] = dot_nt(
                dpre_s[k, block(r + half_blocks), :], up_ref[...]
            ).astype(B16)

        swaps[k] = [remote(bsend.at[k], brecv.at[k], sems, 3 + 2 * k, core)]
        swaps[k][0].start()
        keep(dpre_s.at[k], dpre_o.at[pl.ds(k * seq, seq), :], k)

    def attend(k):
        @pl.loop(0, blocks)
        def _(r):
            dctx_s[block(r), :] = dot_nt(g_s[k, swapped(r), :], ow_ref[...]).astype(B16)
            dq_s[block(r), :] = jnp.zeros((QB, w), F32)
            dk_s[block(r), :] = jnp.zeros((QB, w), F32)
            dv_s[block(r), :] = jnp.zeros((QB, w), F32)

        base = k * seq

        @pl.loop(0, heads)
        def _(h):
            mine = (lax.broadcasted_iota(jnp.int32, (1, w), 1) // HEAD) == h
            scale = jnp.where(mine, SCALE, 0.0).astype(B16)
            only = jnp.where(mine, 1.0, 0.0).astype(B16)
            lane = lax.broadcasted_iota(jnp.int32, (QB, 128), 1)
            for i in range(blocks):
                n = (i + 1) * QB
                q = qkv_ref[base + i * QB : base + n, :w] * scale
                d = dctx_s[i * QB : n, :] * only
                s = causal(dot_nt(q, qkv_ref[base : base + n, w : 2 * w]), n)
                lse = jnp.sum(
                    jnp.where(lane == h, lse_ref[base + i * QB : base + n, :], 0.0),
                    axis=1,
                    keepdims=True,
                )
                p = jnp.exp(s - lse)
                dp = dot_nt(d, qkv_ref[base : base + n, 2 * w :])
                inner = jnp.sum(p * dp, axis=1, keepdims=True)
                ds = (p * (dp - inner)).astype(B16)
                dq_s[i * QB : n, :] += dot_nn(ds, qkv_ref[base : base + n, w : 2 * w] * scale)
                dk_s[:n, :] += dot_tn(ds, q)
                dv_s[:n, :] += dot_tn(p.astype(B16), d)

        @pl.loop(0, blocks)
        def _(r):
            at = block(r)
            qk = jnp.concatenate([dq_s[at, :], dk_s[at, :]], axis=1)
            qk = rope(qk, cos_ref[at, :], lo_ref[at, :], hi_ref[at, :], -1)
            low = by_head(jnp.concatenate([qk, dv_s[at, :]], axis=1), heads).astype(B16)
            dqkv_s[k, swapped(r), :] = low
            small_ref[9:10, : 3 * w] += jnp.sum(low.astype(F32), axis=0, keepdims=True)

        @pl.loop(0, half_blocks)
        def _(r):
            asend[k, block(r), :] = dot_nt(
                dqkv_s[k, block(r + half_blocks), :], qkvw_ref[...]
            ).astype(B16)

        swaps[k].append(remote(asend.at[k], arecv.at[k], sems, 4 + 2 * k, core))
        swaps[k][1].start()
        keep(dqkv_s.at[k], dqkv_o.at[pl.ds(base, seq), :], 2 + k)

    def x_rows(k, r):
        if not first:
            return x_ref[block(r + k * half_blocks), :]
        return (far_ref if k else x_ref)[block(r), :].astype(F32)

    def fold(k):
        for copy in swaps[k]:
            copy.wait()

        @pl.loop(0, half_blocks)
        def _(r):
            at = block(r)
            d_na = dot_nt(dqkv_s[k, at, :], qkvw_ref[...]) + arecv[k, at, :].astype(F32)
            d_nb = dot_nt(dpre_s[k, at, :], up_ref[...]) + brecv[k, at, :].astype(F32)
            z, _ = standardize(x_rows(k, r))
            small_ref[0:1, :] += jnp.sum(d_na * z, axis=0, keepdims=True)
            small_ref[1:2, :] += jnp.sum(d_nb * z, axis=0, keepdims=True)
            small_ref[2:3, :] += jnp.sum(d_na, axis=0, keepdims=True)
            small_ref[3:4, :] += jnp.sum(d_nb, axis=0, keepdims=True)
            d_z = d_na * gain_ref[0:1, :] + d_nb * gain_ref[1:2, :]
            if k == 0:
                zown[at, :] = d_z
            else:
                ysend[at, :] = d_z.astype(B16)

    near0.wait()
    keep(g_s.at[0], g_o.at[pl.ds(0, seq), :], 4)
    feed(0)
    if not final:
        across.wait()
    near1 = remote(own_half(g_s, 1), other_half(g_s, 1), sems, 2, core)
    near1.start()
    near1.wait()
    keep(g_s.at[1], g_o.at[pl.ds(seq, seq), :], 5)
    feed(1)
    attend(1)
    fold(1)
    back = remote(ysend, yrecv, sems, 7, far)
    back.start()
    attend(0)
    fold(0)
    for copy in contexts:
        copy.wait()

    @pl.loop(0, half_blocks)
    def _(r):
        at = block(r)
        attn = dot_nn(cfull[at, :], outall_ref[...]) + ob_ref[...]
        x_next = xn_ref[at, :]
        feed_out = x_next - x_rows(0, r) - attn
        small_ref[5:6, :] += jnp.sum(x_next * x_next, axis=0, keepdims=True)
        small_ref[6:7, :] += jnp.sum(attn * attn, axis=0, keepdims=True)
        small_ref[7:8, :] += jnp.sum(feed_out * feed_out, axis=0, keepdims=True)

    for at, other in ((0, core), (1, far)):
        copy = remote(small_ref.at[pl.ds(0, 8), :], got_s.at[at], sems, 11 + at, other)
        copy.start()
        copy.wait()
        small_ref[0:8, :] += got_s[at]
    back.wait()

    @pl.loop(0, half_blocks)
    def _(r):
        at = block(r)
        total = zown[at, :] + yrecv[at, :].astype(F32)
        z, inverse = standardize(x_rows(0, r))
        slope = total - jnp.mean(total, axis=-1, keepdims=True)
        slope = slope - z * jnp.mean(total * z, axis=-1, keepdims=True)
        dx_ref[at, :] = grad_ref[at, :].astype(F32) + slope * inverse

    for copy in outs:
        copy.wait()


def backward_layer(
    l, layers, grad, u, down, up, out_w, qkvw, qkv, lse, ctx, out_all, ob, xn, x, far_x, far_g, gains, tables
):
    first, final = l == 0, l == layers - 1
    rows, features = grad.shape
    seq = 2 * rows
    w = qkvw.shape[1] // 3
    ff = up.shape[1]
    shape = jax.ShapeDtypeStruct
    args = [grad, u, down, up, out_w, qkvw, qkv, lse, ctx, out_all, ob, xn, x]
    in_specs = [VMEM, ANY] + [VMEM] * 11
    if first:
        args.append(far_x)
        in_specs.append(VMEM)
    if final:
        args.append(far_g)
        in_specs.append(VMEM)
    args += [gains, *tables]
    in_specs += [VMEM] * 4
    out_shape = [
        shape((2 * seq, features), B16),
        shape((2 * seq, ff), B16),
        shape((2 * seq, 3 * w), B16),
        shape((rows, features), F32),
        shape((16, features), F32),
    ]
    half = lambda dtype: pltpu.VMEM((2, rows, features), dtype)
    scratch = [
        pltpu.VMEM((2, seq, features), B16),
        pltpu.VMEM((2, seq, ff), B16),
        pltpu.VMEM((2, seq, 3 * w), B16),
        pltpu.VMEM((seq, w), F32),
        pltpu.VMEM((seq, w), F32),
        pltpu.VMEM((seq, w), F32),
        pltpu.VMEM((seq, w), B16),
        pltpu.VMEM((2, QB, ff), F32),
        half(B16),
        half(B16),
        half(B16),
        half(B16),
        pltpu.VMEM((rows, features), F32),
        pltpu.VMEM((rows, features), B16),
        pltpu.VMEM((rows, features), B16),
        pltpu.VMEM((rows, 4 * w), B16),
        pltpu.VMEM((2, 8, features), F32),
        DMA((13,)),
        DMA((13,)),
        DMA((6,)),
        DMA((2,)),
    ]
    return pl.pallas_call(
        functools.partial(backward_layer_kernel, first, final, rows, w),
        in_specs=in_specs,
        out_specs=[ANY] * 3 + [VMEM] * 2,
        out_shape=out_shape,
        scratch_shapes=scratch,
        compiler_params=pltpu.CompilerParams(
            vmem_limit_bytes=63 * MIB, collective_id=layers + l, has_side_effects=True
        ),
        cost_estimate=pl.CostEstimate(
            flops=2 * 2 * seq * features * (3 * w + 2 * ff + w) * 2,
            bytes_accessed=40 * MIB,
            transcendentals=4 * seq * seq * w // HEAD,
        ),
        name="backward_layer",
    )(*args)


def ring_place(index, size):
    side = lax.rem(index, 2)
    level = index // 2
    return level * (1 - side) + (size - 1 - level) * side


def ring_device(place, size):
    side = place // (size // 2)
    return (1 - side) * 2 * place + side * (2 * (size - 1 - place) + 1)


def ring_sum_kernel(n, shapes, *refs):
    count = len(shapes)
    it = iter(refs)
    ins = [next(it) for _ in range(count)]
    small_in = next(it)
    outs = [next(it) for _ in range(count)]
    small_out = next(it)
    slots = [next(it) for _ in range(count)]
    done = [next(it) for _ in range(count)]
    small_s = next(it)
    send, recv, small_send, small_recv = (next(it) for _ in range(4))

    place = ring_place(lax.axis_index("dp"), n)
    ahead = ring_device(lax.rem(place + 1, n), n)
    behind = ring_device(lax.rem(place + n - 1, n), n)
    barrier = pltpu.get_barrier_semaphore()
    for other in (ahead, behind):
        pl.semaphore_signal(barrier, inc=1, device_id={"dp": other}, device_id_type=MESH)
    pl.semaphore_wait(barrier, 2)

    def rows_of(a, way, step):
        size = shapes[a][0] // (2 * n)
        chunk = lax.rem(place + n - step, n) if way == 0 else lax.rem(place + step, n)
        return pl.ds(pl.multiple_of((chunk * 2 + way) * size, size), size)

    def copy(src, dst, a, way, step):
        return pltpu.make_async_remote_copy(
            src_ref=src,
            dst_ref=dst,
            send_sem=send.at[a, way, step],
            recv_sem=recv.at[a, way, step],
            device_id={"dp": (ahead, behind)[way]},
            device_id_type=MESH,
        )

    def small_copy(step):
        at = lax.rem(place + n - step, n)
        return pltpu.make_async_remote_copy(
            src_ref=small_s.at[at],
            dst_ref=small_s.at[at],
            send_sem=small_send.at[step],
            recv_sem=small_recv.at[step],
            device_id={"dp": ahead},
            device_id_type=MESH,
        )

    small_s[place] = small_in[...]
    flying = []

    def launch(item):
        item.start()
        flying.append(item)
        return item

    last = n - 2
    moving = {}
    for a in range(count):
        for way in (0, 1):
            moving[a, way] = launch(
                copy(ins[a].at[rows_of(a, way, 0), :], slots[a].at[way, 0], a, way, 0)
            )
    small = launch(small_copy(0))
    for step in range(n - 1):
        for a in range(count):
            for way in (0, 1):
                moving[a, way].wait_recv()
                mine = ins[a][rows_of(a, way, step + 1), :].astype(F32)
                total = slots[a][way, step].astype(F32) + mine
                low = total.astype(B16)
                slots[a][way, step] = low
                if step < last:
                    target = slots[a].at[way, step + 1]
                else:
                    target = done[a].at[rows_of(a, way, step + 1), :]
                    outs[a][rows_of(a, way, step + 1), :] = low.astype(F32)
                moving[a, way] = launch(
                    copy(slots[a].at[way, step], target, a, way, step + 1)
                )
        small.wait_recv()
        if step < last:
            small = launch(small_copy(step + 1))
    for step in range(n - 1):
        for a in range(count):
            for way in (0, 1):
                at = rows_of(a, way, step)
                moving[a, way].wait_recv()
                if step < last:
                    moving[a, way] = launch(
                        copy(done[a].at[at, :], done[a].at[at, :], a, way, n + step)
                    )
                outs[a][at, :] = done[a][at, :].astype(F32)
    total = small_s[0]
    for i in range(1, n):
        total = total + small_s[i]
    small_out[...] = total
    for item in flying:
        item.wait_send()


def ring_sum(arrays, small, collective_id):
    n = lax.axis_size("dp")
    shapes = [item.shape for item in arrays]
    shape = jax.ShapeDtypeStruct
    size = sum(a * b for a, b in shapes)
    steps = 2 * n - 2
    return pl.pallas_call(
        functools.partial(ring_sum_kernel, n, shapes),
        in_specs=[VMEM] * (len(arrays) + 1),
        out_specs=[VMEM] * (len(arrays) + 1),
        out_shape=[shape(item, F32) for item in shapes] + [shape(small.shape, F32)],
        scratch_shapes=[pltpu.VMEM((2, n - 1, a // (2 * n), b), B16) for a, b in shapes]
        + [pltpu.VMEM(item, B16) for item in shapes]
        + [pltpu.VMEM((n,) + small.shape, F32)]
        + [DMA((len(arrays), 2, steps))] * 2
        + [DMA((n - 1,))] * 2,
        compiler_params=pltpu.CompilerParams(
            vmem_limit_bytes=56 * MIB, collective_id=collective_id, has_side_effects=True
        ),
        cost_estimate=pl.CostEstimate(
            flops=size, bytes_accessed=400 * MIB, transcendentals=0
        ),
        name="ring_sum",
    )(*arrays, small)


def on_group(
    tokens,
    cotangent,
    qkv_weight,
    qkv_bias,
    out_weight,
    out_bias,
    up_weight,
    up_bias,
    down_weight,
    down_bias,
    norm_gain,
    norm_shift,
):
    rows, features = tokens.shape
    tensor = lax.axis_size("tensor")
    dp = lax.axis_size("dp")
    dp_index = lax.axis_index("dp")
    w = qkv_weight.shape[2] // 3
    ff = up_weight.shape[2]
    tables = rope_tables(SEQ_LEN, 128)

    wide = lambda v: v.astype(F32)

    share = out_weight.shape[1] // dp
    piece = lax.dynamic_slice_in_dim(out_weight, dp_index * share, share, axis=1)
    near = [out_weight, lax.all_gather(swap(piece, "tensor", 2), "dp", axis=1, tiled=True)]
    far = [swap(item, "tensor", 1) for item in near]
    out_all = jnp.concatenate([near[0], far[0], near[1], far[1]], axis=1)

    x = tokens
    stored = []
    far_x = None
    bias_sum = wide(out_bias) + wide(down_bias)
    for l in range(LAYERS):
        got = forward_layer(
            l,
            LAYERS,
            x,
            up_weight[l],
            wide(up_bias[l])[None],
            down_weight[l],
            qkv_weight[l],
            wide(qkv_bias[l])[None],
            out_weight[l],
            bias_sum[l][None],
            wide(norm_gain[l]),
            wide(norm_shift[l]),
            tables,
            cotangent,
        )
        na, nb, u, hidden, qkv, ctx, lse, x_next = got[:8]
        if l == 0:
            far_x = got[8]
        if l == LAYERS - 1:
            far_g = got[8]
        stored.append((x, na, nb, u, hidden, qkv, ctx, lse, x_next))
        x = x_next
    output = x

    grad = cotangent
    big = [None] * LAYERS
    small = [None] * LAYERS
    for l in reversed(range(LAYERS)):
        x, na, nb, u, hidden, qkv, ctx, lse, x_next = stored[l]
        g, d_pre, d_qkv, grad, small[l] = backward_layer(
            l,
            LAYERS,
            grad,
            u,
            down_weight[l],
            up_weight[l],
            out_weight[l],
            qkv_weight[l],
            qkv,
            lse,
            ctx,
            out_all[l],
            wide(out_bias[l])[None],
            x_next,
            x,
            far_x,
            far_g,
            wide(norm_gain[l]),
            tables,
        )
        grads = (dot_tn(hidden, g), dot_tn(nb, d_pre), dot_tn(na, d_qkv), dot_tn(ctx, g))
        grads = tuple(item.astype(B16) for item in grads)
        if l > 0:
            big[l] = [item.astype(F32) for item in lax.psum(grads, "dp")]
        else:
            *big[l], small = ring_sum(grads, jnp.concatenate(small), 2 * LAYERS)
    small = small.reshape(LAYERS, 16, features)
    down_all, up_all, qkv_all, out_w_all = (
        jnp.stack([item[i] for item in big]) for i in range(4)
    )
    layer_stats = jnp.sqrt(jnp.sum(small[:, 5:8], axis=2) / (rows * dp * tensor * features))
    bias_all = small[:, 4]
    return (
        output,
        grad,
        qkv_all,
        small[:, 9, : 3 * w],
        out_w_all,
        bias_all,
        up_all,
        small[:, 8, :ff],
        down_all,
        bias_all,
        small[:, 0:2],
        small[:, 2:4],
        layer_stats,
    )


def solution(mesh):
    in_specs = (
        P(("dp", "tensor"), None),
        P(("dp", "tensor"), None),
        P(None, None, "tensor"),
        P(None, "tensor"),
        P(None, "tensor", None),
        P(),
        P(None, None, "tensor"),
        P(None, "tensor"),
        P(None, "tensor", None),
        P(),
        P(),
        P(),
    )
    out_specs = (
        P(("dp", "tensor"), None),
        P(("dp", "tensor"), None),
        P(None, None, "tensor"),
        P(None, "tensor"),
        P(None, "tensor", None),
        P(),
        P(None, None, "tensor"),
        P(None, "tensor"),
        P(None, "tensor", None),
        P(),
        P(),
        P(),
        P(),
    )
    small = mesh.shape["tensor"] == 4 and mesh.shape["dp"] == 8
    return jax.shard_map(
        on_group if small else on_device,
        mesh=mesh, in_specs=in_specs, out_specs=out_specs, check_vma=False
    )
```

time: 2110 us -> 697 us (0.33)
  waiting for transfers between devices: 1210 us -> 0.06 us
  Pallas kernels: 0 us -> 555 us
  local copies, waits for them, and re-layouts: 357 us -> 40.8 us
  matrix products: 299 us -> 45.1 us
  other arithmetic: 120 us -> 27 us
  blocking collectives: 84 us -> 0 us
    psum x1, waiting for transfers between devices: 700 us -> 0.01 us  [on_group(): big[l] = [item.astype(F32) for item in lax.psum(grads, 'dp')]]
    pallas_call x0 -> x5, Pallas kernels: none -> 555 us  [the longest x1 224 us: ring_sum(): pl.pallas_call(functools.partial(ring_sum_kernel, n, shapes), in_specs=[V...]
    reduce_scatter x4 -> x0, waiting for transfers between devices: 379 us -> none  [the longest x2 249 us: on_device(): lax.psum_scatter(jnp.concatenate([jnp.dot(context_part, out_local, prefer...]
    dot_general x80 -> x8, matrix products: 299 us -> 45.1 us  [dot_tn(): lax.dot_general(left, right, (((0,), (0,)), ((), ())), preferred_element_...]
    dynamic_update_slice x24 -> x0, local copies, waits for them, and re-layouts: 232 us -> none  [on_device(): lax.map(lambda parts: attend_backward(parts[0], parts[1], parts[2], parts...]
    all_gather x6 -> x1, waiting for transfers between devices: 126 us -> 0.02 us  [on_group(): lax.all_gather(swap(piece, 'tensor', 2), 'dp', axis=1, tiled=True)]
    psum x2 -> x0, blocking collectives: 84 us -> none  [the longest x1 45.9 us: on_device(): lax.psum((jnp.stack(bias_list), jnp.stack(gain_list), jnp.stack(shift_lis...]
    unnamed x248 -> x63, local copies, waits for them, and re-layouts: 61.2 us -> 12.6 us
  transfers between devices with their start and end apart: 11 -> 5, of which waited for: 9 -> 0; matrix products, arithmetic and copies ran while one was open for 19% -> 9% of each run, Pallas kernels for 0% -> 69%
where the time goes in v1:
time: 697 us; the launch traced here: 686 us
  Pallas kernels  555 us (80%)
  matrix products  45.1 us (6%)
  local copies, waits for them, and re-layouts  40.8 us (6%)
  other arithmetic  27 us (4%)
  between operations  14.5 us (2%)
    pallas_call x1, Pallas kernels, ring_sum(): pl.pallas_call(functools.partial(ring_sum_kernel, n, shapes), in_specs=[V...  224 us
    pallas_call x2, Pallas kernels, backward_layer(): pl.pallas_call(functools.partial(backward_layer_kernel, first, final, row...  183 us
    pallas_call x2, Pallas kernels, forward_layer(): pl.pallas_call(functools.partial(forward_layer_kernel, first, final, rows...  148 us
    dot_general x8, matrix products, dot_tn(): lax.dot_general(left, right, (((0,), (0,)), ((), ())), preferred_element_...  45.1 us
    another operation x8, other arithmetic, on_group(): jnp.stack([item[i] for item in big])  16.9 us
  transfers between devices with their start and end apart: 5, of which 0 were waited for; matrix products, arithmetic and copies ran while one was open for 9% of the time, Pallas kernels for 69%

profile of v1, /device:TPU:0, one launch (start us, length us, event | category | flops | bytes accessed | tf_op | source)
XLA Modules:
  0.0 686.1 jit_solution(18350424593620357037)
XLA Ops:
  7.7 1.6 constant_dynamic-slice_fusion
  9.3 2.5 collective-permute-start.1
  11.9 2.4 slice_bitcast_fusion.8
  21.6 2.1 copy.27.refs_12_.refs_17_
  23.7 1.8 tile.14
  25.5 2.1 copy.26.refs_11_.refs_16_
  28.4 2.1 copy.25.refs_10_.refs_15_
  30.5 1.9 slice_bitcast_fusion.6
  32.4 1.4 copy-done
  33.8 4.9 slice_bitcast_fusion.2
  40.0 88.1 %forward_layer.2 = (bf16[2048,1024]{1,0:T(8,128)(2,1)}, bf16[2048,1024]{1,0:T(8,128)(2,1)}, f32[2048,1024]{1,0:T(8,128)}, bf16[2048,1024]{1,0:T(8,128)(2,1)}, bf...) custom-call(bf16[512,1024]{1,0:T(8,128)(2,1)} %refs_12_.1, ...), custom_call_target="tpu_custom_call" | custom-call | flops 25769803776 | bytes 41943040 | tf_op jit(solution)/shard_map/forward_layer/pallas_call | solution.py:836
  128.3 60.1 %forward_layer.3 = (bf16[2048,1024]{1,0:T(8,128)(2,1)}, bf16[2048,1024]{1,0:T(8,128)(2,1)}, f32[2048,1024]{1,0:T(8,128)}, bf16[2048,1024]{1,0:T(8,128)(2,1)}, bf...) custom-call(f32[1024,1024]{1,0:T(8,128)} %get-tuple-element.46.refs_, ...), custom_call_target="tpu_custom_call" | custom-call | flops 25769803776 | bytes 41943040 | tf_op jit(solution)/shard_map/forward_layer/pallas_call | solution.py:836
  193.2 2.4 slice_bitcast_fusion
  195.6 84.6 %backward_layer.2 = (bf16[2048,1024]{1,0:T(8,128)(2,1)}, bf16[2048,1024]{1,0:T(8,128)(2,1)}, bf16[2048,768]{1,0:T(8,128)(2,1)}, f32[512,1024]{1,0:T(8,128)}, f32[16,1024]{1,0:T(8,128)}) custom-call(bf16[512,1024]{1,0:T(8,128)(2,1)} %refs_0_.3, f32[2048,1024]{1,0:T(8,128)} %get-tuple-element.48.refs_1_, bf16[1024,1024]{1,0:T(8,128)(2,1)} %get-tuple-element.85.refs_3_.refs_2_, ...), custom_call_target="tpu_custom_call" | custom-call | flops 25769803776 | bytes 41943040 | tf_op jit(solution)/shard_map/backward_layer/pallas_call | solution.py:1121
  280.2 4.7 fusion.1
  285.0 8.1 %convert_bitcast_fusion = bf16[1,1024,1024]{2,1,0:T(8,128)(2,1)} fusion(bf16[2048,1024]{1,0:T(8,128)(2,1)} %get-tuple-element.78, bf16[2048,1024]{1,0:T(8,128)(2,1)S(1)} %copy-done.17), kind=kOutput, calls=%fused_computation.6 | convolution fusion | flops 4296015872 | bytes 10485760 | tf_op jit(solution)/shard_map/dot_general | solution.py:34
  293.1 5.7 convert_bitcast_fusion.1
  298.8 4.8 fusion
  303.7 98.6 %backward_layer.3 = (bf16[2048,1024]{1,0:T(8,128)(2,1)}, bf16[2048,1024]{1,0:T(8,128)(2,1)}, bf16[2048,768]{1,0:T(8,128)(2,1)}, f32[512,1024]{1,0:T(8,128)}, f32[16,1024]{1,0:T(8,128)}) custom-call(f32[512,1024]{1,0:T(8,128)} %get-tuple-element.53.refs_0_, f32[2048,1024]{1,0:T(8,128)} %get-tuple-element.54.refs_1_, ...), custom_call_target="tpu_custom_call" | custom-call | flops 25769803776 | bytes 41943040 | tf_op jit(solution)/shard_map/backward_layer/pallas_call | solution.py:1121
  402.3 1.7 pad_maximum_fusion.4.refs_4_
  404.0 5.3 convolution_convert_fusion.5.refs_3_
  409.3 4.7 convolution_convert_fusion.3.refs_2_
  414.0 5.8 convolution_convert_fusion.1.refs_0_
  419.8 5.9 convolution_convert_fusion.refs_1_
  425.7 224.0 %ring_sum.1 = (f32[1024,1024]{1,0:T(8,128)}, f32[1024,1024]{1,0:T(8,128)}, f32[1024,768]{1,0:T(8,128)}, f32[256,1024]{1,0:T(8,128)}, f32[32,1024]{1,0:T(8,128)}) custom-call(bf16[1024,1024]{1,0:T(8,128)(2,1)} %convolution_convert_fusion.1.refs_0_, bf16[1024,1024]{1,0:T(8,128)(2,1)} %convolution_convert_fusion.refs_1_, ...), custom_call_target="tpu_custom_call" | custom-call | flops 3145728 | bytes 419430400 | tf_op jit(solution)/shard_map/ring_sum/pallas_call | solution.py:1255
  654.1 1.5 fusion.3
  657.0 1.6 stack.50
  661.3 3.1 pad_maximum_fusion.2
  664.4 1.5 pad_maximum_fusion.3
  665.8 1.5 copy-done.2
  667.3 4.2 pad_maximum_fusion
  671.6 4.3 pad_maximum_fusion.1
  (98 shorter events, 26.4 us)
Async XLA Ops:
  7.2 121.0 %all-gather.2.cloned.1.call-start = ((), (), s32[]{:S(2)}) async-start(), calls=%async_computation | async-start | bytes 1179648 | tf_op jit(solution)/shard_map/all_gather | solution.py:1301
  7.2 183.3 %collective-permute-start = (bf16[2,256,1024]{2,1,0:T(8,128)(2,1)}, bf16[2,256,1024]{2,1,0:T(8,128)(2,1)}, u32[]{:S(2)}, u32[]{:S(2)}) collective-permute-start(bf16[2,256,1024]{2,1,0:T(8,128)(2,1)} %param.16), channel_id=1, source_target_pairs={{0,1},{1,0},{2,3},{3,2},{4,5},{5,4},{6,7},{7,6},{8,9},{9,8},{10,11... | collective-permute-start | bytes 3145736 | tf_op jit(solution)/shard_map/ppermute | solution.py:276
  9.3 30.0 %collective-permute-start.1 = (bf16[2,32,1024]{2,1,0:T(8,128)(2,1)}, bf16[2,32,1024]{2,1,0:T(8,128)(2,1)S(1)}, u32[]{:S(2)}, u32[]{:S(2)}) collective-permute-start(bf16[2,32,1024]{2,1,0:T(8,128)(2,1)} %constant_dynamic-slice_fusion), channel_id=1, source_target_pairs={{0,2},{1,3},{2,0},{3,1},{4,6},{5,7},{6,4},{7,5},{8,10},{9,11},{10,... | collective-permute-start | bytes 393224 | tf_op jit(solution)/shard_map/ppermute | solution.py:276
  11.9 18.6 %copy-start.3 = (bf16[2,1024,768]{2,1,0:T(8,128)(2,1)S(1)}, bf16[2,1024,768]{2,1,0:T(8,128)(2,1)}, u32[]{:S(2)}) copy-start(bf16[2,1024,768]{2,1,0:T(8,128)(2,1)} %param.14) | copy-start | bytes 9437188
  30.5 3.3 copy-start
  33.8 4.9 copy-start.15
  39.3 0.7 copy-start.11
  40.0 615.7 %all-reduce.3.cloned.1.call-start = ((), (), s32[]{:S(2)}) async-start(), calls=%async_computation.1 | async-start | bytes 12582912 | tf_op jit(solution)/shard_map/psum | solution.py:1364
  128.2 63.6 %collective-permute-start.2 = (bf16[2,256,1024]{2,1,0:T(8,128)(2,1)}, bf16[2,256,1024]{2,1,0:T(8,128)(2,1)}, u32[]{:S(2)}, u32[]{:S(2)}) collective-permute-start(bf16[2,256,1024]{2,1,0:T(8,128)(2,1)} %all-gather.2.cloned.1.call-done), channel_id=1, source_target_pairs={{0,1},{1,0},{2,3},{3,2},{4,5},{5,4},{6,7},{7,6},{8,9},{9,8},{10,11... | collective-permute-start | bytes 3145736 | tf_op jit(solution)/shard_map/ppermute | solution.py:276
  128.3 61.6 %copy-start.13 = (bf16[2,1024]{1,0:T(2,128)(2,1)S(1)}, bf16[2,1024]{1,0:T(2,128)(2,1)}, u32[]{:S(2)}) copy-start(bf16[2,1024]{1,0:T(2,128)(2,1)} %param.17) | copy-start | bytes 12292
  188.5 3.3 copy-start.9
  280.2 4.7 copy-start.17
  285.0 8.1 %copy-start.24 = (bf16[2048,1024]{1,0:T(8,128)(2,1)S(1)}, bf16[2048,1024]{1,0:T(8,128)(2,1)}, u32[]{:S(2)}) copy-start(bf16[2048,1024]{1,0:T(8,128)(2,1)} %get-tuple-element.75) | copy-start | bytes 12582916
  285.0 8.1 %copy-start.26 = (bf16[2048,1024]{1,0:T(8,128)(2,1)S(1)}, bf16[2048,1024]{1,0:T(8,128)(2,1)}, u32[]{:S(2)}) copy-start(bf16[2048,1024]{1,0:T(8,128)(2,1)} %get-tuple-element.76) | copy-start | bytes 12582916
  293.1 5.8 copy-start.19
  293.1 5.8 copy-start.21
  303.7 98.6 %copy-start.12 = (f32[16,1024]{1,0:T(8,128)S(1)}, f32[16,1024]{1,0:T(8,128)}, u32[]{:S(2)}) copy-start(f32[16,1024]{1,0:T(8,128)} %get-tuple-element.67) | copy-start | bytes 196612
  402.3 7.0 %copy-start.18 = (bf16[2048,1024]{1,0:T(8,128)(2,1)S(1)}, bf16[2048,1024]{1,0:T(8,128)(2,1)}, u32[]{:S(2)}) copy-start(bf16[2048,1024]{1,0:T(8,128)(2,1)} %get-tuple-element.64) | copy-start | bytes 12582916
  402.3 7.0 %copy-start.20 = (bf16[2048,768]{1,0:T(8,128)(2,1)S(1)}, bf16[2048,768]{1,0:T(8,128)(2,1)}, u32[]{:S(2)}) copy-start(bf16[2048,768]{1,0:T(8,128)(2,1)} %get-tuple-element.65) | copy-start | bytes 9437188
  409.3 4.7 copy-start.16
  409.3 4.7 copy-start.23
  414.0 5.8 copy-start.22
  414.0 5.8 copy-start.25
  652.6 23.2 %copy-start.14 = (f32[2,1,1024]{2,0,1:T(2,128)}, f32[2,1,1024]{2,0,1:T(2,128)S(1)}, u32[]{:S(2)}) copy-start(f32[2,1,1024]{2,0,1:T(2,128)S(1)} %copy.44) | copy-start | bytes 24580
  655.7 3.0 copy-start.6
  658.6 1.6 copy-start.5
  659.1 2.2 copy-start.4
  661.3 3.1 copy-start.10
  664.4 2.9 copy-start.2
  667.3 4.2 copy-start.1
  671.6 4.9 copy-start.7
  675.8 1.9 copy-start.8
Sparse Core Ops, SparseCore 0:
  40.1 40.3 all-gather.1
  303.8 286.7 all-reduce.2

commit v2 on v1

--- a/solution.py
+++ b/solution.py
@@ -529,11 +529,11 @@
     return me + 1 - 2 * lax.rem(me, 2), lax.rem(me + 2, 4)
 
 
-def greet(others):
+def greet(others, more=0):
     barrier = pltpu.get_barrier_semaphore()
     for other in others:
         pl.semaphore_signal(barrier, inc=1, device_id={"tensor": other}, device_id_type=MESH)
-    pl.semaphore_wait(barrier, len(others))
+    pl.semaphore_wait(barrier, len(others) + more)
 
 
 def remote(src, dst, sems, index, target):
@@ -551,6 +551,20 @@
     return pl.ds(pl.multiple_of(i * size, size), size)
 
 
+def loader(sems, **pairs):
+    waiting = {}
+    for i, (name, (src, dst)) in enumerate(pairs.items()):
+        waiting[name] = pltpu.make_async_copy(src, dst, sems.at[i])
+        waiting[name].start()
+
+    def need(*names):
+        for name in names:
+            if name in waiting:
+                waiting.pop(name).wait()
+
+    return need
+
+
 def by_kind(rows, heads):
     return jnp.concatenate(
         [
@@ -581,11 +595,10 @@
     return last if n == QB else jnp.concatenate([s[:, : n - QB], last], axis=1)
 
 
-def forward_layer_kernel(first, final, rows, w, *refs):
+def forward_layer_kernel(l, first, final, rows, w, *refs):
     it = iter(refs)
-    x_ref, up_ref, upb_ref, down_ref, qkvw_ref, qkvb_ref = (next(it) for _ in range(6))
-    out_ref, ob_ref, gain_ref, shift_ref = (next(it) for _ in range(4))
-    cos_ref, lo_ref, hi_ref = (next(it) for _ in range(3))
+    x_ref, up_h, down_h, qkvw_h, out_h, cos_h, lo_h, hi_h = (next(it) for _ in range(8))
+    upb_ref, qkvb_ref, ob_ref, gain_ref, shift_ref = (next(it) for _ in range(5))
     cot_ref = next(it) if final else None
     na_o, nb_o, u_o, hid_o, qkv_o, ctx_o, lse_o, x_o = (next(it) for _ in range(8))
     far_o = next(it) if first or final else None
@@ -593,8 +606,19 @@
     qkv_s, ctx_s, lse_s = (next(it) for _ in range(3))
     far_s = next(it) if first or final else None
     mine_s = next(it)
-    send, recv, local, u_sem = (next(it) for _ in range(4))
+    up_ref, down_ref, qkvw_ref, out_ref, cos_ref, lo_ref, hi_ref = (next(it) for _ in range(7))
+    send, recv, local, u_sem, load_sem = (next(it) for _ in range(5))
     sems = (send, recv)
+    need = loader(
+        load_sem,
+        up=(up_h.at[l], up_ref),
+        qkvw=(qkvw_h.at[l], qkvw_ref),
+        cos=(cos_h, cos_ref),
+        lo=(lo_h, lo_ref),
+        hi=(hi_h, hi_ref),
+        down=(down_h.at[l], down_ref),
+        out=(out_h.at[l], out_ref),
+    )
 
     seq = 2 * rows
     heads = w // HEAD
@@ -646,6 +670,7 @@
 
     def feed(k):
         gathers[k][0].wait()
+        need("up")
         keep(nb_s.at[k], nb_o.at[pl.ds(k * seq, seq), :], 2 * k)
         for h in (1, 0):
             for copy in u_out:
@@ -668,6 +693,8 @@
         keep(hid_s.at[k], hid_o.at[pl.ds(k * seq, seq), :], 2 * k + 1)
 
     def join(k):
+        need("down", "out")
+
         @pl.loop(0, half_blocks)
         def _(r):
             at = block(r + half_blocks)
@@ -692,9 +719,8 @@
         def _(r):
             at = block(r)
             total = precv[k, at, :] + mine_s[at, :]
-            if final and k == 0:
-                precv[k, at, :] = total
-            else:
+            precv[k, at, :] = total
+            if not (final and k == 0):
                 ysend[k, at, :] = total.astype(B16)
 
         if not (final and k == 0):
@@ -705,6 +731,7 @@
 
     def attend(k):
         gathers[k][1].wait()
+        need("qkvw", "cos", "lo", "hi")
         keep(na_s.at[k], na_o.at[pl.ds(k * seq, seq), :], 4 + 2 * k)
         swapped = lambda i: block(lax.rem(i + shift, blocks))
 
@@ -750,8 +777,7 @@
         @pl.loop(0, half_blocks)
         def _(r):
             at = block(r)
-            mine = precv[k, at, :] if final else ysend[k, at, :].astype(F32)
-            both = mine + yrecv[k, at, :].astype(F32)
+            both = precv[k, at, :] + yrecv[k, at, :].astype(F32)
             precv[k, at, :] = x_rows(k, r) + (both + ob_ref[...])
 
         keep(precv.at[k], x_o.at[pl.ds(k * rows, rows), :], 12 + k)
@@ -793,13 +819,13 @@
         copy.wait_send()
 
 
-def forward_layer(l, layers, x, up, upb, down, qkvw, qkvb, out, ob, gains, shifts, tables, cot):
+def forward_layer(l, layers, x, up, down, qkvw, out, tables, upb, qkvb, ob, gains, shifts, cot):
     first, final = l == 0, l == layers - 1
     features = x.shape[1]
     rows = x.shape[0] if first else x.shape[0] // 2
     seq = 2 * rows
-    w = qkvw.shape[1] // 3
-    ff = up.shape[1]
+    w = qkvw.shape[2] // 3
+    ff = up.shape[2]
     shape = jax.ShapeDtypeStruct
     out_shape = [
         shape((2 * seq, features), B16),
@@ -813,7 +839,7 @@
     ]
     if first or final:
         out_shape.append(shape((rows, features), B16))
-    args = [x, up, upb, down, qkvw, qkvb, out, ob, gains, shifts, *tables]
+    args = [x, up, down, qkvw, out, *tables, upb, qkvb, ob, gains, shifts]
     if final:
         args.append(cot)
     scratch = [
@@ -832,10 +858,12 @@
     if first or final:
         scratch.append(pltpu.VMEM((rows, features), B16))
     scratch.append(pltpu.VMEM((rows, features), F32))
-    scratch += [DMA((9,)), DMA((9,)), DMA((15,)), DMA((rows // QB,))]
+    scratch += [pltpu.VMEM(item.shape[1:], B16) for item in (up, down, qkvw, out)]
+    scratch += [pltpu.VMEM(item.shape, F32) for item in tables]
+    scratch += [DMA((9,)), DMA((9,)), DMA((15,)), DMA((rows // QB,)), DMA((7,))]
     return pl.pallas_call(
-        functools.partial(forward_layer_kernel, first, final, rows, w),
-        in_specs=[VMEM] * len(args),
+        functools.partial(forward_layer_kernel, l, first, final, rows, w),
+        in_specs=[VMEM] + [ANY] * 7 + [VMEM] * (len(args) - 8),
         out_specs=[ANY] * len(out_shape),
         out_shape=out_shape,
         scratch_shapes=scratch,
@@ -851,20 +879,295 @@
     )(*args)
 
 
-def backward_layer_kernel(first, final, rows, w, *refs):
+def ring_place(index, size):
+    side = lax.rem(index, 2)
+    level = index // 2
+    return level * (1 - side) + (size - 1 - level) * side
+
+
+def ring_device(place, size):
+    side = place // (size // 2)
+    return (1 - side) * 2 * place + side * (2 * (size - 1 - place) + 1)
+
+
+class Ring:
+    def __init__(self, n):
+        self.n = n
+        self.place = ring_place(lax.axis_index("dp"), n)
+        self.targets = (
+            ring_device(lax.rem(self.place + 1, n), n),
+            ring_device(lax.rem(self.place + n - 1, n), n),
+        )
+        far = n // 2
+        self.routes = ((0, 0, far), (0, 1, n - 1 - far), (1, 0, n - 1 - far), (1, 1, far))
+
+    def greet(self):
+        barrier = pltpu.get_barrier_semaphore()
+        for other in self.targets:
+            pl.semaphore_signal(barrier, inc=1, device_id={"dp": other}, device_id_type=MESH)
+
+    def rows(self, array, half, offset):
+        size = array.shape[0] // (2 * self.n)
+        chunk = lax.rem(self.place + offset + 2 * self.n, self.n)
+        return pl.ds(pl.multiple_of((chunk * 2 + half) * size, size), size)
+
+    def copy(self, src, dst, sems, at, way):
+        return pltpu.make_async_remote_copy(
+            src_ref=src,
+            dst_ref=dst,
+            send_sem=sems[0].at[at],
+            recv_sem=sems[1].at[at],
+            device_id={"dp": self.targets[way]},
+            device_id_type=MESH,
+        )
+
+
+class Scatter:
+    def __init__(self, ring, ins, chunk, it):
+        self.ring, self.ins, self.chunk = ring, ins, chunk
+        self.slots = [next(it) for _ in ins]
+        self.mine = [next(it) for _ in ins]
+        self.sems = (next(it), next(it))
+        self.load = next(it)
+        self.parts = [(a, m) for a in range(len(ins)) for m in range(4)]
+
+    @staticmethod
+    def scratch(n, shapes):
+        count = len(shapes)
+        size = lambda a: a // (2 * n)
+        return (
+            [pltpu.VMEM((4, n // 2, size(a), b), B16) for a, b in shapes]
+            + [pltpu.VMEM((4, size(a), b), B16) for a, b in shapes]
+            + [DMA((count, 4, n // 2)), DMA((count, 4, n // 2)), DMA((count, 4))]
+        )
+
+    def sent(self, a, m, step):
+        half, way, steps = self.ring.routes[m]
+        offset = steps - step
+        if step:
+            src = self.slots[a].at[m, step - 1]
+        else:
+            src = self.ins[a].at[self.ring.rows(self.ins[a], half, -offset if way else offset), :]
+        return self.ring.copy(src, self.slots[a].at[m, step], self.sems, (a, m, step), way)
+
+    def fetch(self, a, m, step):
+        half, way, steps = self.ring.routes[m]
+        offset = steps - step - 1
+        return pltpu.make_async_copy(
+            self.ins[a].at[self.ring.rows(self.ins[a], half, -offset if way else offset), :],
+            self.mine[a].at[m],
+            self.load.at[a, m],
+        )
+
+    def start(self):
+        for a, m in self.parts:
+            self.sent(a, m, 0).start()
+        for a, m in self.parts:
+            self.fetch(a, m, 0).start()
+
+    def step(self, step):
+        for a, m in self.parts:
+            half, way, steps = self.ring.routes[m]
+            if step >= steps:
+                continue
+            self.sent(a, m, step).wait_recv()
+            if step + 1 < steps:
+                self.fetch(a, m, step).wait()
+                total = self.slots[a][m, step].astype(F32) + self.mine[a][m].astype(F32)
+                self.slots[a][m, step] = total.astype(B16)
+                self.sent(a, m, step + 1).start()
+                if way == 0 or step + 2 < steps:
+                    self.fetch(a, m, step + 1).start()
+        if step == self.ring.n // 2 - 1:
+            for a in range(len(self.ins)):
+                for half in (0, 1):
+                    m, other = 2 * half, 2 * half + 1
+                    self.fetch(a, m, self.ring.routes[m][2] - 1).wait()
+                    total = self.mine[a][m].astype(F32)
+                    for route in (m, other):
+                        last = self.ring.routes[route][2] - 1
+                        total = total + self.slots[a][route, last].astype(F32)
+                    size = total.shape[0]
+                    self.chunk[a][half * size : (half + 1) * size, :] = total.astype(B16)
+
+    def finish(self):
+        for a, m in self.parts:
+            for step in range(self.ring.routes[m][2]):
+                self.sent(a, m, step).wait_send()
+
+
+class Gather:
+    def __init__(self, ring, chunk, done, it):
+        self.ring, self.chunk, self.done = ring, chunk, done
+        self.sems = (next(it), next(it))
+        self.local = next(it)
+        self.parts = [(a, m) for a in range(len(chunk)) for m in range(4)]
+
+    @staticmethod
+    def scratch(n, count):
+        return [DMA((count, 4, n // 2)), DMA((count, 4, n // 2)), DMA((count, 2))]
+
+    def sent(self, a, m, step):
+        half, way, steps = self.ring.routes[m]
+        at = self.ring.rows(self.done[a], half, step if way else -step)
+        size = self.done[a].shape[0] // (2 * self.ring.n)
+        src = self.done[a].at[at, :] if step else self.chunk[a].at[pl.ds(half * size, size), :]
+        return self.ring.copy(src, self.done[a].at[at, :], self.sems, (a, m, step), way)
+
+    def own(self, a, half):
+        size = self.done[a].shape[0] // (2 * self.ring.n)
+        return pltpu.make_async_copy(
+            self.chunk[a].at[pl.ds(half * size, size), :],
+            self.done[a].at[self.ring.rows(self.done[a], half, 0), :],
+            self.local.at[a, half],
+        )
+
+    def start(self):
+        for a, m in self.parts:
+            self.sent(a, m, 0).start()
+        for a in range(len(self.chunk)):
+            for half in (0, 1):
+                self.own(a, half).start()
+
+    def step(self, step):
+        for a, m in self.parts:
+            steps = self.ring.routes[m][2]
+            if step < steps:
+                self.sent(a, m, step).wait_recv()
+                if step + 1 < steps:
+                    self.sent(a, m, step + 1).start()
+
+    def finish(self):
+        for a, m in self.parts:
+            for step in range(self.ring.routes[m][2]):
+                self.sent(a, m, step).wait_send()
+        for a in range(len(self.chunk)):
+            for half in (0, 1):
+                self.own(a, half).wait()
+
+
+def last_sums_kernel(n, *refs):
     it = iter(refs)
-    grad_ref, u_ref, down_ref, up_ref, ow_ref, qkvw_ref = (next(it) for _ in range(6))
-    qkv_ref, lse_ref, ctx_ref, outall_ref, ob_ref, xn_ref, x_ref = (next(it) for _ in range(7))
+    ready = [next(it) for _ in range(2)]
+    ins = [next(it) for _ in range(2)]
+    small_in = next(it)
+    done = [next(it) for _ in range(4)]
+    small_out = next(it)
+    ring = Ring(n)
+    chunk = [next(it) for _ in range(2)]
+    first = Gather(ring, ready, done[:2], it)
+    sums = Scatter(ring, ins, chunk, it)
+    second = Gather(ring, chunk, done[2:], it)
+    small_s, small_send, small_recv = (next(it) for _ in range(3))
+    ring.greet()
+    pl.semaphore_wait(pltpu.get_barrier_semaphore(), 2)
+
+    def small_copy(step):
+        at = lax.rem(ring.place + n - step, n)
+        return pltpu.make_async_remote_copy(
+            src_ref=small_s.at[at],
+            dst_ref=small_s.at[at],
+            send_sem=small_send.at[step],
+            recv_sem=small_recv.at[step],
+            device_id={"dp": ring.targets[0]},
+            device_id_type=MESH,
+        )
+
+    small_s[ring.place] = small_in[...]
+    sums.start()
+    small_copy(0).start()
+    first.start()
+    for step in range(n // 2):
+        sums.step(step)
+        if step == n // 2 - 1:
+            second.start()
+        first.step(step)
+        small_copy(step).wait_recv()
+        small_copy(step + 1).start()
+    for step in range(n // 2):
+        second.step(step)
+        if n // 2 + step < n - 1:
+            small_copy(n // 2 + step).wait_recv()
+            if n // 2 + step < n - 2:
+                small_copy(n // 2 + step + 1).start()
+    total = small_s[0]
+    for i in range(1, n):
+        total = total + small_s[i]
+    small_out[...] = total
+    for part in (first, sums, second):
+        part.finish()
+    for step in range(n - 1):
+        small_copy(step).wait_send()
+
+
+def last_sums(ready, arrays, small, collective_id):
+    n = lax.axis_size("dp")
+    shape = jax.ShapeDtypeStruct
+    shapes = [item.shape for item in arrays]
+    full = [(item.shape[0] * n, item.shape[1]) for item in ready] + shapes
+    size = sum(a * b for a, b in full)
+    return pl.pallas_call(
+        functools.partial(last_sums_kernel, n),
+        in_specs=[ANY] * 4 + [VMEM],
+        out_specs=[ANY] * 4 + [VMEM],
+        out_shape=[shape(item, B16) for item in full] + [shape(small.shape, F32)],
+        scratch_shapes=[pltpu.VMEM((a // n, b), B16) for a, b in shapes]
+        + Gather.scratch(n, 2)
+        + Scatter.scratch(n, shapes)
+        + Gather.scratch(n, 2)
+        + [pltpu.VMEM((n,) + small.shape, F32)]
+        + [DMA((n - 1,))] * 2,
+        compiler_params=pltpu.CompilerParams(
+            vmem_limit_bytes=40 * MIB, collective_id=collective_id, has_side_effects=True
+        ),
+        cost_estimate=pl.CostEstimate(flops=size, bytes_accessed=400 * MIB, transcendentals=0),
+        name="last_sums",
+    )(*ready, *arrays, small)
+
+
+def backward_layer_kernel(l, first, final, rows, w, n, *refs):
+    it = iter(refs)
+    grad_ref, u_ref, down_h, up_h, ow_h, qkvw_h = (next(it) for _ in range(6))
+    outall_h, cos_h, lo_h, hi_h = (next(it) for _ in range(4))
+    qkv_h, lse_h, ctx_ref, xn_h, x_ref = (next(it) for _ in range(5))
     far_ref = next(it) if first else None
     farg_ref = next(it) if final else None
-    gain_ref, cos_ref, lo_ref, hi_ref = (next(it) for _ in range(4))
-    g_o, dpre_o, dqkv_o = (next(it) for _ in range(3))
-    dx_ref, small_ref = (next(it) for _ in range(2))
+    gain_ref, ob_ref = (next(it) for _ in range(2))
+    hid_h, nb_h, na_h = (next(it) for _ in range(3))
+    ready = [next(it) for _ in range(4)] if first else []
+    dx_o, small_ref = (next(it) for _ in range(2))
+    wide_g = [next(it) for _ in range(2)]
+    narrow_g = [next(it) for _ in range(2)]
+    chunk_ref = [next(it) for _ in range(2)]
+    done = [next(it) for _ in range(4)] if first else []
     g_s, dpre_s, dqkv_s, dq_s, dk_s, dv_s, dctx_s = (next(it) for _ in range(7))
-    u_s, bsend, brecv, asend, arecv, zown, ysend, yrecv = (next(it) for _ in range(8))
+    u_s, osend, brecv, arecv, ysend, yrecv = (next(it) for _ in range(6))
     cfull, got_s = (next(it) for _ in range(2))
-    send, recv, local, u_sem = (next(it) for _ in range(4))
+    down_ref, up_ref, ow_ref, qkvw_ref, outall_ref = (next(it) for _ in range(5))
+    cos_ref, lo_ref, hi_ref, qkv_ref, lse_ref = (next(it) for _ in range(5))
+    send, recv, local, u_sem, load_sem = (next(it) for _ in range(5))
     sems = (send, recv)
+    a_s, o_s, a_sem, o_sem = (next(it) for _ in range(4))
+    ring = Ring(n)
+    wide_sum = Scatter(ring, wide_g, chunk_ref, it)
+    if first:
+        chunk_s = [next(it) for _ in range(2)]
+        wide_last = Gather(ring, ready[:2], done[:2], it)
+        narrow_sum = Scatter(ring, ready[2:], chunk_s, it)
+        narrow_last = Gather(ring, chunk_s, done[2:], it)
+    need = loader(
+        load_sem,
+        down=(down_h.at[l], down_ref),
+        up=(up_h.at[l], up_ref),
+        ow=(ow_h.at[l], ow_ref),
+        qkv=(qkv_h, qkv_ref),
+        lse=(lse_h, lse_ref),
+        cos=(cos_h, cos_ref),
+        lo=(lo_h, lo_ref),
+        hi=(hi_h, hi_ref),
+        qkvw=(qkvw_h.at[l], qkvw_ref),
+        outall=(outall_h.at[l], outall_ref),
+    )
 
     seq = 2 * rows
     ff = up_ref.shape[1]
@@ -875,14 +1178,8 @@
     swapped = lambda i: block(lax.rem(i + shift, blocks))
     core, far = partners()
     diag = lax.rem(core + 2, 4)
-    greet((core, far, diag))
-    outs = []
-
-    def keep(src, dst, index):
-        copy = pltpu.make_async_copy(src, dst, local.at[index])
-        copy.start()
-        outs.append(copy)
-
+    ring.greet()
+    greet((core, far, diag), 2)
     def load_u(k, i):
         return pltpu.make_async_copy(
             u_ref.at[pl.ds(k * seq + i * QB, QB), :], u_s.at[i % 2], u_sem.at[i % 2]
@@ -907,6 +1204,9 @@
         across.start()
     near0 = remote(own_half(g_s, 0), other_half(g_s, 0), sems, 1, core)
     near0.start()
+    if first:
+        wide_last.start()
+        narrow_sum.start()
     cfull[:, :w] = ctx_ref[:rows, :]
     contexts = [
         remote(ctx_ref.at[pl.ds(rows, rows), :], cfull.at[:, pl.ds(w, w)], sems, 8, core),
@@ -919,6 +1219,7 @@
     swaps = {}
 
     def feed(k):
+        need("down")
         for i in range(blocks):
             load_u(k, i).wait()
             at = pl.ds(i * QB, QB)
@@ -931,17 +1232,20 @@
             elif k == 0:
                 load_u(1, i + 2 - blocks).start()
 
+        need("up")
+        if k == 1:
+            swaps[0][0].wait_send()
+
         @pl.loop(0, half_blocks)
         def _(r):
-            bsend[k, block(r), :] = dot_nt(
-                dpre_s[k, block(r + half_blocks), :], up_ref[...]
-            ).astype(B16)
-
-        swaps[k] = [remote(bsend.at[k], brecv.at[k], sems, 3 + 2 * k, core)]
+            osend[block(r), :] = dot_nt(dpre_s[k, block(r + half_blocks), :], up_ref[...])
+
+        swaps[k] = [remote(osend, brecv.at[k], sems, 3 + 2 * k, core)]
         swaps[k][0].start()
-        keep(dpre_s.at[k], dpre_o.at[pl.ds(k * seq, seq), :], k)
-
-    def attend(k):
+
+    def attend(k, pump):
+        need("ow", "qkv", "lse", "cos", "lo", "hi", "qkvw")
+
         @pl.loop(0, blocks)
         def _(r):
             dctx_s[block(r), :] = dot_nt(g_s[k, swapped(r), :], ow_ref[...]).astype(B16)
@@ -974,6 +1278,7 @@
                 dq_s[i * QB : n, :] += dot_nn(ds, qkv_ref[base : base + n, w : 2 * w] * scale)
                 dk_s[:n, :] += dot_tn(ds, q)
                 dv_s[:n, :] += dot_tn(p.astype(B16), d)
+            pump(h)
 
         @pl.loop(0, blocks)
         def _(r):
@@ -984,15 +1289,14 @@
             dqkv_s[k, swapped(r), :] = low
             small_ref[9:10, : 3 * w] += jnp.sum(low.astype(F32), axis=0, keepdims=True)
 
+        swaps[1][1 - k].wait_send()
+
         @pl.loop(0, half_blocks)
         def _(r):
-            asend[k, block(r), :] = dot_nt(
-                dqkv_s[k, block(r + half_blocks), :], qkvw_ref[...]
-            ).astype(B16)
-
-        swaps[k].append(remote(asend.at[k], arecv.at[k], sems, 4 + 2 * k, core))
+            osend[block(r), :] = dot_nt(dqkv_s[k, block(r + half_blocks), :], qkvw_ref[...])
+
+        swaps[k].append(remote(osend, arecv.at[k], sems, 4 + 2 * k, core))
         swaps[k][1].start()
-        keep(dqkv_s.at[k], dqkv_o.at[pl.ds(base, seq), :], 2 + k)
 
     def x_rows(k, r):
         if not first:
@@ -1001,13 +1305,13 @@
 
     def fold(k):
         for copy in swaps[k]:
-            copy.wait()
+            copy.wait_recv()
 
         @pl.loop(0, half_blocks)
         def _(r):
             at = block(r)
-            d_na = dot_nt(dqkv_s[k, at, :], qkvw_ref[...]) + arecv[k, at, :].astype(F32)
-            d_nb = dot_nt(dpre_s[k, at, :], up_ref[...]) + brecv[k, at, :].astype(F32)
+            d_na = dot_nt(dqkv_s[k, at, :], qkvw_ref[...]) + arecv[k, at, :]
+            d_nb = dot_nt(dpre_s[k, at, :], up_ref[...]) + brecv[k, at, :]
             z, _ = standardize(x_rows(k, r))
             small_ref[0:1, :] += jnp.sum(d_na * z, axis=0, keepdims=True)
             small_ref[1:2, :] += jnp.sum(d_nb * z, axis=0, keepdims=True)
@@ -1015,26 +1319,116 @@
             small_ref[3:4, :] += jnp.sum(d_nb, axis=0, keepdims=True)
             d_z = d_na * gain_ref[0:1, :] + d_nb * gain_ref[1:2, :]
             if k == 0:
-                zown[at, :] = d_z
+                arecv[0, at, :] = d_z
             else:
                 ysend[at, :] = d_z.astype(B16)
 
+    def weight_grad(left, right, out):
+        tiles = left.shape[1] // QB
+        width = out.shape[1]
+
+        def load(i):
+            slot = lax.rem(i, 2)
+            return pltpu.make_async_copy(left.at[:, block(i)], a_s.at[slot], a_sem.at[slot])
+
+        def store(i):
+            slot = lax.rem(i, 2)
+            return pltpu.make_async_copy(
+                o_s.at[slot, :, pl.ds(0, width)], out.at[block(i), :], o_sem.at[slot]
+            )
+
+        load(0).start()
+
+        @pl.loop(0, tiles)
+        def _(i):
+            slot = lax.rem(i, 2)
+            load(i).wait()
+
+            @pl.when(i + 1 < tiles)
+            def _():
+                load(i + 1).start()
+
+            @pl.when(i >= 2)
+            def _():
+                store(i - 2).wait()
+
+            total = dot_tn(a_s[slot, :seq, :], right[0]) + dot_tn(a_s[slot, seq:, :], right[1])
+            o_s[slot, :, :width] = total.astype(B16)
+            store(i).start()
+
+        for i in range(max(tiles - 2, 0), tiles):
+            store(i).wait()
+
+    def at_heads(**calls):
+        def pump(h):
+            for name, todo in calls.items():
+
+                @pl.when(h == int(name[1:]))
+                def _():
+                    todo()
+
+        return pump
+
     near0.wait()
-    keep(g_s.at[0], g_o.at[pl.ds(0, seq), :], 4)
     feed(0)
-    if not final:
+    if first:
+        narrow_sum.step(0)
         across.wait()
     near1 = remote(own_half(g_s, 1), other_half(g_s, 1), sems, 2, core)
     near1.start()
+    if first:
+        wide_last.step(0)
     near1.wait()
-    keep(g_s.at[1], g_o.at[pl.ds(seq, seq), :], 5)
     feed(1)
-    attend(1)
+    if first:
+        narrow_sum.step(1)
+    weight_grad(hid_h, g_s, wide_g[0])
+    if first:
+        wide_last.step(1)
+    weight_grad(nb_h, dpre_s, wide_g[1])
+    wide_sum.start()
+    if first:
+        narrow_sum.step(2)
+
+        def later():
+            wide_last.step(2)
+            narrow_sum.step(3)
+            narrow_last.start()
+
+        attend(1, at_heads(h2=later))
+    else:
+        attend(1, at_heads(h2=lambda: wide_sum.step(0)))
     fold(1)
     back = remote(ysend, yrecv, sems, 7, far)
     back.start()
-    attend(0)
+    next_rows = pltpu.make_async_copy(xn_h.at[pl.ds(0, rows), :], arecv.at[1], local.at[0])
+    next_rows.start()
+    if first:
+        wide_sum.step(0)
+
+        def later():
+            wide_last.step(3)
+            narrow_last.step(0)
+            wide_sum.step(1)
+
+        attend(0, at_heads(h2=later))
+        narrow_last.step(1)
+    else:
+        wide_sum.step(1)
+        attend(0, at_heads(h2=lambda: wide_sum.step(2)))
     fold(0)
+    if first:
+        wide_sum.step(2)
+        narrow_last.step(2)
+    else:
+        wide_sum.step(3)
+    weight_grad(na_h, dqkv_s, narrow_g[0])
+    weight_grad(ctx_ref, g_s, narrow_g[1])
+    if first:
+        wide_sum.step(3)
+        narrow_last.step(3)
+    need("outall")
+    next_rows.wait()
     for copy in contexts:
         copy.wait()
 
@@ -1042,7 +1436,7 @@
     def _(r):
         at = block(r)
         attn = dot_nn(cfull[at, :], outall_ref[...]) + ob_ref[...]
-        x_next = xn_ref[at, :]
+        x_next = arecv[1, at, :]
         feed_out = x_next - x_rows(0, r) - attn
         small_ref[5:6, :] += jnp.sum(x_next * x_next, axis=0, keepdims=True)
         small_ref[6:7, :] += jnp.sum(attn * attn, axis=0, keepdims=True)
@@ -1058,43 +1452,75 @@
     @pl.loop(0, half_blocks)
     def _(r):
         at = block(r)
-        total = zown[at, :] + yrecv[at, :].astype(F32)
+        total = arecv[0, at, :] + yrecv[at, :].astype(F32)
         z, inverse = standardize(x_rows(0, r))
         slope = total - jnp.mean(total, axis=-1, keepdims=True)
         slope = slope - z * jnp.mean(total * z, axis=-1, keepdims=True)
-        dx_ref[at, :] = grad_ref[at, :].astype(F32) + slope * inverse
-
-    for copy in outs:
-        copy.wait()
+        arecv[0, at, :] = grad_ref[at, :].astype(F32) + slope * inverse
+
+    grad_out = pltpu.make_async_copy(arecv.at[0], dx_o, local.at[1])
+    grad_out.start()
+    swaps[0][1].wait_send()
+    wide_sum.finish()
+    if first:
+        wide_last.finish()
+        narrow_sum.finish()
+        narrow_last.finish()
+    grad_out.wait()
 
 
 def backward_layer(
-    l, layers, grad, u, down, up, out_w, qkvw, qkv, lse, ctx, out_all, ob, xn, x, far_x, far_g, gains, tables
+    l,
+    layers,
+    grad,
+    u,
+    down,
+    up,
+    out_w,
+    qkvw,
+    out_all,
+    tables,
+    qkv,
+    lse,
+    ctx,
+    xn,
+    x,
+    far_x,
+    far_g,
+    gains,
+    ob,
+    hidden,
+    nb,
+    na,
+    ready,
 ):
     first, final = l == 0, l == layers - 1
     rows, features = grad.shape
     seq = 2 * rows
-    w = qkvw.shape[1] // 3
-    ff = up.shape[1]
+    w = qkvw.shape[2] // 3
+    ff = up.shape[2]
+    n = lax.axis_size("dp")
+    wide_shapes = [(ff, features), (features, ff)]
+    narrow_shapes = [(features, 3 * w), (w, features)]
     shape = jax.ShapeDtypeStruct
-    args = [grad, u, down, up, out_w, qkvw, qkv, lse, ctx, out_all, ob, xn, x]
-    in_specs = [VMEM, ANY] + [VMEM] * 11
+    args = [grad, u, down, up, out_w, qkvw, out_all, *tables, qkv, lse, ctx, xn, x]
+    in_specs = [VMEM] + [ANY] * 11 + [VMEM, ANY, VMEM]
     if first:
         args.append(far_x)
         in_specs.append(VMEM)
     if final:
         args.append(far_g)
         in_specs.append(VMEM)
-    args += [gains, *tables]
-    in_specs += [VMEM] * 4
-    out_shape = [
-        shape((2 * seq, features), B16),
-        shape((2 * seq, ff), B16),
-        shape((2 * seq, 3 * w), B16),
-        shape((rows, features), F32),
-        shape((16, features), F32),
-    ]
-    half = lambda dtype: pltpu.VMEM((2, rows, features), dtype)
+    args += [gains, ob, hidden, nb, na, *ready]
+    in_specs += [VMEM] * 2 + [ANY] * (3 + len(ready))
+    low = lambda shapes: [shape(item, B16) for item in shapes]
+    chunks = [(a // n, b) for a, b in wide_shapes]
+    out_shape = [shape((rows, features), F32), shape((16, features), F32)]
+    out_shape += low(wide_shapes + narrow_shapes + chunks)
+    out_specs = [ANY, VMEM] + [ANY] * 4 + [VMEM] * 2
+    if first:
+        out_shape += low(wide_shapes + narrow_shapes)
+        out_specs += [ANY] * 4
     scratch = [
         pltpu.VMEM((2, seq, features), B16),
         pltpu.VMEM((2, seq, ff), B16),
@@ -1104,24 +1530,30 @@
         pltpu.VMEM((seq, w), F32),
         pltpu.VMEM((seq, w), B16),
         pltpu.VMEM((2, QB, ff), F32),
-        half(B16),
-        half(B16),
-        half(B16),
-        half(B16),
         pltpu.VMEM((rows, features), F32),
+        pltpu.VMEM((2, rows, features), F32),
+        pltpu.VMEM((2, rows, features), F32),
         pltpu.VMEM((rows, features), B16),
         pltpu.VMEM((rows, features), B16),
         pltpu.VMEM((rows, 4 * w), B16),
         pltpu.VMEM((2, 8, features), F32),
-        DMA((13,)),
-        DMA((13,)),
-        DMA((6,)),
-        DMA((2,)),
     ]
+    scratch += [pltpu.VMEM(item.shape[1:], B16) for item in (down, up, out_w, qkvw, out_all)]
+    scratch += [pltpu.VMEM(item.shape, F32) for item in tables]
+    scratch += [pltpu.VMEM(qkv.shape, B16), pltpu.VMEM(lse.shape, F32)]
+    scratch += [DMA((13,)), DMA((13,)), DMA((2,)), DMA((2,)), DMA((10,))]
+    scratch += [pltpu.VMEM((2, 2 * seq, QB), B16), pltpu.VMEM((2, QB, features), B16)]
+    scratch += [DMA((2,)), DMA((2,))]
+    scratch += Scatter.scratch(n, wide_shapes)
+    if first:
+        scratch += [pltpu.VMEM((a // n, b), B16) for a, b in narrow_shapes]
+        scratch += Gather.scratch(n, 2)
+        scratch += Scatter.scratch(n, narrow_shapes)
+        scratch += Gather.scratch(n, 2)
     return pl.pallas_call(
-        functools.partial(backward_layer_kernel, first, final, rows, w),
+        functools.partial(backward_layer_kernel, l, first, final, rows, w, n),
         in_specs=in_specs,
-        out_specs=[ANY] * 3 + [VMEM] * 2,
+        out_specs=out_specs,
         out_shape=out_shape,
         scratch_shapes=scratch,
         compiler_params=pltpu.CompilerParams(
@@ -1134,142 +1566,6 @@
         ),
         name="backward_layer",
     )(*args)
-
-
-def ring_place(index, size):
-    side = lax.rem(index, 2)
-    level = index // 2
-    return level * (1 - side) + (size - 1 - level) * side
-
-
-def ring_device(place, size):
-    side = place // (size // 2)
-    return (1 - side) * 2 * place + side * (2 * (size - 1 - place) + 1)
-
-
-def ring_sum_kernel(n, shapes, *refs):
-    count = len(shapes)
-    it = iter(refs)
-    ins = [next(it) for _ in range(count)]
-    small_in = next(it)
-    outs = [next(it) for _ in range(count)]
-    small_out = next(it)
-    slots = [next(it) for _ in range(count)]
-    done = [next(it) for _ in range(count)]
-    small_s = next(it)
-    send, recv, small_send, small_recv = (next(it) for _ in range(4))
-
-    place = ring_place(lax.axis_index("dp"), n)
-    ahead = ring_device(lax.rem(place + 1, n), n)
-    behind = ring_device(lax.rem(place + n - 1, n), n)
-    barrier = pltpu.get_barrier_semaphore()
-    for other in (ahead, behind):
-        pl.semaphore_signal(barrier, inc=1, device_id={"dp": other}, device_id_type=MESH)
-    pl.semaphore_wait(barrier, 2)
-
-    def rows_of(a, way, step):
-        size = shapes[a][0] // (2 * n)
-        chunk = lax.rem(place + n - step, n) if way == 0 else lax.rem(place + step, n)
-        return pl.ds(pl.multiple_of((chunk * 2 + way) * size, size), size)
-
-    def copy(src, dst, a, way, step):
-        return pltpu.make_async_remote_copy(
-            src_ref=src,
-            dst_ref=dst,
-            send_sem=send.at[a, way, step],
-            recv_sem=recv.at[a, way, step],
-            device_id={"dp": (ahead, behind)[way]},
-            device_id_type=MESH,
-        )
-
-    def small_copy(step):
-        at = lax.rem(place + n - step, n)
-        return pltpu.make_async_remote_copy(
-            src_ref=small_s.at[at],
-            dst_ref=small_s.at[at],
-            send_sem=small_send.at[step],
-            recv_sem=small_recv.at[step],
-            device_id={"dp": ahead},
-            device_id_type=MESH,
-        )
-
-    small_s[place] = small_in[...]
-    flying = []
-
-    def launch(item):
-        item.start()
-        flying.append(item)
-        return item
-
-    last = n - 2
-    moving = {}
-    for a in range(count):
-        for way in (0, 1):
-            moving[a, way] = launch(
-                copy(ins[a].at[rows_of(a, way, 0), :], slots[a].at[way, 0], a, way, 0)
-            )
-    small = launch(small_copy(0))
-    for step in range(n - 1):
-        for a in range(count):
-            for way in (0, 1):
-                moving[a, way].wait_recv()
-                mine = ins[a][rows_of(a, way, step + 1), :].astype(F32)
-                total = slots[a][way, step].astype(F32) + mine
-                low = total.astype(B16)
-                slots[a][way, step] = low
-                if step < last:
-                    target = slots[a].at[way, step + 1]
-                else:
-                    target = done[a].at[rows_of(a, way, step + 1), :]
-                    outs[a][rows_of(a, way, step + 1), :] = low.astype(F32)
-                moving[a, way] = launch(
-                    copy(slots[a].at[way, step], target, a, way, step + 1)
-                )
-        small.wait_recv()
-        if step < last:
-            small = launch(small_copy(step + 1))
-    for step in range(n - 1):
-        for a in range(count):
-            for way in (0, 1):
-                at = rows_of(a, way, step)
-                moving[a, way].wait_recv()
-                if step < last:
-                    moving[a, way] = launch(
-                        copy(done[a].at[at, :], done[a].at[at, :], a, way, n + step)
-                    )
-                outs[a][at, :] = done[a][at, :].astype(F32)
-    total = small_s[0]
-    for i in range(1, n):
-        total = total + small_s[i]
-    small_out[...] = total
-    for item in flying:
-        item.wait_send()
-
-
-def ring_sum(arrays, small, collective_id):
-    n = lax.axis_size("dp")
-    shapes = [item.shape for item in arrays]
-    shape = jax.ShapeDtypeStruct
-    size = sum(a * b for a, b in shapes)
-    steps = 2 * n - 2
-    return pl.pallas_call(
-        functools.partial(ring_sum_kernel, n, shapes),
-        in_specs=[VMEM] * (len(arrays) + 1),
-        out_specs=[VMEM] * (len(arrays) + 1),
-        out_shape=[shape(item, F32) for item in shapes] + [shape(small.shape, F32)],
-        scratch_shapes=[pltpu.VMEM((2, n - 1, a // (2 * n), b), B16) for a, b in shapes]
-        + [pltpu.VMEM(item, B16) for item in shapes]
-        + [pltpu.VMEM((n,) + small.shape, F32)]
-        + [DMA((len(arrays), 2, steps))] * 2
-        + [DMA((n - 1,))] * 2,
-        compiler_params=pltpu.CompilerParams(
-            vmem_limit_bytes=56 * MIB, collective_id=collective_id, has_side_effects=True
-        ),
-        cost_estimate=pl.CostEstimate(
-            flops=size, bytes_accessed=400 * MIB, transcendentals=0
-        ),
-        name="ring_sum",
-    )(*arrays, small)
 
 
 def on_group(
@@ -1311,16 +1607,16 @@
             l,
             LAYERS,
             x,
-            up_weight[l],
+            up_weight,
+            down_weight,
+            qkv_weight,
+            out_weight,
+            tables,
             wide(up_bias[l])[None],
-            down_weight[l],
-            qkv_weight[l],
             wide(qkv_bias[l])[None],
-            out_weight[l],
             bias_sum[l][None],
             wide(norm_gain[l]),
             wide(norm_shift[l]),
-            tables,
             cotangent,
         )
         na, nb, u, hidden, qkv, ctx, lse, x_next = got[:8]
@@ -1334,39 +1630,42 @@
 
     grad = cotangent
     big = [None] * LAYERS
+    ready = ()
     small = [None] * LAYERS
     for l in reversed(range(LAYERS)):
         x, na, nb, u, hidden, qkv, ctx, lse, x_next = stored[l]
-        g, d_pre, d_qkv, grad, small[l] = backward_layer(
+        grad, small[l], *found = backward_layer(
             l,
             LAYERS,
             grad,
             u,
-            down_weight[l],
-            up_weight[l],
-            out_weight[l],
-            qkv_weight[l],
+            down_weight,
+            up_weight,
+            out_weight,
+            qkv_weight,
+            out_all,
+            tables,
             qkv,
             lse,
             ctx,
-            out_all[l],
-            wide(out_bias[l])[None],
             x_next,
             x,
             far_x,
             far_g,
             wide(norm_gain[l]),
-            tables,
+            wide(out_bias[l])[None],
+            hidden,
+            nb,
+            na,
+            ready,
         )
-        grads = (dot_tn(hidden, g), dot_tn(nb, d_pre), dot_tn(na, d_qkv), dot_tn(ctx, g))
-        grads = tuple(item.astype(B16) for item in grads)
-        if l > 0:
-            big[l] = [item.astype(F32) for item in lax.psum(grads, "dp")]
-        else:
-            *big[l], small = ring_sum(grads, jnp.concatenate(small), 2 * LAYERS)
+        ready = (*found[4:6], *found[2:4])
+        if l < LAYERS - 1:
+            big[l + 1] = found[6:]
+    *big[0], small = last_sums(ready[:2], ready[2:], jnp.concatenate(small), 2 * LAYERS)
     small = small.reshape(LAYERS, 16, features)
     down_all, up_all, qkv_all, out_w_all = (
-        jnp.stack([item[i] for item in big]) for i in range(4)
+        jnp.stack([item[i] for item in big]).astype(F32) for i in range(4)
     )
     layer_stats = jnp.sqrt(jnp.sum(small[:, 5:8], axis=2) / (rows * dp * tensor * features))
     bias_all = small[:, 4]

time: 697 us -> 581 us (0.83)
  Pallas kernels: 555 us -> 509 us
  matrix products: 45.1 us -> 0 us
  local copies, waits for them, and re-layouts: 40.8 us -> 22.8 us
    pallas_call x5, Pallas kernels: 555 us -> 509 us  [the longest x2 263 us: backward_layer(): pl.pallas_call(functools.partial(backward_layer_kernel, l, first, final,...]
    dot_general x8 -> x0, matrix products: 45.1 us -> none  [dot_tn(): lax.dot_general(left, right, (((0,), (0,)), ((), ())), preferred_element_...]
    another operation x8 -> x0, other arithmetic: 16.9 us -> none  [on_group(): jnp.stack([item[i] for item in big])]
    convert_element_type x0 -> x4, other arithmetic: none -> 13.5 us  [on_group(): jnp.stack([item[i] for item in big]).astype(F32)]
    squeeze x4 -> x0, local copies, waits for them, and re-layouts: 11.7 us -> none  [the longest x1 4.92 us: on_group(): down_weight[l]]
    unnamed x63 -> x39, local copies, waits for them, and re-layouts: 12.6 us -> 15.1 us
  transfers between devices with their start and end apart: 5 -> 4, of which waited for: 0 -> 0; matrix products, arithmetic and copies ran while one was open for 9% -> 3% of each run, Pallas kernels for 69% -> 25%
where the time goes in v2:
time: 581 us; the launch traced here: 571 us
  Pallas kernels  509 us (88%)
  local copies, waits for them, and re-layouts  22.8 us (4%)
  other arithmetic  21.2 us (4%)
  between operations  14.7 us (3%)
    pallas_call x2, Pallas kernels, backward_layer(): pl.pallas_call(functools.partial(backward_layer_kernel, l, first, final,...  263 us
    pallas_call x2, Pallas kernels, forward_layer(): pl.pallas_call(functools.partial(forward_layer_kernel, l, first, final, r...  144 us
    pallas_call x1, Pallas kernels, last_sums(): pl.pallas_call(functools.partial(last_sums_kernel, n), in_specs=[ANY] * 4...  102 us
    unnamed x39, local copies, waits for them, and re-layouts  15.1 us
    convert_element_type x4, other arithmetic, on_group(): jnp.stack([item[i] for item in big]).astype(F32)  13.5 us
  transfers between devices with their start and end apart: 4, of which 0 were waited for; matrix products, arithmetic and copies ran while one was open for 3% of the time, Pallas kernels for 25%

profile of v2, /device:TPU:0, one launch (start us, length us, event | category | flops | bytes accessed | tf_op | source)
XLA Modules:
  0.0 570.9 jit_solution(11477762972080684958)
XLA Ops:
  7.8 0.9 constant_dynamic-slice_fusion
  8.7 2.6 collective-permute-start.1
  11.5 0.7 convert_add_fusion
  12.2 0.6 fusion.3
  12.8 1.4 slice_convert_fusion.2
  14.1 1.3 bitcast_convert_fusion.3
  15.4 1.3 bitcast_convert_fusion
  17.1 1.0 copy.27.refs_7_.refs_9_
  18.2 1.0 copy.26.refs_6_.refs_8_
  19.2 1.0 copy.25.refs_5_.refs_7_
  20.8 0.7 copy-done.10
  21.5 85.6 %forward_layer.2 = (bf16[2048,1024]{1,0:T(8,128)(2,1)}, bf16[2048,1024]{1,0:T(8,128)(2,1)}, f32[2048,1024]{1,0:T(8,128)}, bf16[2048,1024]{1,0:T(8,128)(2,1)}, bf...) custom-call(bf16[512,1024]{1,0:T(8,128)(2,1)} %refs_14_.1, ...), custom_call_target="tpu_custom_call" | custom-call | flops 25769803776 | bytes 41943040 | tf_op jit(solution)/shard_map/forward_layer/pallas_call | solution.py:864
  107.3 58.0 %forward_layer.3 = (bf16[2048,1024]{1,0:T(8,128)(2,1)}, bf16[2048,1024]{1,0:T(8,128)(2,1)}, f32[2048,1024]{1,0:T(8,128)}, bf16[2048,1024]{1,0:T(8,128)(2,1)}, bf...) custom-call(f32[1024,1024]{1,0:T(8,128)} %get-tuple-element.52.refs_, ...), custom_call_target="tpu_custom_call" | custom-call | flops 25769803776 | bytes 41943040 | tf_op jit(solution)/shard_map/forward_layer/pallas_call | solution.py:864
  165.3 2.4 constant_dynamic-update-slice_fusion.3
  168.3 2.3 constant_dynamic-update-slice_fusion.2
  170.5 1.0 constant_dynamic-update-slice_fusion.1
  171.6 2.3 constant_dynamic-update-slice_fusion.refs_6_
  173.9 117.9 %backward_layer.2 = (f32[512,1024]{1,0:T(8,128)}, f32[16,1024]{1,0:T(8,128)}, bf16[1024,1024]{1,0:T(8,128)(2,1)}, bf16[1024,1024]{1,0:T(8,128)(2,1)}, bf16[1024,...) custom-call(bf16[512,1024]{1,0:T(8,128)(2,1)} %refs_0_.3, ...), custom_call_target="tpu_custom_call" | custom-call | flops 25769803776 | bytes 41943040 | tf_op jit(solution)/shard_map/backward_layer/pallas_call | solution.py:1553
  291.7 145.0 %backward_layer.3 = (f32[512,1024]{1,0:T(8,128)}, f32[16,1024]{1,0:T(8,128)}, bf16[1024,1024]{1,0:T(8,128)(2,1)}, bf16[1024,1024]{1,0:T(8,128)(2,1)}, bf16[1024,...) custom-call(f32[512,1024]{1,0:T(8,128)} %get-tuple-element.62.refs_0, ...), custom_call_target="tpu_custom_call" | custom-call | flops 25769803776 | bytes 41943040 | tf_op jit(solution)/shard_map/backward_layer/pallas_call | solution.py:1553
  436.7 0.9 pad_maximum_fusion.refs_4_
  437.6 1.4 copy-done
  439.0 1.0 copy-done.1
  440.0 0.9 copy-done.2
  441.0 0.9 copy-done.3
  441.9 102.4 %last_sums.1 = (bf16[1024,1024]{1,0:T(8,128)(2,1)S(1)}, bf16[1024,1024]{1,0:T(8,128)(2,1)S(1)}, bf16[1024,768]{1,0:T(8,128)(2,1)S(1)}, bf16[256,1024]{1,0:T(8,128)(2,1)S(1)}, f32[32,1024]{1,0:T(8,128)S(1)}) custom-call(bf16[128,1024]{1,0:T(8,128)(2,1)S(1)} %copy-done.2, bf16[128,1024]{1,0:T(8,128)(2,1)S(1)} %copy-done.3, bf16[1024,768]{1,0:T(8,128)(2,1)S(1)} %copy-done, ...), custom_call_target="tpu_custom_call" | custom-call | flops 3145728 | bytes 419430400 | tf_op jit(solution)/shard_map/last_sums/pallas_call | solution.py:1109
  544.5 0.6 fusion.1
  546.9 2.5 maximum_convert_fusion.3
  549.4 3.1 maximum_convert_fusion.2
  552.5 3.9 maximum_convert_fusion
  556.5 3.9 maximum_convert_fusion.1
  561.0 1.3 copy.53
  562.3 1.3 copy.54
  (55 shorter events, 5.0 us)
Async XLA Ops:
  7.2 13.1 %copy-start.14 = (bf16[2,768]{1,0:T(2,128)(2,1)S(1)}, bf16[2,768]{1,0:T(2,128)(2,1)}, u32[]{:S(2)}) copy-start(bf16[2,768]{1,0:T(2,128)(2,1)} %param.15) | copy-start | bytes 9220
  7.2 100.0 %all-gather.2.cloned.1.call-start = ((), (), s32[]{:S(2)}) async-start(), calls=%async_computation | async-start | bytes 1179648 | tf_op jit(solution)/shard_map/all_gather | solution.py:1597
  7.2 161.0 %collective-permute-start = (bf16[2,256,1024]{2,1,0:T(8,128)(2,1)}, bf16[2,256,1024]{2,1,0:T(8,128)(2,1)}, u32[]{:S(2)}, u32[]{:S(2)}) collective-permute-start(bf16[2,256,1024]{2,1,0:T(8,128)(2,1)} %refs_4_.7), channel_id=1, source_target_pairs={{0,1},{1,0},{2,3},{3,2},{4,5},{5,4},{6,7},{7,6},{8,9},{9,8},{10,11... | collective-permute-start | bytes 3145736 | tf_op jit(solution)/shard_map/ppermute | solution.py:276
  8.7 12.2 %collective-permute-start.1 = (bf16[2,32,1024]{2,1,0:T(8,128)(2,1)S(1)}, bf16[2,32,1024]{2,1,0:T(8,128)(2,1)S(1)}, u32[]{:S(2)}, u32[]{:S(2)}) collective-permute-start(bf16[2,32,1024]{2,1,0:T(8,128)(2,1)S(1)} %constant_dynamic-slice_fusion), channel_id=1, source_target_pairs={{0,2},{1,3},{2,0},{3,1},{4,6},{5,7},{6,4},{7,5},{8,10},{9,11},{10,... | collective-permute-start | bytes 393224 | tf_op jit(solution)/shard_map/ppermute | solution.py:276
  20.8 0.7 copy-start.10
  107.2 64.4 %collective-permute-start.2 = (bf16[2,256,1024]{2,1,0:T(8,128)(2,1)}, bf16[2,256,1024]{2,1,0:T(8,128)(2,1)}, u32[]{:S(2)}, u32[]{:S(2)}) collective-permute-start(bf16[2,256,1024]{2,1,0:T(8,128)(2,1)} %all-gather.2.cloned.1.call-done), channel_id=1, source_target_pairs={{0,1},{1,0},{2,3},{3,2},{4,5},{5,4},{6,7},{7,6},{8,9},{9,8},{10,11... | collective-permute-start | bytes 3145736 | tf_op jit(solution)/shard_map/ppermute | solution.py:276
  107.3 60.4 %copy-start.12 = (bf16[2,1024]{1,0:T(2,128)(2,1)S(1)}, bf16[2,1024]{1,0:T(2,128)(2,1)}, u32[]{:S(2)}) copy-start(bf16[2,1024]{1,0:T(2,128)(2,1)} %param.17) | copy-start | bytes 12292
  165.3 5.2 copy-start.9
  291.7 145.0 %copy-start.11 = (f32[16,1024]{1,0:T(8,128)S(1)}, f32[16,1024]{1,0:T(8,128)}, u32[]{:S(2)}) copy-start(f32[16,1024]{1,0:T(8,128)} %get-tuple-element.81) | copy-start | bytes 196612
  437.6 1.4 copy-start
  439.0 1.0 copy-start.1
  440.0 0.9 copy-start.2
  441.0 0.9 copy-start.3
  441.9 107.5 %copy-start.8 = (bf16[1024,768]{1,0:T(8,128)(2,1)S(1)}, bf16[1024,768]{1,0:T(8,128)(2,1)}, u32[]{:S(2)}) copy-start(bf16[1024,768]{1,0:T(8,128)(2,1)} %get-tuple-element.83) | copy-start | bytes 4718596
  546.9 13.5 %copy-start.13 = (f32[2,1,1024]{2,0,1:T(2,128)}, f32[2,1,1024]{2,0,1:T(2,128)S(1)}, u32[]{:S(2)}) copy-start(f32[2,1,1024]{2,0,1:T(2,128)S(1)} %copy.44) | copy-start | bytes 24580
  549.4 3.1 copy-start.7
  552.5 3.9 copy-start.6
  556.4 4.5 copy-start.4
  560.4 1.9 copy-start.5
Sparse Core Ops, SparseCore 0:
  21.6 40.3 all-gather.1

commit v3 on v2

--- a/solution.py
+++ b/solution.py
@@ -3,6 +3,7 @@
 
 import jax
 import jax.numpy as jnp
+import numpy as np
 from jax import lax
 from jax.experimental import pallas as pl
 from jax.experimental.pallas import tpu as pltpu
@@ -35,13 +36,15 @@
 
 
 def rope_tables(seq, width):
-    positions = jnp.arange(seq, dtype=jnp.int32).astype(F32)
-    inverse = jnp.exp(jnp.arange(ROT // 2, dtype=F32) * (-2.0 * math.log(10000.0) / ROT))
-    angles = positions[:, None] * inverse[None, :]
-    cosine, sine = jnp.cos(angles), jnp.sin(angles)
-    zero = jnp.zeros_like(sine)
-    rest = jnp.zeros((seq, HEAD - ROT), F32)
-    repeat = lambda parts: jnp.tile(jnp.concatenate(parts, axis=1), (1, width // HEAD))
+    positions = np.arange(seq, dtype=np.float32)
+    inverse = np.exp(np.arange(ROT // 2, dtype=np.float32) * (-2.0 * math.log(10000.0) / ROT))
+    angles = (positions[:, None] * inverse.astype(np.float32)[None, :]).astype(np.float64)
+    cosine, sine = np.cos(angles), np.sin(angles)
+    zero = np.zeros_like(sine)
+    rest = np.zeros((seq, HEAD - ROT))
+    repeat = lambda parts: jnp.asarray(
+        np.tile(np.concatenate(parts, axis=1), (1, width // HEAD)).astype(np.float32)
+    )
     return (
         repeat([cosine, cosine, rest + 1.0]),
         repeat([-sine, zero, rest]),
@@ -598,7 +601,7 @@
 def forward_layer_kernel(l, first, final, rows, w, *refs):
     it = iter(refs)
     x_ref, up_h, down_h, qkvw_h, out_h, cos_h, lo_h, hi_h = (next(it) for _ in range(8))
-    upb_ref, qkvb_ref, ob_ref, gain_ref, shift_ref = (next(it) for _ in range(5))
+    upb_h, qkvb_h, ob_h, db_h, gain_h, shift_h = (next(it) for _ in range(6))
     cot_ref = next(it) if final else None
     na_o, nb_o, u_o, hid_o, qkv_o, ctx_o, lse_o, x_o = (next(it) for _ in range(8))
     far_o = next(it) if first or final else None
@@ -607,6 +610,7 @@
     far_s = next(it) if first or final else None
     mine_s = next(it)
     up_ref, down_ref, qkvw_ref, out_ref, cos_ref, lo_ref, hi_ref = (next(it) for _ in range(7))
+    upb_ref, qkvb_ref, ob_ref, gain_ref, shift_ref = (next(it) for _ in range(5))
     send, recv, local, u_sem, load_sem = (next(it) for _ in range(5))
     sems = (send, recv)
     need = loader(
@@ -626,6 +630,11 @@
     half_blocks = rows // QB
     shift = lax.rem(lax.axis_index("tensor"), 2) * half_blocks
     core, far = partners()
+    upb_ref[...] = upb_h[l : l + 1, :].astype(F32)
+    qkvb_ref[...] = qkvb_h[l : l + 1, :].astype(F32)
+    ob_ref[...] = ob_h[l : l + 1, :].astype(F32) + db_h[l : l + 1, :].astype(F32)
+    gain_ref[...] = gain_h[l].astype(F32)
+    shift_ref[...] = shift_h[l].astype(F32)
     greet((core, far))
     outs = []
 
@@ -819,7 +828,9 @@
         copy.wait_send()
 
 
-def forward_layer(l, layers, x, up, down, qkvw, out, tables, upb, qkvb, ob, gains, shifts, cot):
+def forward_layer(
+    l, layers, x, up, down, qkvw, out, tables, upb, qkvb, ob, db, gains, shifts, cot
+):
     first, final = l == 0, l == layers - 1
     features = x.shape[1]
     rows = x.shape[0] if first else x.shape[0] // 2
@@ -839,7 +850,7 @@
     ]
     if first or final:
         out_shape.append(shape((rows, features), B16))
-    args = [x, up, down, qkvw, out, *tables, upb, qkvb, ob, gains, shifts]
+    args = [x, up, down, qkvw, out, *tables, upb, qkvb, ob, db, gains, shifts]
     if final:
         args.append(cot)
     scratch = [
@@ -860,6 +871,8 @@
     scratch.append(pltpu.VMEM((rows, features), F32))
     scratch += [pltpu.VMEM(item.shape[1:], B16) for item in (up, down, qkvw, out)]
     scratch += [pltpu.VMEM(item.shape, F32) for item in tables]
+    scratch += [pltpu.VMEM((1, width), F32) for width in (ff, 3 * w, features)]
+    scratch += [pltpu.VMEM((2, features), F32)] * 2
     scratch += [DMA((9,)), DMA((9,)), DMA((15,)), DMA((rows // QB,)), DMA((7,))]
     return pl.pallas_call(
         functools.partial(forward_layer_kernel, l, first, final, rows, w),
@@ -898,18 +911,17 @@
             ring_device(lax.rem(self.place + 1, n), n),
             ring_device(lax.rem(self.place + n - 1, n), n),
         )
-        far = n // 2
-        self.routes = ((0, 0, far), (0, 1, n - 1 - far), (1, 0, n - 1 - far), (1, 1, far))
+        self.steps = n // 2
 
     def greet(self):
         barrier = pltpu.get_barrier_semaphore()
         for other in self.targets:
             pl.semaphore_signal(barrier, inc=1, device_id={"dp": other}, device_id_type=MESH)
 
-    def rows(self, array, half, offset):
-        size = array.shape[0] // (2 * self.n)
+    def rows(self, array, offset):
+        size = array.shape[0] // self.n
         chunk = lax.rem(self.place + offset + 2 * self.n, self.n)
-        return pl.ds(pl.multiple_of((chunk * 2 + half) * size, size), size)
+        return pl.ds(pl.multiple_of(chunk * size, size), size)
 
     def copy(self, src, dst, sems, at, way):
         return pltpu.make_async_remote_copy(
@@ -923,238 +935,248 @@
 
 
 class Scatter:
-    def __init__(self, ring, ins, chunk, it):
-        self.ring, self.ins, self.chunk = ring, ins, chunk
+    def __init__(self, ring, ins, turns, chunk, it):
+        self.ring, self.ins, self.turns, self.chunk = ring, ins, turns, chunk
         self.slots = [next(it) for _ in ins]
         self.mine = [next(it) for _ in ins]
         self.sems = (next(it), next(it))
         self.load = next(it)
-        self.parts = [(a, m) for a in range(len(ins)) for m in range(4)]
+        self.parts = [(a, way) for a in range(len(ins)) for way in (0, 1)]
 
     @staticmethod
-    def scratch(n, shapes):
+    def scratch(n, shapes, dtypes=None):
         count = len(shapes)
-        size = lambda a: a // (2 * n)
+        kinds = [(a, b, B16) for a, b in shapes]
+        if dtypes:
+            kinds = [(a, b, dtype) for (a, b), dtype in zip(shapes, dtypes)]
         return (
-            [pltpu.VMEM((4, n // 2, size(a), b), B16) for a, b in shapes]
-            + [pltpu.VMEM((4, size(a), b), B16) for a, b in shapes]
-            + [DMA((count, 4, n // 2)), DMA((count, 4, n // 2)), DMA((count, 4))]
+            [pltpu.VMEM((2, n // 2, a // n, b), dtype) for a, b, dtype in kinds]
+            + [pltpu.VMEM((2, a // n, b), dtype) for a, b, dtype in kinds]
+            + [DMA((count, 2, n // 2)), DMA((count, 2, n // 2)), DMA((count, 2))]
         )
 
-    def sent(self, a, m, step):
-        half, way, steps = self.ring.routes[m]
-        offset = steps - step
+    def steps(self, a, way):
+        return self.ring.steps - (way ^ self.turns[a])
+
+    def rows(self, a, way, offset):
+        return self.ring.rows(self.ins[a], -offset if way else offset)
+
+    def sent(self, a, way, step):
         if step:
-            src = self.slots[a].at[m, step - 1]
+            src = self.slots[a].at[way, step - 1]
         else:
-            src = self.ins[a].at[self.ring.rows(self.ins[a], half, -offset if way else offset), :]
-        return self.ring.copy(src, self.slots[a].at[m, step], self.sems, (a, m, step), way)
-
-    def fetch(self, a, m, step):
-        half, way, steps = self.ring.routes[m]
-        offset = steps - step - 1
+            src = self.ins[a].at[self.rows(a, way, self.steps(a, way)), :]
+        return self.ring.copy(src, self.slots[a].at[way, step], self.sems, (a, way, step), way)
+
+    def fetch(self, a, way, step):
+        at = self.rows(a, way, self.steps(a, way) - step - 1)
         return pltpu.make_async_copy(
-            self.ins[a].at[self.ring.rows(self.ins[a], half, -offset if way else offset), :],
-            self.mine[a].at[m],
-            self.load.at[a, m],
+            self.ins[a].at[at, :], self.mine[a].at[way], self.load.at[a, way]
         )
 
     def start(self):
-        for a, m in self.parts:
-            self.sent(a, m, 0).start()
-        for a, m in self.parts:
-            self.fetch(a, m, 0).start()
+        for part in self.parts:
+            self.sent(*part, 0).start()
+        for part in self.parts:
+            self.fetch(*part, 0).start()
 
     def step(self, step):
-        for a, m in self.parts:
-            half, way, steps = self.ring.routes[m]
+        for a, way in self.parts:
+            steps = self.steps(a, way)
             if step >= steps:
                 continue
-            self.sent(a, m, step).wait_recv()
+            self.sent(a, way, step).wait_recv()
             if step + 1 < steps:
-                self.fetch(a, m, step).wait()
-                total = self.slots[a][m, step].astype(F32) + self.mine[a][m].astype(F32)
-                self.slots[a][m, step] = total.astype(B16)
-                self.sent(a, m, step + 1).start()
+                self.fetch(a, way, step).wait()
+                total = self.slots[a][way, step].astype(F32) + self.mine[a][way].astype(F32)
+                self.slots[a][way, step] = total.astype(self.slots[a].dtype)
+                self.sent(a, way, step + 1).start()
                 if way == 0 or step + 2 < steps:
-                    self.fetch(a, m, step + 1).start()
-        if step == self.ring.n // 2 - 1:
+                    self.fetch(a, way, step + 1).start()
+        if step == self.ring.steps - 1:
             for a in range(len(self.ins)):
-                for half in (0, 1):
-                    m, other = 2 * half, 2 * half + 1
-                    self.fetch(a, m, self.ring.routes[m][2] - 1).wait()
-                    total = self.mine[a][m].astype(F32)
-                    for route in (m, other):
-                        last = self.ring.routes[route][2] - 1
-                        total = total + self.slots[a][route, last].astype(F32)
-                    size = total.shape[0]
-                    self.chunk[a][half * size : (half + 1) * size, :] = total.astype(B16)
+                self.fetch(a, 0, self.steps(a, 0) - 1).wait()
+                total = self.mine[a][0].astype(F32)
+                for way in (0, 1):
+                    total = total + self.slots[a][way, self.steps(a, way) - 1].astype(F32)
+                self.chunk[a][...] = total.astype(self.chunk[a].dtype)
 
     def finish(self):
-        for a, m in self.parts:
-            for step in range(self.ring.routes[m][2]):
-                self.sent(a, m, step).wait_send()
+        for part in self.parts:
+            for step in range(self.steps(*part)):
+                self.sent(*part, step).wait_send()
 
 
 class Gather:
-    def __init__(self, ring, chunk, done, it):
-        self.ring, self.chunk, self.done = ring, chunk, done
+    def __init__(self, ring, chunk, turns, done, it):
+        self.ring, self.chunk, self.turns, self.done = ring, chunk, turns, done
         self.sems = (next(it), next(it))
         self.local = next(it)
-        self.parts = [(a, m) for a in range(len(chunk)) for m in range(4)]
+        self.parts = [(a, way) for a in range(len(chunk)) for way in (0, 1)]
 
     @staticmethod
     def scratch(n, count):
-        return [DMA((count, 4, n // 2)), DMA((count, 4, n // 2)), DMA((count, 2))]
-
-    def sent(self, a, m, step):
-        half, way, steps = self.ring.routes[m]
-        at = self.ring.rows(self.done[a], half, step if way else -step)
-        size = self.done[a].shape[0] // (2 * self.ring.n)
-        src = self.done[a].at[at, :] if step else self.chunk[a].at[pl.ds(half * size, size), :]
-        return self.ring.copy(src, self.done[a].at[at, :], self.sems, (a, m, step), way)
-
-    def own(self, a, half):
-        size = self.done[a].shape[0] // (2 * self.ring.n)
-        return pltpu.make_async_copy(
-            self.chunk[a].at[pl.ds(half * size, size), :],
-            self.done[a].at[self.ring.rows(self.done[a], half, 0), :],
-            self.local.at[a, half],
-        )
+        return [DMA((count, 2, n // 2)), DMA((count, 2, n // 2)), DMA((count,))]
+
+    steps = Scatter.steps
+
+    def sent(self, a, way, step):
+        at = self.ring.rows(self.done[a], step if way else -step)
+        src = self.done[a].at[at, :] if step else self.chunk[a]
+        return self.ring.copy(src, self.done[a].at[at, :], self.sems, (a, way, step), way)
+
+    def own(self, a):
+        at = self.ring.rows(self.done[a], 0)
+        return pltpu.make_async_copy(self.chunk[a], self.done[a].at[at, :], self.local.at[a])
 
     def start(self):
-        for a, m in self.parts:
-            self.sent(a, m, 0).start()
+        for part in self.parts:
+            self.sent(*part, 0).start()
         for a in range(len(self.chunk)):
-            for half in (0, 1):
-                self.own(a, half).start()
+            self.own(a).start()
 
     def step(self, step):
-        for a, m in self.parts:
-            steps = self.ring.routes[m][2]
+        for a, way in self.parts:
+            steps = self.steps(a, way)
             if step < steps:
-                self.sent(a, m, step).wait_recv()
+                self.sent(a, way, step).wait_recv()
                 if step + 1 < steps:
-                    self.sent(a, m, step + 1).start()
+                    self.sent(a, way, step + 1).start()
 
     def finish(self):
-        for a, m in self.parts:
-            for step in range(self.ring.routes[m][2]):
-                self.sent(a, m, step).wait_send()
+        for part in self.parts:
+            for step in range(self.steps(*part)):
+                self.sent(*part, step).wait_send()
         for a in range(len(self.chunk)):
-            for half in (0, 1):
-                self.own(a, half).wait()
-
-
-def last_sums_kernel(n, *refs):
+            self.own(a).wait()
+
+
+class Total:
+    def __init__(self, scatter, gather):
+        self.phases = [item for item in (scatter, gather) if item is not None]
+        self.steps = self.phases[0].ring.steps
+        self.at = 0
+
+    def start(self):
+        self.phases[0].start()
+
+    def step(self):
+        which, step = divmod(self.at, self.steps)
+        self.phases[which].step(step)
+        self.at += 1
+        if step == self.steps - 1 and which + 1 < len(self.phases):
+            self.phases[which + 1].start()
+
+    def finish(self):
+        while self.at < len(self.phases) * self.steps:
+            self.step()
+        for item in self.phases:
+            item.finish()
+
+
+def halves(ref):
+    width = ref.shape[1] // 2
+    return [ref.at[:, pl.ds(0, width)], ref.at[:, pl.ds(width, width)]]
+
+
+def half_shapes(shape):
+    return [(shape[0], shape[1] // 2)] * 2
+
+
+def chunk_scratch(n, shapes):
+    return [pltpu.VMEM((a // n, b), B16) for a, b in shapes]
+
+
+def last_sums_kernel(n, count, *refs):
     it = iter(refs)
-    ready = [next(it) for _ in range(2)]
-    ins = [next(it) for _ in range(2)]
+    ins = [item for _ in range(count) for item in halves(next(it))]
     small_in = next(it)
-    done = [next(it) for _ in range(4)]
+    done = [item for _ in range(count) for item in halves(next(it))]
     small_out = next(it)
+    small_s, small_d = next(it), next(it)
     ring = Ring(n)
-    chunk = [next(it) for _ in range(2)]
-    first = Gather(ring, ready, done[:2], it)
-    sums = Scatter(ring, ins, chunk, it)
-    second = Gather(ring, chunk, done[2:], it)
-    small_s, small_send, small_recv = (next(it) for _ in range(3))
+    turns = (0, 1) * count + (0,)
+    ins.append(small_s)
+    done.append(small_d)
+    chunk = [next(it) for _ in ins]
+    total = Total(Scatter(ring, ins, turns, chunk, it), Gather(ring, chunk, turns, done, it))
     ring.greet()
+    rows, width = small_in.shape[0], small_in.shape[1] // 2
+    small_s[:rows, :] = small_in[:, :width]
+    small_s[rows:, :] = small_in[:, width:]
     pl.semaphore_wait(pltpu.get_barrier_semaphore(), 2)
-
-    def small_copy(step):
-        at = lax.rem(ring.place + n - step, n)
-        return pltpu.make_async_remote_copy(
-            src_ref=small_s.at[at],
-            dst_ref=small_s.at[at],
-            send_sem=small_send.at[step],
-            recv_sem=small_recv.at[step],
-            device_id={"dp": ring.targets[0]},
-            device_id_type=MESH,
-        )
-
-    small_s[ring.place] = small_in[...]
-    sums.start()
-    small_copy(0).start()
-    first.start()
-    for step in range(n // 2):
-        sums.step(step)
-        if step == n // 2 - 1:
-            second.start()
-        first.step(step)
-        small_copy(step).wait_recv()
-        small_copy(step + 1).start()
-    for step in range(n // 2):
-        second.step(step)
-        if n // 2 + step < n - 1:
-            small_copy(n // 2 + step).wait_recv()
-            if n // 2 + step < n - 2:
-                small_copy(n // 2 + step + 1).start()
-    total = small_s[0]
-    for i in range(1, n):
-        total = total + small_s[i]
-    small_out[...] = total
-    for part in (first, sums, second):
-        part.finish()
-    for step in range(n - 1):
-        small_copy(step).wait_send()
-
-
-def last_sums(ready, arrays, small, collective_id):
+    total.start()
+    total.finish()
+    small_out[:, :width] = small_d[:rows, :]
+    small_out[:, width:] = small_d[rows:, :]
+
+
+def last_sums(arrays, small, collective_id):
     n = lax.axis_size("dp")
     shape = jax.ShapeDtypeStruct
-    shapes = [item.shape for item in arrays]
-    full = [(item.shape[0] * n, item.shape[1]) for item in ready] + shapes
-    size = sum(a * b for a, b in full)
+    count = len(arrays)
+    folded = (2 * small.shape[0], small.shape[1] // 2)
+    shapes = [half for item in arrays for half in half_shapes(item.shape)] + [folded]
+    dtypes = [B16] * (2 * count) + [F32]
     return pl.pallas_call(
-        functools.partial(last_sums_kernel, n),
-        in_specs=[ANY] * 4 + [VMEM],
-        out_specs=[ANY] * 4 + [VMEM],
-        out_shape=[shape(item, B16) for item in full] + [shape(small.shape, F32)],
-        scratch_shapes=[pltpu.VMEM((a // n, b), B16) for a, b in shapes]
-        + Gather.scratch(n, 2)
-        + Scatter.scratch(n, shapes)
-        + Gather.scratch(n, 2)
-        + [pltpu.VMEM((n,) + small.shape, F32)]
-        + [DMA((n - 1,))] * 2,
+        functools.partial(last_sums_kernel, n, count),
+        in_specs=[ANY] * count + [VMEM],
+        out_specs=[ANY] * count + [VMEM],
+        out_shape=[shape(item.shape, B16) for item in arrays] + [shape(small.shape, F32)],
+        scratch_shapes=[pltpu.VMEM(folded, F32)] * 2
+        + [pltpu.VMEM((a // n, b), dtype) for (a, b), dtype in zip(shapes, dtypes)]
+        + Scatter.scratch(n, shapes, dtypes)
+        + Gather.scratch(n, len(shapes)),
         compiler_params=pltpu.CompilerParams(
             vmem_limit_bytes=40 * MIB, collective_id=collective_id, has_side_effects=True
         ),
-        cost_estimate=pl.CostEstimate(flops=size, bytes_accessed=400 * MIB, transcendentals=0),
+        cost_estimate=pl.CostEstimate(
+            flops=arrays[0].size, bytes_accessed=200 * MIB, transcendentals=0
+        ),
         name="last_sums",
-    )(*ready, *arrays, small)
+    )(*arrays, small)
 
 
 def backward_layer_kernel(l, first, final, rows, w, n, *refs):
     it = iter(refs)
     grad_ref, u_ref, down_h, up_h, ow_h, qkvw_h = (next(it) for _ in range(6))
-    outall_h, cos_h, lo_h, hi_h = (next(it) for _ in range(4))
+    cos_h, lo_h, hi_h = (next(it) for _ in range(3))
     qkv_h, lse_h, ctx_ref, xn_h, x_ref = (next(it) for _ in range(5))
     far_ref = next(it) if first else None
     farg_ref = next(it) if final else None
-    gain_ref, ob_ref = (next(it) for _ in range(2))
+    gain_h, ob_h = (next(it) for _ in range(2))
     hid_h, nb_h, na_h = (next(it) for _ in range(3))
-    ready = [next(it) for _ in range(4)] if first else []
+    chunk_in, ready = (next(it), next(it)) if first else (None, None)
     dx_o, small_ref = (next(it) for _ in range(2))
-    wide_g = [next(it) for _ in range(2)]
-    narrow_g = [next(it) for _ in range(2)]
-    chunk_ref = [next(it) for _ in range(2)]
-    done = [next(it) for _ in range(4)] if first else []
+    down_g, out_g, up_g, qkv_g, down_done, out_done = (next(it) for _ in range(6))
+    up_chunk = None if first else next(it)
+    up_done, ready_done = (next(it), next(it)) if first else (None, None)
     g_s, dpre_s, dqkv_s, dq_s, dk_s, dv_s, dctx_s = (next(it) for _ in range(7))
     u_s, osend, brecv, arecv, ysend, yrecv = (next(it) for _ in range(6))
     cfull, got_s = (next(it) for _ in range(2))
     down_ref, up_ref, ow_ref, qkvw_ref, outall_ref = (next(it) for _ in range(5))
     cos_ref, lo_ref, hi_ref, qkv_ref, lse_ref = (next(it) for _ in range(5))
+    gain_ref, ob_ref = (next(it) for _ in range(2))
     send, recv, local, u_sem, load_sem = (next(it) for _ in range(5))
     sems = (send, recv)
     a_s, o_s, a_sem, o_sem = (next(it) for _ in range(4))
     ring = Ring(n)
-    wide_sum = Scatter(ring, wide_g, chunk_ref, it)
-    if first:
-        chunk_s = [next(it) for _ in range(2)]
-        wide_last = Gather(ring, ready[:2], done[:2], it)
-        narrow_sum = Scatter(ring, ready[2:], chunk_s, it)
-        narrow_last = Gather(ring, chunk_s, done[2:], it)
+    sums = {}
+    turns = (0, 1, 0)
+    chunk = [next(it) for _ in range(3)]
+    sums["a"] = Total(
+        Scatter(ring, halves(down_g) + [out_g], turns, chunk, it),
+        Gather(ring, chunk, turns, halves(down_done) + [out_done], it),
+    )
+    if not first:
+        sums["b"] = Total(Scatter(ring, halves(up_g), turns, halves(up_chunk), it), None)
+    else:
+        chunk = [next(it) for _ in range(2)]
+        sums["c"] = Total(
+            Scatter(ring, halves(ready), turns, chunk, it),
+            Gather(ring, chunk, turns, halves(ready_done), it),
+        )
+        sums["d"] = Total(None, Gather(ring, halves(chunk_in), turns, halves(up_done), it))
     need = loader(
         load_sem,
         down=(down_h.at[l], down_ref),
@@ -1166,7 +1188,6 @@
         lo=(lo_h, lo_ref),
         hi=(hi_h, hi_ref),
         qkvw=(qkvw_h.at[l], qkvw_ref),
-        outall=(outall_h.at[l], outall_ref),
     )
 
     seq = 2 * rows
@@ -1186,6 +1207,8 @@
         )
 
     small_ref[...] = jnp.zeros_like(small_ref)
+    gain_ref[...] = gain_h[l].astype(F32)
+    ob_ref[...] = ob_h[l : l + 1, :].astype(F32)
     load_u(0, 0).start()
     load_u(0, 1).start()
 
@@ -1205,18 +1228,25 @@
     near0 = remote(own_half(g_s, 0), other_half(g_s, 0), sems, 1, core)
     near0.start()
     if first:
-        wide_last.start()
-        narrow_sum.start()
+        sums["c"].start()
+        sums["d"].start()
     cfull[:, :w] = ctx_ref[:rows, :]
     contexts = [
         remote(ctx_ref.at[pl.ds(rows, rows), :], cfull.at[:, pl.ds(w, w)], sems, 8, core),
         remote(ctx_ref.at[pl.ds(seq, rows), :], cfull.at[:, pl.ds(2 * w, w)], sems, 9, far),
         remote(ctx_ref.at[pl.ds(seq + rows, rows), :], cfull.at[:, pl.ds(3 * w, w)], sems, 10, diag),
     ]
+    need("ow")
+    outall_ref[:w, :] = ow_ref[...]
+    for i, other in enumerate((core, far, diag)):
+        contexts.append(
+            remote(ow_ref, outall_ref.at[pl.ds((i + 1) * w, w), :], sems, 13 + i, other)
+        )
     for copy in contexts:
         copy.start()
 
     swaps = {}
+    latest = []
 
     def feed(k):
         need("down")
@@ -1231,10 +1261,12 @@
                 load_u(k, i + 2).start()
             elif k == 0:
                 load_u(1, i + 2 - blocks).start()
+            if 2 * (i + 1) == blocks:
+                pump("feed%d half" % k)
 
         need("up")
-        if k == 1:
-            swaps[0][0].wait_send()
+        if latest:
+            latest.pop().wait_send()
 
         @pl.loop(0, half_blocks)
         def _(r):
@@ -1242,6 +1274,7 @@
 
         swaps[k] = [remote(osend, brecv.at[k], sems, 3 + 2 * k, core)]
         swaps[k][0].start()
+        latest.append(swaps[k][0])
 
     def attend(k, pump):
         need("ow", "qkv", "lse", "cos", "lo", "hi", "qkvw")
@@ -1289,7 +1322,7 @@
             dqkv_s[k, swapped(r), :] = low
             small_ref[9:10, : 3 * w] += jnp.sum(low.astype(F32), axis=0, keepdims=True)
 
-        swaps[1][1 - k].wait_send()
+        latest.pop().wait_send()
 
         @pl.loop(0, half_blocks)
         def _(r):
@@ -1297,6 +1330,7 @@
 
         swaps[k].append(remote(osend, arecv.at[k], sems, 4 + 2 * k, core))
         swaps[k][1].start()
+        latest.append(swaps[k][1])
 
     def x_rows(k, r):
         if not first:
@@ -1359,75 +1393,90 @@
         for i in range(max(tiles - 2, 0), tiles):
             store(i).wait()
 
-    def at_heads(**calls):
-        def pump(h):
-            for name, todo in calls.items():
-
-                @pl.when(h == int(name[1:]))
-                def _():
-                    todo()
-
-        return pump
+    if first:
+        plan = {
+            "feed0": "cd",
+            "attend0 2": "cd",
+            "near": "cd",
+            "hid": "cd",
+            "feed1 half": "c",
+            "feed1": "ca",
+            "nb": "a",
+            "attend1 0": "c",
+            "attend1 1": "a",
+            "attend1 2": "c",
+            "attend1 3": "a",
+            "fold1": "a",
+            "na": "a",
+            "stats": "a",
+        }
+    else:
+        plan = {
+            "feed0": "a",
+            "feed1 half": "a",
+            "feed1": "a",
+            "nb": "a",
+            "attend1 3": "ab",
+            "attend0 1": "ab",
+            "fold0": "ab",
+            "stats": "ab",
+        }
+
+    def pump(point):
+        for name in plan.get(point, ""):
+            sums[name].step()
+
+    def at_heads(k):
+        def at_head(h):
+            for i in range(heads):
+                if "attend%d %d" % (k, i) in plan:
+
+                    @pl.when(h == i)
+                    def _():
+                        pump("attend%d %d" % (k, i))
+
+        return at_head
+
+    def early_grads():
+        weight_grad(hid_h, g_s, down_g)
+        pump("hid")
+        weight_grad(ctx_ref, g_s, out_g)
+        sums["a"].start()
+        pump("ctx")
 
     near0.wait()
-    feed(0)
     if first:
-        narrow_sum.step(0)
+        feed(0)
+        pump("feed0")
+        attend(0, at_heads(0))
         across.wait()
     near1 = remote(own_half(g_s, 1), other_half(g_s, 1), sems, 2, core)
     near1.start()
-    if first:
-        wide_last.step(0)
+    pump("near")
     near1.wait()
+    early_grads()
+    if not first:
+        feed(0)
+        pump("feed0")
     feed(1)
-    if first:
-        narrow_sum.step(1)
-    weight_grad(hid_h, g_s, wide_g[0])
-    if first:
-        wide_last.step(1)
-    weight_grad(nb_h, dpre_s, wide_g[1])
-    wide_sum.start()
-    if first:
-        narrow_sum.step(2)
-
-        def later():
-            wide_last.step(2)
-            narrow_sum.step(3)
-            narrow_last.start()
-
-        attend(1, at_heads(h2=later))
-    else:
-        attend(1, at_heads(h2=lambda: wide_sum.step(0)))
+    pump("feed1")
+    weight_grad(nb_h, dpre_s, up_g)
+    if not first:
+        sums["b"].start()
+    pump("nb")
+    attend(1, at_heads(1))
     fold(1)
     back = remote(ysend, yrecv, sems, 7, far)
     back.start()
     next_rows = pltpu.make_async_copy(xn_h.at[pl.ds(0, rows), :], arecv.at[1], local.at[0])
     next_rows.start()
-    if first:
-        wide_sum.step(0)
-
-        def later():
-            wide_last.step(3)
-            narrow_last.step(0)
-            wide_sum.step(1)
-
-        attend(0, at_heads(h2=later))
-        narrow_last.step(1)
-    else:
-        wide_sum.step(1)
-        attend(0, at_heads(h2=lambda: wide_sum.step(2)))
+    pump("fold1")
+    if not first:
+        attend(0, at_heads(0))
     fold(0)
-    if first:
-        wide_sum.step(2)
-        narrow_last.step(2)
-    else:
-        wide_sum.step(3)
-    weight_grad(na_h, dqkv_s, narrow_g[0])
-    weight_grad(ctx_ref, g_s, narrow_g[1])
-    if first:
-        wide_sum.step(3)
-        narrow_last.step(3)
-    need("outall")
+    pump("fold0")
+    weight_grad(na_h, dqkv_s, qkv_g)
+    pump("na")
     next_rows.wait()
     for copy in contexts:
         copy.wait()
@@ -1447,6 +1496,7 @@
         copy.start()
         copy.wait()
         small_ref[0:8, :] += got_s[at]
+    pump("stats")
     back.wait()
 
     @pl.loop(0, half_blocks)
@@ -1460,12 +1510,10 @@
 
     grad_out = pltpu.make_async_copy(arecv.at[0], dx_o, local.at[1])
     grad_out.start()
-    swaps[0][1].wait_send()
-    wide_sum.finish()
-    if first:
-        wide_last.finish()
-        narrow_sum.finish()
-        narrow_last.finish()
+    latest.pop().wait_send()
+    pump("end")
+    for item in sums.values():
+        item.finish()
     grad_out.wait()
 
 
@@ -1478,7 +1526,6 @@
     up,
     out_w,
     qkvw,
-    out_all,
     tables,
     qkv,
     lse,
@@ -1500,11 +1547,15 @@
     w = qkvw.shape[2] // 3
     ff = up.shape[2]
     n = lax.axis_size("dp")
-    wide_shapes = [(ff, features), (features, ff)]
-    narrow_shapes = [(features, 3 * w), (w, features)]
+    down_shape, out_w_shape, up_shape, qkv_shape = (
+        (ff, features),
+        (w, features),
+        (features, ff),
+        (features, 3 * w),
+    )
     shape = jax.ShapeDtypeStruct
-    args = [grad, u, down, up, out_w, qkvw, out_all, *tables, qkv, lse, ctx, xn, x]
-    in_specs = [VMEM] + [ANY] * 11 + [VMEM, ANY, VMEM]
+    args = [grad, u, down, up, out_w, qkvw, *tables, qkv, lse, ctx, xn, x]
+    in_specs = [VMEM] + [ANY] * 10 + [VMEM, ANY, VMEM]
     if first:
         args.append(far_x)
         in_specs.append(VMEM)
@@ -1512,15 +1563,19 @@
         args.append(far_g)
         in_specs.append(VMEM)
     args += [gains, ob, hidden, nb, na, *ready]
-    in_specs += [VMEM] * 2 + [ANY] * (3 + len(ready))
+    in_specs += [VMEM] * 2 + [ANY] * 3
+    if first:
+        in_specs += [VMEM, ANY]
     low = lambda shapes: [shape(item, B16) for item in shapes]
-    chunks = [(a // n, b) for a, b in wide_shapes]
     out_shape = [shape((rows, features), F32), shape((16, features), F32)]
-    out_shape += low(wide_shapes + narrow_shapes + chunks)
-    out_specs = [ANY, VMEM] + [ANY] * 4 + [VMEM] * 2
+    out_shape += low([down_shape, out_w_shape, up_shape, qkv_shape, down_shape, out_w_shape])
+    out_specs = [ANY, VMEM] + [ANY] * 6
     if first:
-        out_shape += low(wide_shapes + narrow_shapes)
-        out_specs += [ANY] * 4
+        out_shape += low([up_shape, qkv_shape])
+        out_specs += [ANY] * 2
+    else:
+        out_shape += low([(features // n, ff)])
+        out_specs += [VMEM]
     scratch = [
         pltpu.VMEM((2, seq, features), B16),
         pltpu.VMEM((2, seq, ff), B16),
@@ -1538,18 +1593,22 @@
         pltpu.VMEM((rows, 4 * w), B16),
         pltpu.VMEM((2, 8, features), F32),
     ]
-    scratch += [pltpu.VMEM(item.shape[1:], B16) for item in (down, up, out_w, qkvw, out_all)]
+    scratch += [pltpu.VMEM(item.shape[1:], B16) for item in (down, up, out_w, qkvw)]
+    scratch += [pltpu.VMEM((4 * w, features), B16)]
     scratch += [pltpu.VMEM(item.shape, F32) for item in tables]
     scratch += [pltpu.VMEM(qkv.shape, B16), pltpu.VMEM(lse.shape, F32)]
-    scratch += [DMA((13,)), DMA((13,)), DMA((2,)), DMA((2,)), DMA((10,))]
+    scratch += [pltpu.VMEM((2, features), F32), pltpu.VMEM((1, features), F32)]
+    scratch += [DMA((16,)), DMA((16,)), DMA((2,)), DMA((2,)), DMA((9,))]
     scratch += [pltpu.VMEM((2, 2 * seq, QB), B16), pltpu.VMEM((2, QB, features), B16)]
     scratch += [DMA((2,)), DMA((2,))]
-    scratch += Scatter.scratch(n, wide_shapes)
-    if first:
-        scratch += [pltpu.VMEM((a // n, b), B16) for a, b in narrow_shapes]
-        scratch += Gather.scratch(n, 2)
-        scratch += Scatter.scratch(n, narrow_shapes)
-        scratch += Gather.scratch(n, 2)
+    shapes = half_shapes(down_shape) + [out_w_shape]
+    scratch += chunk_scratch(n, shapes) + Scatter.scratch(n, shapes) + Gather.scratch(n, 3)
+    if not first:
+        scratch += Scatter.scratch(n, half_shapes(up_shape))
+    else:
+        shapes = half_shapes(qkv_shape)
+        scratch += chunk_scratch(n, shapes) + Scatter.scratch(n, shapes)
+        scratch += Gather.scratch(n, 2) * 2
     return pl.pallas_call(
         functools.partial(backward_layer_kernel, l, first, final, rows, w, n),
         in_specs=in_specs,
@@ -1585,23 +1644,13 @@
     rows, features = tokens.shape
     tensor = lax.axis_size("tensor")
     dp = lax.axis_size("dp")
-    dp_index = lax.axis_index("dp")
     w = qkv_weight.shape[2] // 3
     ff = up_weight.shape[2]
     tables = rope_tables(SEQ_LEN, 128)
 
-    wide = lambda v: v.astype(F32)
-
-    share = out_weight.shape[1] // dp
-    piece = lax.dynamic_slice_in_dim(out_weight, dp_index * share, share, axis=1)
-    near = [out_weight, lax.all_gather(swap(piece, "tensor", 2), "dp", axis=1, tiled=True)]
-    far = [swap(item, "tensor", 1) for item in near]
-    out_all = jnp.concatenate([near[0], far[0], near[1], far[1]], axis=1)
-
     x = tokens
     stored = []
     far_x = None
-    bias_sum = wide(out_bias) + wide(down_bias)
     for l in range(LAYERS):
         got = forward_layer(
             l,
@@ -1612,11 +1661,12 @@
             qkv_weight,
             out_weight,
             tables,
-            wide(up_bias[l])[None],
-            wide(qkv_bias[l])[None],
-            bias_sum[l][None],
-            wide(norm_gain[l]),
-            wide(norm_shift[l]),
+            up_bias,
+            qkv_bias,
+            out_bias,
+            down_bias,
+            norm_gain,
+            norm_shift,
             cotangent,
         )
         na, nb, u, hidden, qkv, ctx, lse, x_next = got[:8]
@@ -1629,7 +1679,7 @@
     output = x
 
     grad = cotangent
-    big = [None] * LAYERS
+    down_sums, out_sums, up_sums, qkv_sums = ([None] * LAYERS for _ in range(4))
     ready = ()
     small = [None] * LAYERS
     for l in reversed(range(LAYERS)):
@@ -1643,7 +1693,6 @@
             up_weight,
             out_weight,
             qkv_weight,
-            out_all,
             tables,
             qkv,
             lse,
@@ -1652,20 +1701,22 @@
             x,
             far_x,
             far_g,
-            wide(norm_gain[l]),
-            wide(out_bias[l])[None],
+            norm_gain,
+            out_bias,
             hidden,
             nb,
             na,
             ready,
         )
-        ready = (*found[4:6], *found[2:4])
+        down_sums[l], out_sums[l] = found[4:6]
         if l < LAYERS - 1:
-            big[l + 1] = found[6:]
-    *big[0], small = last_sums(ready[:2], ready[2:], jnp.concatenate(small), 2 * LAYERS)
+            up_sums[l + 1], qkv_sums[l + 1] = found[6:]
+        else:
+            ready = (found[6], found[3])
+    up_sums[0], qkv_sums[0], small = last_sums(found[2:4], jnp.concatenate(small), 2 * LAYERS)
     small = small.reshape(LAYERS, 16, features)
     down_all, up_all, qkv_all, out_w_all = (
-        jnp.stack([item[i] for item in big]).astype(F32) for i in range(4)
+        jnp.stack(item).astype(F32) for item in (down_sums, up_sums, qkv_sums, out_sums)
     )
     layer_stats = jnp.sqrt(jnp.sum(small[:, 5:8], axis=2) / (rows * dp * tensor * features))
     bias_all = small[:, 4]

time: 581 us -> 514 us (0.88)
  Pallas kernels: 509 us -> 482 us
  between operations: 14.7 us -> 1.18 us
  local copies, waits for them, and re-layouts: 22.8 us -> 9.63 us
  other arithmetic: 21.2 us -> 13 us
    pallas_call x1, Pallas kernels: 102 us -> 77.4 us  [last_sums(): pl.pallas_call(functools.partial(last_sums_kernel, n, count), in_specs=[A...]
    pallas_call x2, Pallas kernels: 263 us -> 249 us  [backward_layer(): pl.pallas_call(functools.partial(backward_layer_kernel, l, first, final,...]
    pallas_call x2, Pallas kernels: 144 us -> 156 us  [forward_layer(): pl.pallas_call(functools.partial(forward_layer_kernel, l, first, final, r...]
    convert_element_type x10 -> x3, other arithmetic: 18.7 us -> 11.5 us  [on_group(): jnp.stack(item).astype(F32)]
    unnamed x39 -> x29, local copies, waits for them, and re-layouts: 15.1 us -> 8.98 us
  transfers between devices with their start and end apart: 4 -> 0, of which waited for: 0 -> 0; matrix products, arithmetic and copies ran while one was open for 3% -> 0% of each run, Pallas kernels for 25% -> 0%
where the time goes in v3:
time: 514 us; the launch traced here: 505 us
  Pallas kernels  482 us (94%)
  other arithmetic  13 us (3%)
  local copies, waits for them, and re-layouts  9.63 us (2%)
    pallas_call x2, Pallas kernels, backward_layer(): pl.pallas_call(functools.partial(backward_layer_kernel, l, first, final,...  249 us
    pallas_call x2, Pallas kernels, forward_layer(): pl.pallas_call(functools.partial(forward_layer_kernel, l, first, final, r...  156 us
    pallas_call x1, Pallas kernels, last_sums(): pl.pallas_call(functools.partial(last_sums_kernel, n, count), in_specs=[A...  77.4 us
    convert_element_type x3, other arithmetic, on_group(): jnp.stack(item).astype(F32)  11.5 us

profile of v3, /device:TPU:0, one launch (start us, length us, event | category | flops | bytes accessed | tf_op | source)
XLA Modules:
  0.0 505.4 jit_solution(5120608363816626759)
XLA Ops:
  0.6 87.0 %forward_layer.2 = (bf16[2048,1024]{1,0:T(8,128)(2,1)}, bf16[2048,1024]{1,0:T(8,128)(2,1)}, f32[2048,1024]{1,0:T(8,128)}, bf16[2048,1024]{1,0:T(8,128)(2,1)}, bf...) custom-call(bf16[512,1024]{1,0:T(8,128)(2,1)} %refs_13_.5, ...), custom_call_target="tpu_custom_call" | custom-call | flops 25769803776 | bytes 41943040 | tf_op jit(solution)/shard_map/forward_layer/pallas_call | solution.py:877
  87.7 68.5 %forward_layer.3 = (bf16[2048,1024]{1,0:T(8,128)(2,1)}, bf16[2048,1024]{1,0:T(8,128)(2,1)}, f32[2048,1024]{1,0:T(8,128)}, bf16[2048,1024]{1,0:T(8,128)(2,1)}, bf...) custom-call(f32[1024,1024]{1,0:T(8,128)} %get-tuple-element.48.refs_, ...), custom_call_target="tpu_custom_call" | custom-call | flops 25769803776 | bytes 41943040 | tf_op jit(solution)/shard_map/forward_layer/pallas_call | solution.py:877
  156.2 118.1 %backward_layer.2 = (f32[512,1024]{1,0:T(8,128)}, f32[16,1024]{1,0:T(8,128)}, bf16[1024,1024]{1,0:T(8,128)(2,1)}, bf16[256,1024]{1,0:T(8,128)(2,1)}, bf16[1024,1...) custom-call(bf16[512,1024]{1,0:T(8,128)(2,1)} %refs_0_.3, ...), custom_call_target="tpu_custom_call" | custom-call | flops 25769803776 | bytes 41943040 | tf_op jit(solution)/shard_map/backward_layer/pallas_call | solution.py:1612
  274.2 0.0 copy-start.10
  274.3 0.0 copy-start.8
  274.3 130.5 %backward_layer.3 = (f32[512,1024]{1,0:T(8,128)}, f32[16,1024]{1,0:T(8,128)}, bf16[1024,1024]{1,0:T(8,128)(2,1)}, bf16[256,1024]{1,0:T(8,128)(2,1)}, bf16[1024,1...) custom-call(f32[512,1024]{1,0:T(8,128)} %get-tuple-element.58.refs_0, ...), custom_call_target="tpu_custom_call" | custom-call | flops 25769803776 | bytes 41943040 | tf_op jit(solution)/shard_map/backward_layer/pallas_call | solution.py:1612
  404.8 0.0 copy-done.10
  404.8 0.9 pad_maximum_fusion.refs_2_
  405.7 0.0 copy-start
  405.7 1.6 copy-done
  407.3 1.4 copy-done.1
  408.7 77.4 %last_sums.1 = (bf16[1024,1024]{1,0:T(8,128)(2,1)S(1)}, bf16[1024,768]{1,0:T(8,128)(2,1)S(1)}, f32[32,1024]{1,0:T(8,128)S(1)}) custom-call(bf16[1024,1024]{1,0:T(8,128)(2,1)S(1)} %copy-done, bf16[1024,768]{1,0:T(8,128)(2,1)S(1)} %copy-done.1, f32[32,1024]{1,0:T(8,128)S(1)} %pad_maximum_fusion.refs_2_), custom_call_target="tpu_custom_call" | custom-call | flops 1048576 | bytes 209715200 | tf_op jit(solution)/shard_map/last_sums/pallas_call | solution.py:1121
  486.1 0.1 slice_reduce_fusion
  486.2 0.6 multiply_sqrt_fusion
  486.8 0.6 copy.34
  487.4 0.6 fusion
  488.0 0.6 copy_bitcast_fusion
  488.6 0.0 copy-done.8
  488.6 0.0 copy-done.9
  488.6 1.5 maximum_convert_fusion.3
  490.1 0.0 copy-done.7
  490.1 3.6 maximum_convert_fusion.2
  493.7 0.0 copy-done.2
  493.7 0.7 copy-done.3
  494.4 0.8 copy-done.4
  495.2 6.5 %maximum_convert_fusion = (f32[2,1024,1024]{2,1,0:T(8,128)}, f32[2,1024,1024]{2,1,0:T(8,128)}) fusion(bf16[1,1024,1024]{2,1,0:T(8,128)(2,1)S(1)} %bitcast.24, bf16[1,1024,1024]{2,1,0:T(8,128)(2,1)S(1)} %bitcast.16, bf16[1,1024,1024]{2,1,0:T(8,128)(2,1)S(1)} %bitcast.22, bf16[1,1024,1024]{2,1,0:T(8,128)(2,1)S(1)} %bitcast.23), kind=kLoop, calls=%fused_computation | loop fusion | flops 8388608 | bytes 25165824 | tf_op jit(solution)/shard_map/convert_element_type | solution.py:1719
  501.7 0.0 copy-done.11
  501.7 0.6 copy.38
  502.3 0.0 copy-done.5
  502.3 1.3 copy.39
  503.6 0.0 copy-done.6
  503.6 1.3 copy.40
  (11 shorter events, 0.0 us)
Async XLA Ops:
  274.2 130.6 %copy-start.10 = (f32[16,1024]{1,0:T(8,128)S(1)}, f32[16,1024]{1,0:T(8,128)}, u32[]{:S(2)}) copy-start(f32[16,1024]{1,0:T(8,128)} %get-tuple-element.73) | copy-start | bytes 196612
  274.3 214.4 %copy-start.8 = (bf16[256,1024]{1,0:T(8,128)(2,1)S(1)}, bf16[256,1024]{1,0:T(8,128)(2,1)}, u32[]{:S(2)}) copy-start(bf16[256,1024]{1,0:T(8,128)(2,1)} %get-tuple-element.78) | copy-start | bytes 1572868
  405.7 1.6 copy-start
  407.3 1.4 copy-start.1
  408.7 80.0 %copy-start.9 = (bf16[256,1024]{1,0:T(8,128)(2,1)S(1)}, bf16[256,1024]{1,0:T(8,128)(2,1)}, u32[]{:S(2)}) copy-start(bf16[256,1024]{1,0:T(8,128)(2,1)} %get-tuple-element.77) | copy-start | bytes 1572868
  408.7 81.4 %copy-start.7 = (bf16[1024,768]{1,0:T(8,128)(2,1)S(1)}, bf16[1024,768]{1,0:T(8,128)(2,1)}, u32[]{:S(2)}) copy-start(bf16[1024,768]{1,0:T(8,128)(2,1)} %get-tuple-element.75) | copy-start | bytes 4718596
  488.6 13.1 %copy-start.11 = (f32[2,1024]{1,0:T(2,128)}, f32[2,1024]{1,0:T(2,128)S(1)}, u32[]{:S(2)}) copy-start(f32[2,1024]{1,0:T(2,128)S(1)} %get-tuple-element.135) | copy-start | bytes 24580
  490.1 3.6 copy-start.2
  490.1 4.3 copy-start.3
  490.1 5.1 %copy-start.4 = (bf16[1024,1024]{1,0:T(8,128)(2,1)S(1)}, bf16[1024,1024]{1,0:T(8,128)(2,1)}, u32[]{:S(2)}) copy-start(bf16[1024,1024]{1,0:T(8,128)(2,1)} %get-tuple-element.80) | copy-start | bytes 6291460
  495.2 7.1 %copy-start.5 = (f32[512,1024]{1,0:T(8,128)S(1)}, f32[512,1024]{1,0:T(8,128)}, u32[]{:S(2)}) copy-start(f32[512,1024]{1,0:T(8,128)} %get-tuple-element.130.refs_12_) | copy-start | bytes 6291460
  501.7 1.9 copy-start.6

commit v4 on v3

--- a/solution.py
+++ b/solution.py
@@ -264,6 +264,11 @@
 def gelu_slope(u):
     share, bell = normal_parts(u)
     return share + u * bell * ((2.0 * math.pi) ** -0.5)
+
+
+def gelu_and_slope(u):
+    share, bell = normal_parts(u)
+    return u * share, share + u * bell * ((2.0 * math.pi) ** -0.5)
 
 
 def standardize(x):
@@ -690,8 +695,9 @@
             def _(r):
                 at = block(r + h * half_blocks)
                 u = dot_nn(nb_s[k, at, :], up_ref[...]) + upb_ref[...]
-                u_s[r] = u
-                hid_s[k, at, :] = gelu(u).astype(B16)
+                value, slope = gelu_and_slope(u)
+                u_s[r] = slope
+                hid_s[k, at, :] = value.astype(B16)
 
             for r in range(half_blocks):
                 copy = pltpu.make_async_copy(
@@ -1254,7 +1260,7 @@
             load_u(k, i).wait()
             at = pl.ds(i * QB, QB)
             d_hidden = dot_nt(g_s[k, at, :], down_ref[...])
-            d_pre = (d_hidden * gelu_slope(u_s[i % 2])).astype(B16)
+            d_pre = (d_hidden * u_s[i % 2]).astype(B16)
             dpre_s[k, at, :] = d_pre
             small_ref[8:9, :ff] += jnp.sum(d_pre.astype(F32), axis=0, keepdims=True)
             if i + 2 < blocks:
@@ -1265,8 +1271,9 @@
                 pump("feed%d half" % k)
 
         need("up")
-        if latest:
-            latest.pop().wait_send()
+        for copy in latest:
+            copy.wait_send()
+        latest.clear()
 
         @pl.loop(0, half_blocks)
         def _(r):
@@ -1322,15 +1329,21 @@
             dqkv_s[k, swapped(r), :] = low
             small_ref[9:10, : 3 * w] += jnp.sum(low.astype(F32), axis=0, keepdims=True)
 
-        latest.pop().wait_send()
+        for copy in latest:
+            copy.wait_send()
+        latest.clear()
 
         @pl.loop(0, half_blocks)
         def _(r):
             osend[block(r), :] = dot_nt(dqkv_s[k, block(r + half_blocks), :], qkvw_ref[...])
-
-        swaps[k].append(remote(osend, arecv.at[k], sems, 4 + 2 * k, core))
-        swaps[k][1].start()
-        latest.append(swaps[k][1])
+            piece(k, r).start()
+
+        latest.extend(piece(k, r) for r in range(half_blocks))
+
+    def piece(k, r):
+        at = block(r)
+        index = 16 + k * half_blocks + r
+        return remote(osend.at[at, :], arecv.at[k, at, :], sems, index, core)
 
     def x_rows(k, r):
         if not first:
@@ -1338,11 +1351,11 @@
         return (far_ref if k else x_ref)[block(r), :].astype(F32)
 
     def fold(k):
-        for copy in swaps[k]:
-            copy.wait_recv()
+        swaps[k][0].wait_recv()
 
         @pl.loop(0, half_blocks)
         def _(r):
+            piece(k, r).wait_recv()
             at = block(r)
             d_na = dot_nt(dqkv_s[k, at, :], qkvw_ref[...]) + arecv[k, at, :]
             d_nb = dot_nt(dpre_s[k, at, :], up_ref[...]) + brecv[k, at, :]
@@ -1407,15 +1420,15 @@
             "attend1 2": "c",
             "attend1 3": "a",
             "fold1": "a",
+            "stats": "a",
             "na": "a",
-            "stats": "a",
         }
     else:
         plan = {
             "feed0": "a",
-            "feed1 half": "a",
             "feed1": "a",
             "nb": "a",
+            "attend1 0": "a",
             "attend1 3": "ab",
             "attend0 1": "ab",
             "fold0": "ab",
@@ -1475,8 +1488,6 @@
         attend(0, at_heads(0))
     fold(0)
     pump("fold0")
-    weight_grad(na_h, dqkv_s, qkv_g)
-    pump("na")
     next_rows.wait()
     for copy in contexts:
         copy.wait()
@@ -1491,12 +1502,15 @@
         small_ref[6:7, :] += jnp.sum(attn * attn, axis=0, keepdims=True)
         small_ref[7:8, :] += jnp.sum(feed_out * feed_out, axis=0, keepdims=True)
 
-    for at, other in ((0, core), (1, far)):
-        copy = remote(small_ref.at[pl.ds(0, 8), :], got_s.at[at], sems, 11 + at, other)
-        copy.start()
-        copy.wait()
-        small_ref[0:8, :] += got_s[at]
     pump("stats")
+    near_sums = remote(small_ref.at[pl.ds(0, 8), :], got_s.at[0], sems, 11, core)
+    near_sums.start()
+    weight_grad(na_h, dqkv_s, qkv_g)
+    near_sums.wait()
+    small_ref[0:8, :] += got_s[0]
+    far_sums = remote(small_ref.at[pl.ds(0, 8), :], got_s.at[1], sems, 12, far)
+    far_sums.start()
+    pump("na")
     back.wait()
 
     @pl.loop(0, half_blocks)
@@ -1510,7 +1524,10 @@
 
     grad_out = pltpu.make_async_copy(arecv.at[0], dx_o, local.at[1])
     grad_out.start()
-    latest.pop().wait_send()
+    far_sums.wait()
+    small_ref[0:8, :] += got_s[1]
+    for copy in latest:
+        copy.wait_send()
     pump("end")
     for item in sums.values():
         item.finish()
@@ -1598,7 +1615,8 @@
     scratch += [pltpu.VMEM(item.shape, F32) for item in tables]
     scratch += [pltpu.VMEM(qkv.shape, B16), pltpu.VMEM(lse.shape, F32)]
     scratch += [pltpu.VMEM((2, features), F32), pltpu.VMEM((1, features), F32)]
-    scratch += [DMA((16,)), DMA((16,)), DMA((2,)), DMA((2,)), DMA((9,))]
+    sems = 16 + 2 * (rows // QB)
+    scratch += [DMA((sems,)), DMA((sems,)), DMA((2,)), DMA((2,)), DMA((9,))]
     scratch += [pltpu.VMEM((2, 2 * seq, QB), B16), pltpu.VMEM((2, QB, features), B16)]
     scratch += [DMA((2,)), DMA((2,))]
     shapes = half_shapes(down_shape) + [out_w_shape]

time: 514 us -> 503 us (0.979)
  Pallas kernels: 482 us -> 470 us
    pallas_call x2, Pallas kernels: 156 us -> 148 us  [forward_layer(): pl.pallas_call(functools.partial(forward_layer_kernel, l, first, final, r...]
    pallas_call x2, Pallas kernels: 249 us -> 243 us  [backward_layer(): pl.pallas_call(functools.partial(backward_layer_kernel, l, first, final,...]
where the time goes in v4:
time: 503 us; the launch traced here: 494 us
  Pallas kernels  470 us (93%)
  other arithmetic  13 us (3%)
  local copies, waits for them, and re-layouts  9.63 us (2%)
    pallas_call x2, Pallas kernels, backward_layer(): pl.pallas_call(functools.partial(backward_layer_kernel, l, first, final,...  243 us
    pallas_call x2, Pallas kernels, forward_layer(): pl.pallas_call(functools.partial(forward_layer_kernel, l, first, final, r...  148 us
    pallas_call x1, Pallas kernels, last_sums(): pl.pallas_call(functools.partial(last_sums_kernel, n, count), in_specs=[A...  78.9 us
    convert_element_type x3, other arithmetic, on_group(): jnp.stack(item).astype(F32)  11.5 us

profile of v4, /device:TPU:0, one launch (start us, length us, event | category | flops | bytes accessed | tf_op | source)
XLA Modules:
  0.0 493.8 jit_solution(4284539907345703327)
XLA Ops:
  0.6 87.8 %forward_layer.2 = (bf16[2048,1024]{1,0:T(8,128)(2,1)}, bf16[2048,1024]{1,0:T(8,128)(2,1)}, f32[2048,1024]{1,0:T(8,128)}, bf16[2048,1024]{1,0:T(8,128)(2,1)}, bf...) custom-call(bf16[512,1024]{1,0:T(8,128)(2,1)} %refs_13_.5, ...), custom_call_target="tpu_custom_call" | custom-call | flops 25769803776 | bytes 41943040 | tf_op jit(solution)/shard_map/forward_layer/pallas_call | solution.py:883
  88.5 59.9 %forward_layer.3 = (bf16[2048,1024]{1,0:T(8,128)(2,1)}, bf16[2048,1024]{1,0:T(8,128)(2,1)}, f32[2048,1024]{1,0:T(8,128)}, bf16[2048,1024]{1,0:T(8,128)(2,1)}, bf...) custom-call(f32[1024,1024]{1,0:T(8,128)} %get-tuple-element.48.refs_, ...), custom_call_target="tpu_custom_call" | custom-call | flops 25769803776 | bytes 41943040 | tf_op jit(solution)/shard_map/forward_layer/pallas_call | solution.py:883
  148.4 116.0 %backward_layer.2 = (f32[512,1024]{1,0:T(8,128)}, f32[16,1024]{1,0:T(8,128)}, bf16[1024,1024]{1,0:T(8,128)(2,1)}, bf16[256,1024]{1,0:T(8,128)(2,1)}, bf16[1024,1...) custom-call(bf16[512,1024]{1,0:T(8,128)(2,1)} %refs_0_.3, ...), custom_call_target="tpu_custom_call" | custom-call | flops 25769803776 | bytes 41943040 | tf_op jit(solution)/shard_map/backward_layer/pallas_call | solution.py:1630
  264.4 0.0 copy-start.10
  264.4 0.0 copy-start.8
  264.4 127.4 %backward_layer.3 = (f32[512,1024]{1,0:T(8,128)}, f32[16,1024]{1,0:T(8,128)}, bf16[1024,1024]{1,0:T(8,128)(2,1)}, bf16[256,1024]{1,0:T(8,128)(2,1)}, bf16[1024,1...) custom-call(f32[512,1024]{1,0:T(8,128)} %get-tuple-element.58.refs_0, ...), custom_call_target="tpu_custom_call" | custom-call | flops 25769803776 | bytes 41943040 | tf_op jit(solution)/shard_map/backward_layer/pallas_call | solution.py:1630
  391.8 0.0 copy-done.10
  391.8 0.9 pad_maximum_fusion.refs_2_
  392.6 0.0 copy-start
  392.7 1.6 copy-done
  394.2 1.4 copy-done.1
  395.7 78.9 %last_sums.1 = (bf16[1024,1024]{1,0:T(8,128)(2,1)S(1)}, bf16[1024,768]{1,0:T(8,128)(2,1)S(1)}, f32[32,1024]{1,0:T(8,128)S(1)}) custom-call(bf16[1024,1024]{1,0:T(8,128)(2,1)S(1)} %copy-done, bf16[1024,768]{1,0:T(8,128)(2,1)S(1)} %copy-done.1, f32[32,1024]{1,0:T(8,128)S(1)} %pad_maximum_fusion.refs_2_), custom_call_target="tpu_custom_call" | custom-call | flops 1048576 | bytes 209715200 | tf_op jit(solution)/shard_map/last_sums/pallas_call | solution.py:1127
  474.6 0.1 slice_reduce_fusion
  474.7 0.6 multiply_sqrt_fusion
  475.2 0.6 copy.34
  475.9 0.6 fusion
  476.5 0.6 copy_bitcast_fusion
  477.1 0.0 copy-done.8
  477.1 0.0 copy-done.9
  477.1 1.5 maximum_convert_fusion.3
  478.6 0.0 copy-done.7
  478.6 3.6 maximum_convert_fusion.2
  482.2 0.0 copy-done.2
  482.2 0.7 copy-done.3
  482.8 0.8 copy-done.4
  483.7 6.5 %maximum_convert_fusion = (f32[2,1024,1024]{2,1,0:T(8,128)}, f32[2,1024,1024]{2,1,0:T(8,128)}) fusion(bf16[1,1024,1024]{2,1,0:T(8,128)(2,1)S(1)} %bitcast.24, bf16[1,1024,1024]{2,1,0:T(8,128)(2,1)S(1)} %bitcast.16, bf16[1,1024,1024]{2,1,0:T(8,128)(2,1)S(1)} %bitcast.22, bf16[1,1024,1024]{2,1,0:T(8,128)(2,1)S(1)} %bitcast.23), kind=kLoop, calls=%fused_computation | loop fusion | flops 8388608 | bytes 25165824 | tf_op jit(solution)/shard_map/convert_element_type | solution.py:1737
  490.2 0.0 copy-done.11
  490.2 0.6 copy.38
  490.8 0.0 copy-done.5
  490.8 1.3 copy.39
  492.1 0.0 copy-done.6
  492.1 1.3 copy.40
  (11 shorter events, 0.0 us)
Async XLA Ops:
  264.4 127.4 %copy-start.10 = (f32[16,1024]{1,0:T(8,128)S(1)}, f32[16,1024]{1,0:T(8,128)}, u32[]{:S(2)}) copy-start(f32[16,1024]{1,0:T(8,128)} %get-tuple-element.73) | copy-start | bytes 196612
  264.4 212.7 %copy-start.8 = (bf16[256,1024]{1,0:T(8,128)(2,1)S(1)}, bf16[256,1024]{1,0:T(8,128)(2,1)}, u32[]{:S(2)}) copy-start(bf16[256,1024]{1,0:T(8,128)(2,1)} %get-tuple-element.78) | copy-start | bytes 1572868
  392.6 1.6 copy-start
  394.2 1.4 copy-start.1
  395.6 81.5 %copy-start.9 = (bf16[256,1024]{1,0:T(8,128)(2,1)S(1)}, bf16[256,1024]{1,0:T(8,128)(2,1)}, u32[]{:S(2)}) copy-start(bf16[256,1024]{1,0:T(8,128)(2,1)} %get-tuple-element.77) | copy-start | bytes 1572868
  395.7 82.9 %copy-start.7 = (bf16[1024,768]{1,0:T(8,128)(2,1)S(1)}, bf16[1024,768]{1,0:T(8,128)(2,1)}, u32[]{:S(2)}) copy-start(bf16[1024,768]{1,0:T(8,128)(2,1)} %get-tuple-element.75) | copy-start | bytes 4718596
  477.1 13.1 %copy-start.11 = (f32[2,1024]{1,0:T(2,128)}, f32[2,1024]{1,0:T(2,128)S(1)}, u32[]{:S(2)}) copy-start(f32[2,1024]{1,0:T(2,128)S(1)} %get-tuple-element.135) | copy-start | bytes 24580
  478.6 3.6 copy-start.2
  478.6 4.3 copy-start.3
  478.6 5.1 %copy-start.4 = (bf16[1024,1024]{1,0:T(8,128)(2,1)S(1)}, bf16[1024,1024]{1,0:T(8,128)(2,1)}, u32[]{:S(2)}) copy-start(bf16[1024,1024]{1,0:T(8,128)(2,1)} %get-tuple-element.80) | copy-start | bytes 6291460
  483.7 7.1 %copy-start.5 = (f32[512,1024]{1,0:T(8,128)S(1)}, f32[512,1024]{1,0:T(8,128)}, u32[]{:S(2)}) copy-start(f32[512,1024]{1,0:T(8,128)} %get-tuple-element.130.refs_12_) | copy-start | bytes 6291460
  490.2 1.9 copy-start.6

commit v5 on v4

--- a/solution.py
+++ b/solution.py
@@ -1413,26 +1413,30 @@
             "near": "cd",
             "hid": "cd",
             "feed1 half": "c",
-            "feed1": "ca",
-            "nb": "a",
-            "attend1 0": "c",
+            "feed1": "a",
+            "nb": "c",
             "attend1 1": "a",
             "attend1 2": "c",
-            "attend1 3": "a",
-            "fold1": "a",
+            "after1": "a",
+            "fold1": "ac",
             "stats": "a",
             "na": "a",
+            "back": "a",
         }
     else:
         plan = {
             "feed0": "a",
             "feed1": "a",
-            "nb": "a",
             "attend1 0": "a",
-            "attend1 3": "ab",
-            "attend0 1": "ab",
-            "fold0": "ab",
-            "stats": "ab",
+            "attend1 1": "a",
+            "attend1 2": "b",
+            "after1": "a",
+            "attend0 0": "b",
+            "attend0 1": "a",
+            "attend0 3": "b",
+            "fold0": "a",
+            "stats": "b",
+            "na": "a",
         }
 
     def pump(point):
@@ -1478,6 +1482,7 @@
         sums["b"].start()
     pump("nb")
     attend(1, at_heads(1))
+    pump("after1")
     fold(1)
     back = remote(ysend, yrecv, sems, 7, far)
     back.start()
@@ -1512,6 +1517,7 @@
     far_sums.start()
     pump("na")
     back.wait()
+    pump("back")
 
     @pl.loop(0, half_blocks)
     def _(r):

time: 503 us -> 487 us (0.968)
  Pallas kernels: 470 us -> 455 us
    pallas_call x2, Pallas kernels: 243 us -> 230 us  [backward_layer(): pl.pallas_call(functools.partial(backward_layer_kernel, l, first, final,...]
where the time goes in v5:
time: 487 us; the launch traced here: 478 us
  Pallas kernels  455 us (93%)
  other arithmetic  13 us (3%)
  local copies, waits for them, and re-layouts  9.63 us (2%)
    pallas_call x2, Pallas kernels, backward_layer(): pl.pallas_call(functools.partial(backward_layer_kernel, l, first, final,...  230 us
    pallas_call x2, Pallas kernels, forward_layer(): pl.pallas_call(functools.partial(forward_layer_kernel, l, first, final, r...  148 us
    pallas_call x1, Pallas kernels, last_sums(): pl.pallas_call(functools.partial(last_sums_kernel, n, count), in_specs=[A...  77 us
    convert_element_type x3, other arithmetic, on_group(): jnp.stack(item).astype(F32)  11.5 us

profile of v5, /device:TPU:0, one launch (start us, length us, event | category | flops | bytes accessed | tf_op | source)
XLA Modules:
  0.0 478.4 jit_solution(1722682636038896700)
XLA Ops:
  0.6 87.8 %forward_layer.2 = (bf16[2048,1024]{1,0:T(8,128)(2,1)}, bf16[2048,1024]{1,0:T(8,128)(2,1)}, f32[2048,1024]{1,0:T(8,128)}, bf16[2048,1024]{1,0:T(8,128)(2,1)}, bf...) custom-call(bf16[512,1024]{1,0:T(8,128)(2,1)} %refs_13_.5, ...), custom_call_target="tpu_custom_call" | custom-call | flops 25769803776 | bytes 41943040 | tf_op jit(solution)/shard_map/forward_layer/pallas_call | solution.py:883
  88.5 59.9 %forward_layer.3 = (bf16[2048,1024]{1,0:T(8,128)(2,1)}, bf16[2048,1024]{1,0:T(8,128)(2,1)}, f32[2048,1024]{1,0:T(8,128)}, bf16[2048,1024]{1,0:T(8,128)(2,1)}, bf...) custom-call(f32[1024,1024]{1,0:T(8,128)} %get-tuple-element.48.refs_, ...), custom_call_target="tpu_custom_call" | custom-call | flops 25769803776 | bytes 41943040 | tf_op jit(solution)/shard_map/forward_layer/pallas_call | solution.py:883
  148.4 106.2 %backward_layer.2 = (f32[512,1024]{1,0:T(8,128)}, f32[16,1024]{1,0:T(8,128)}, bf16[1024,1024]{1,0:T(8,128)(2,1)}, bf16[256,1024]{1,0:T(8,128)(2,1)}, bf16[1024,1...) custom-call(bf16[512,1024]{1,0:T(8,128)(2,1)} %refs_0_.3, ...), custom_call_target="tpu_custom_call" | custom-call | flops 25769803776 | bytes 41943040 | tf_op jit(solution)/shard_map/backward_layer/pallas_call | solution.py:1636
  254.6 0.0 copy-start.10
  254.6 0.0 copy-start.8
  254.6 123.7 %backward_layer.3 = (f32[512,1024]{1,0:T(8,128)}, f32[16,1024]{1,0:T(8,128)}, bf16[1024,1024]{1,0:T(8,128)(2,1)}, bf16[256,1024]{1,0:T(8,128)(2,1)}, bf16[1024,1...) custom-call(f32[512,1024]{1,0:T(8,128)} %get-tuple-element.58.refs_0, ...), custom_call_target="tpu_custom_call" | custom-call | flops 25769803776 | bytes 41943040 | tf_op jit(solution)/shard_map/backward_layer/pallas_call | solution.py:1636
  378.3 0.0 copy-done.10
  378.3 0.9 pad_maximum_fusion.refs_2_
  379.1 0.0 copy-start
  379.1 1.6 copy-done
  380.7 1.4 copy-done.1
  382.1 77.0 %last_sums.1 = (bf16[1024,1024]{1,0:T(8,128)(2,1)S(1)}, bf16[1024,768]{1,0:T(8,128)(2,1)S(1)}, f32[32,1024]{1,0:T(8,128)S(1)}) custom-call(bf16[1024,1024]{1,0:T(8,128)(2,1)S(1)} %copy-done, bf16[1024,768]{1,0:T(8,128)(2,1)S(1)} %copy-done.1, f32[32,1024]{1,0:T(8,128)S(1)} %pad_maximum_fusion.refs_2_), custom_call_target="tpu_custom_call" | custom-call | flops 1048576 | bytes 209715200 | tf_op jit(solution)/shard_map/last_sums/pallas_call | solution.py:1127
  459.1 0.1 slice_reduce_fusion
  459.2 0.6 multiply_sqrt_fusion
  459.8 0.6 copy.34
  460.4 0.6 fusion
  461.1 0.6 copy_bitcast_fusion
  461.7 0.0 copy-done.8
  461.7 0.0 copy-done.9
  461.7 1.5 maximum_convert_fusion.3
  463.1 0.0 copy-done.7
  463.1 3.6 maximum_convert_fusion.2
  466.7 0.0 copy-done.2
  466.7 0.7 copy-done.3
  467.4 0.8 copy-done.4
  468.3 6.5 %maximum_convert_fusion = (f32[2,1024,1024]{2,1,0:T(8,128)}, f32[2,1024,1024]{2,1,0:T(8,128)}) fusion(bf16[1,1024,1024]{2,1,0:T(8,128)(2,1)S(1)} %bitcast.24, bf16[1,1024,1024]{2,1,0:T(8,128)(2,1)S(1)} %bitcast.16, bf16[1,1024,1024]{2,1,0:T(8,128)(2,1)S(1)} %bitcast.22, bf16[1,1024,1024]{2,1,0:T(8,128)(2,1)S(1)} %bitcast.23), kind=kLoop, calls=%fused_computation | loop fusion | flops 8388608 | bytes 25165824 | tf_op jit(solution)/shard_map/convert_element_type | solution.py:1743
  474.7 0.0 copy-done.11
  474.7 0.6 copy.38
  475.3 0.0 copy-done.5
  475.3 1.3 copy.39
  476.6 0.0 copy-done.6
  476.7 1.3 copy.40
  (11 shorter events, 0.0 us)
Async XLA Ops:
  254.6 123.7 %copy-start.10 = (f32[16,1024]{1,0:T(8,128)S(1)}, f32[16,1024]{1,0:T(8,128)}, u32[]{:S(2)}) copy-start(f32[16,1024]{1,0:T(8,128)} %get-tuple-element.73) | copy-start | bytes 196612
  254.6 207.1 %copy-start.8 = (bf16[256,1024]{1,0:T(8,128)(2,1)S(1)}, bf16[256,1024]{1,0:T(8,128)(2,1)}, u32[]{:S(2)}) copy-start(bf16[256,1024]{1,0:T(8,128)(2,1)} %get-tuple-element.78) | copy-start | bytes 1572868
  379.1 1.6 copy-start
  380.7 1.4 copy-start.1
  382.1 79.5 %copy-start.9 = (bf16[256,1024]{1,0:T(8,128)(2,1)S(1)}, bf16[256,1024]{1,0:T(8,128)(2,1)}, u32[]{:S(2)}) copy-start(bf16[256,1024]{1,0:T(8,128)(2,1)} %get-tuple-element.77) | copy-start | bytes 1572868
  382.1 81.0 %copy-start.7 = (bf16[1024,768]{1,0:T(8,128)(2,1)S(1)}, bf16[1024,768]{1,0:T(8,128)(2,1)}, u32[]{:S(2)}) copy-start(bf16[1024,768]{1,0:T(8,128)(2,1)} %get-tuple-element.75) | copy-start | bytes 4718596
  461.7 13.1 %copy-start.11 = (f32[2,1024]{1,0:T(2,128)}, f32[2,1024]{1,0:T(2,128)S(1)}, u32[]{:S(2)}) copy-start(f32[2,1024]{1,0:T(2,128)S(1)} %get-tuple-element.135) | copy-start | bytes 24580
  463.1 3.6 copy-start.2
  463.1 4.3 copy-start.3
  463.1 5.1 %copy-start.4 = (bf16[1024,1024]{1,0:T(8,128)(2,1)S(1)}, bf16[1024,1024]{1,0:T(8,128)(2,1)}, u32[]{:S(2)}) copy-start(bf16[1024,1024]{1,0:T(8,128)(2,1)} %get-tuple-element.80) | copy-start | bytes 6291460
  468.3 7.1 %copy-start.5 = (f32[512,1024]{1,0:T(8,128)S(1)}, f32[512,1024]{1,0:T(8,128)}, u32[]{:S(2)}) copy-start(f32[512,1024]{1,0:T(8,128)} %get-tuple-element.130.refs_12_) | copy-start | bytes 6291460
  474.7 1.9 copy-start.6

commit v6 on v5

--- a/solution.py
+++ b/solution.py
@@ -679,7 +679,7 @@
             copy.start()
             gathers[k].append(copy)
 
-    products = {}
+    joined = []
     u_out = []
 
     def feed(k):
@@ -707,6 +707,11 @@
                 u_out.append(copy)
         keep(hid_s.at[k], hid_o.at[pl.ds(k * seq, seq), :], 2 * k + 1)
 
+    def part(k, r):
+        at = block(r)
+        index = 9 + k * half_blocks + r
+        return remote(psend.at[k, at, :], precv.at[k, at, :], sems, index, core)
+
     def join(k):
         need("down", "out")
 
@@ -716,10 +721,9 @@
             psend[k, block(r), :] = dot_nn(hid_s[k, at, :], down_ref[...]) + dot_nn(
                 ctx_s[k, at, :], out_ref[...]
             )
-
-        product = remote(psend.at[k], precv.at[k], sems, 5 + k, core)
-        product.start()
-        products[k] = product
+            part(k, r).start()
+
+        joined.append(k)
 
         @pl.loop(0, half_blocks)
         def _(r):
@@ -728,11 +732,10 @@
                 ctx_s[k, at, :], out_ref[...]
             )
 
-        product.wait_recv()
-
         @pl.loop(0, half_blocks)
         def _(r):
             at = block(r)
+            part(k, r).wait_recv()
             total = precv[k, at, :] + mine_s[at, :]
             precv[k, at, :] = total
             if not (final and k == 0):
@@ -828,8 +831,9 @@
         far_copy.wait_send()
     for copy in u_out + outs:
         copy.wait()
-    for copy in products.values():
-        copy.wait_send()
+    for k in joined:
+        for r in range(half_blocks):
+            part(k, r).wait_send()
     for copy in sums.values():
         copy.wait_send()
 
@@ -879,7 +883,8 @@
     scratch += [pltpu.VMEM(item.shape, F32) for item in tables]
     scratch += [pltpu.VMEM((1, width), F32) for width in (ff, 3 * w, features)]
     scratch += [pltpu.VMEM((2, features), F32)] * 2
-    scratch += [DMA((9,)), DMA((9,)), DMA((15,)), DMA((rows // QB,)), DMA((7,))]
+    sems = 9 + 2 * (rows // QB)
+    scratch += [DMA((sems,)), DMA((sems,)), DMA((15,)), DMA((rows // QB,)), DMA((7,))]
     return pl.pallas_call(
         functools.partial(forward_layer_kernel, l, first, final, rows, w),
         in_specs=[VMEM] + [ANY] * 7 + [VMEM] * (len(args) - 8),

time: 487 us -> 485 us (level)
  no operation moved by 1% of the time
where the time goes in v6:
time: 485 us; the launch traced here: 476 us
  Pallas kernels  452 us (93%)
  other arithmetic  13 us (3%)
  local copies, waits for them, and re-layouts  9.63 us (2%)
    pallas_call x2, Pallas kernels, backward_layer(): pl.pallas_call(functools.partial(backward_layer_kernel, l, first, final,...  230 us
    pallas_call x2, Pallas kernels, forward_layer(): pl.pallas_call(functools.partial(forward_layer_kernel, l, first, final, r...  144 us
    pallas_call x1, Pallas kernels, last_sums(): pl.pallas_call(functools.partial(last_sums_kernel, n, count), in_specs=[A...  78.1 us
    convert_element_type x3, other arithmetic, on_group(): jnp.stack(item).astype(F32)  11.5 us

profile of v6, /device:TPU:0, one launch (start us, length us, event | category | flops | bytes accessed | tf_op | source)
XLA Modules:
  0.0 476.2 jit_solution(5023605153899483530)
XLA Ops:
  0.6 86.0 %forward_layer.2 = (bf16[2048,1024]{1,0:T(8,128)(2,1)}, bf16[2048,1024]{1,0:T(8,128)(2,1)}, f32[2048,1024]{1,0:T(8,128)}, bf16[2048,1024]{1,0:T(8,128)(2,1)}, bf...) custom-call(bf16[512,1024]{1,0:T(8,128)(2,1)} %refs_13_.5, ...), custom_call_target="tpu_custom_call" | custom-call | flops 25769803776 | bytes 41943040 | tf_op jit(solution)/shard_map/forward_layer/pallas_call | solution.py:888
  86.6 58.0 %forward_layer.3 = (bf16[2048,1024]{1,0:T(8,128)(2,1)}, bf16[2048,1024]{1,0:T(8,128)(2,1)}, f32[2048,1024]{1,0:T(8,128)}, bf16[2048,1024]{1,0:T(8,128)(2,1)}, bf...) custom-call(f32[1024,1024]{1,0:T(8,128)} %get-tuple-element.48.refs_, ...), custom_call_target="tpu_custom_call" | custom-call | flops 25769803776 | bytes 41943040 | tf_op jit(solution)/shard_map/forward_layer/pallas_call | solution.py:888
  144.6 106.8 %backward_layer.2 = (f32[512,1024]{1,0:T(8,128)}, f32[16,1024]{1,0:T(8,128)}, bf16[1024,1024]{1,0:T(8,128)(2,1)}, bf16[256,1024]{1,0:T(8,128)(2,1)}, bf16[1024,1...) custom-call(bf16[512,1024]{1,0:T(8,128)(2,1)} %refs_0_.3, ...), custom_call_target="tpu_custom_call" | custom-call | flops 25769803776 | bytes 41943040 | tf_op jit(solution)/shard_map/backward_layer/pallas_call | solution.py:1641
  251.5 0.0 copy-start.10
  251.5 0.0 copy-start.8
  251.5 123.4 %backward_layer.3 = (f32[512,1024]{1,0:T(8,128)}, f32[16,1024]{1,0:T(8,128)}, bf16[1024,1024]{1,0:T(8,128)(2,1)}, bf16[256,1024]{1,0:T(8,128)(2,1)}, bf16[1024,1...) custom-call(f32[512,1024]{1,0:T(8,128)} %get-tuple-element.58.refs_0, ...), custom_call_target="tpu_custom_call" | custom-call | flops 25769803776 | bytes 41943040 | tf_op jit(solution)/shard_map/backward_layer/pallas_call | solution.py:1641
  374.9 0.0 copy-done.10
  374.9 0.9 pad_maximum_fusion.refs_2_
  375.8 0.0 copy-start
  375.8 1.6 copy-done
  377.4 1.4 copy-done.1
  378.8 78.1 %last_sums.1 = (bf16[1024,1024]{1,0:T(8,128)(2,1)S(1)}, bf16[1024,768]{1,0:T(8,128)(2,1)S(1)}, f32[32,1024]{1,0:T(8,128)S(1)}) custom-call(bf16[1024,1024]{1,0:T(8,128)(2,1)S(1)} %copy-done, bf16[1024,768]{1,0:T(8,128)(2,1)S(1)} %copy-done.1, f32[32,1024]{1,0:T(8,128)S(1)} %pad_maximum_fusion.refs_2_), custom_call_target="tpu_custom_call" | custom-call | flops 1048576 | bytes 209715200 | tf_op jit(solution)/shard_map/last_sums/pallas_call | solution.py:1132
  456.9 0.1 slice_reduce_fusion
  457.0 0.6 multiply_sqrt_fusion
  457.6 0.6 copy.34
  458.2 0.6 fusion
  458.8 0.6 copy_bitcast_fusion
  459.4 0.0 copy-done.8
  459.4 0.0 copy-done.9
  459.4 1.5 maximum_convert_fusion.3
  460.9 0.0 copy-done.7
  460.9 3.6 maximum_convert_fusion.2
  464.5 0.0 copy-done.2
  464.5 0.7 copy-done.3
  465.2 0.8 copy-done.4
  466.0 6.5 %maximum_convert_fusion = (f32[2,1024,1024]{2,1,0:T(8,128)}, f32[2,1024,1024]{2,1,0:T(8,128)}) fusion(bf16[1,1024,1024]{2,1,0:T(8,128)(2,1)S(1)} %bitcast.24, bf16[1,1024,1024]{2,1,0:T(8,128)(2,1)S(1)} %bitcast.16, bf16[1,1024,1024]{2,1,0:T(8,128)(2,1)S(1)} %bitcast.22, bf16[1,1024,1024]{2,1,0:T(8,128)(2,1)S(1)} %bitcast.23), kind=kLoop, calls=%fused_computation | loop fusion | flops 8388608 | bytes 25165824 | tf_op jit(solution)/shard_map/convert_element_type | solution.py:1748
  472.5 0.0 copy-done.11
  472.5 0.6 copy.38
  473.1 0.0 copy-done.5
  473.1 1.3 copy.39
  474.4 0.0 copy-done.6
  474.4 1.3 copy.40
  (11 shorter events, 0.0 us)
Async XLA Ops:
  251.5 123.5 %copy-start.10 = (f32[16,1024]{1,0:T(8,128)S(1)}, f32[16,1024]{1,0:T(8,128)}, u32[]{:S(2)}) copy-start(f32[16,1024]{1,0:T(8,128)} %get-tuple-element.73) | copy-start | bytes 196612
  251.5 208.0 %copy-start.8 = (bf16[256,1024]{1,0:T(8,128)(2,1)S(1)}, bf16[256,1024]{1,0:T(8,128)(2,1)}, u32[]{:S(2)}) copy-start(bf16[256,1024]{1,0:T(8,128)(2,1)} %get-tuple-element.78) | copy-start | bytes 1572868
  375.8 1.6 copy-start
  377.4 1.4 copy-start.1
  378.8 80.6 %copy-start.9 = (bf16[256,1024]{1,0:T(8,128)(2,1)S(1)}, bf16[256,1024]{1,0:T(8,128)(2,1)}, u32[]{:S(2)}) copy-start(bf16[256,1024]{1,0:T(8,128)(2,1)} %get-tuple-element.77) | copy-start | bytes 1572868
  378.8 82.1 %copy-start.7 = (bf16[1024,768]{1,0:T(8,128)(2,1)S(1)}, bf16[1024,768]{1,0:T(8,128)(2,1)}, u32[]{:S(2)}) copy-start(bf16[1024,768]{1,0:T(8,128)(2,1)} %get-tuple-element.75) | copy-start | bytes 4718596
  459.4 13.1 %copy-start.11 = (f32[2,1024]{1,0:T(2,128)}, f32[2,1024]{1,0:T(2,128)S(1)}, u32[]{:S(2)}) copy-start(f32[2,1024]{1,0:T(2,128)S(1)} %get-tuple-element.135) | copy-start | bytes 24580
  460.9 3.6 copy-start.2
  460.9 4.3 copy-start.3
  460.9 5.1 %copy-start.4 = (bf16[1024,1024]{1,0:T(8,128)(2,1)S(1)}, bf16[1024,1024]{1,0:T(8,128)(2,1)}, u32[]{:S(2)}) copy-start(bf16[1024,1024]{1,0:T(8,128)(2,1)} %get-tuple-element.80) | copy-start | bytes 6291460
  466.0 7.1 %copy-start.5 = (f32[512,1024]{1,0:T(8,128)S(1)}, f32[512,1024]{1,0:T(8,128)}, u32[]{:S(2)}) copy-start(f32[512,1024]{1,0:T(8,128)} %get-tuple-element.130.refs_12_) | copy-start | bytes 6291460
  472.5 1.9 copy-start.6
